TPU v7x, 32 devices: a whole 2x2x4 slice. The times are simulated.
32 devices in a mesh: dp: 2 (over y), ctx: 4 (over x, core), tensor: 4 (over z).
Axes of the slice: x: 2, y: 2, z: 4, core: 2. Of those that a mesh axis runs over, the one named last changes fastest.
Arguments:
- tokens: bfloat16 [8, 320, 1024], P('dp', 'ctx'), may hold values from -6 to 6
- keep_mask: int32 [8, 256], P('dp'), may hold values from 0 to 1, as said below
- cotangent: bfloat16 [8, 320, 1024], P('dp', 'ctx'), may hold values from -6 to 6
- first_gain: bfloat16 [1024], P(('dp', 'ctx')), may hold values from 0.099609375 to 1.8984375
- first_shift: bfloat16 [1024], P(('dp', 'ctx')), may hold values from -4 to 4
- attend_in: bfloat16 [1024, 3, 1024], P(('dp', 'ctx'), None, 'tensor'), may hold values from -0.1875 to 0.1875
- attend_bias: bfloat16 [2, 16, 64], P(None, 'tensor', ('dp', 'ctx')), may hold values from -0.59765625 to 0.59765625
- attend_out: bfloat16 [1024, 1024], P('tensor', ('dp', 'ctx')), may hold values from -0.75 to 0.75
- out_bias: bfloat16 [1024], P(('dp', 'ctx')), may hold values from -4 to 4
- second_gain: bfloat16 [1024], P(('dp', 'ctx')), may hold values from 0.099609375 to 1.8984375
- second_shift: bfloat16 [1024], P(('dp', 'ctx')), may hold values from -4 to 4
- expand_in: bfloat16 [1024, 4096], P(('dp', 'ctx'), 'tensor'), may hold values from -0.1875 to 0.1875
- expand_bias: bfloat16 [64, 64], P('tensor', ('dp', 'ctx')), may hold values from -3 to 3
- contract_out: bfloat16 [4096, 1024], P('tensor', ('dp', 'ctx')), may hold values from -0.09375 to 0.09375
- contract_bias: bfloat16 [1024], P(('dp', 'ctx')), may hold values from -4 to 4
Outputs:
- block_out: bfloat16 [8, 320, 1024], P('dp', 'ctx')
- tokens_grad: bfloat16 [8, 320, 1024], P('dp', 'ctx')
- first_gain_grad: float32 [1024], P(('dp', 'ctx'))
- first_shift_grad: float32 [1024], P(('dp', 'ctx'))
- attend_in_grad: float32 [1024, 3, 1024], P(('dp', 'ctx'), None, 'tensor')
- attend_bias_grad: float32 [2, 16, 64], P(None, 'tensor', ('dp', 'ctx'))
- attend_out_grad: float32 [1024, 1024], P('tensor', ('dp', 'ctx'))
- out_bias_grad: float32 [1024], P(('dp', 'ctx'))
- second_gain_grad: float32 [1024], P(('dp', 'ctx'))
- second_shift_grad: float32 [1024], P(('dp', 'ctx'))
- expand_in_grad: float32 [1024, 4096], P(('dp', 'ctx'), 'tensor')
- expand_bias_grad: float32 [64, 64], P('tensor', ('dp', 'ctx'))
- contract_out_grad: float32 [4096, 1024], P('tensor', ('dp', 'ctx'))
- contract_bias_grad: float32 [1024], P(('dp', 'ctx'))
Inputs may be any that keep to these rules, and one draw needn't show every extreme that they name: `keep_mask`: in every aligned block of 2 images one image, drawn from the seed, keeps all 256 patches. The kept patches' tokens fill the slots from 64 on; the slots after them are padding.
All inputs are finite; a program needn't handle non-finite values.
Results may differ from a plain program's by a relative error of at most 0.02.
Values may be sent and summed in bfloat16 or wider, within the bound.
A program may use at most 64 MiB of HBM per device.

v0:
```python
import jax
import jax.numpy as jnp
from jax import lax
from jax.sharding import PartitionSpec as P

HD = 64
BUFFER = 64
MICRO = 2


eps = 1e-06
neg_big = -1e30
root_half = 0.7071067811865476
inv_root_two_pi = 0.3989422804014327


def layer_norm(values, gain, shift):
    mean = jnp.mean(values, axis=-1, keepdims=True)
    centered = values - mean
    spread = jnp.mean(centered * centered, axis=-1, keepdims=True)
    inv_std = lax.rsqrt(spread + eps)
    normed = centered * inv_std
    return (normed * gain + shift, normed, inv_std)


def norm_back(grad_out, normed, inv_std, gain):
    scaled = grad_out * gain
    inner = (
        scaled
        - jnp.mean(scaled, axis=-1, keepdims=True)
        - normed * jnp.mean(scaled * normed, axis=-1, keepdims=True)
    )
    return inner * inv_std


def gelu_value(inner):
    return 0.5 * inner * (1.0 + lax.erf(inner * root_half))


def gelu_slope(inner):
    return (
        0.5 * (1.0 + lax.erf(inner * root_half))
        + inner * jnp.exp(-0.5 * inner * inner) * inv_root_two_pi
    )


def row_product(left, right):
    return jnp.dot(left, right, preferred_element_type=jnp.float32)


def outer_sum(left, right):
    flat_left = left.reshape(-1, left.shape[-1])
    flat_right = right.reshape(-1, right.shape[-1])
    return lax.dot_general(
        flat_left, flat_right, (((0,), (0,)), ((), ())), preferred_element_type=jnp.float32
    )


def back_product(grad, weight):
    return lax.dot_general(
        grad, weight, (((2,), (1,)), ((), ())), preferred_element_type=jnp.float32
    )


def forward_pass(block_tokens, live_rows, key_live, whole):
    (
        gain_one,
        shift_one,
        weight_in,
        bias_pair,
        weight_out,
        bias_out,
        gain_two,
        shift_two,
        weight_up,
        bias_up,
        weight_down,
        bias_down,
    ) = whole
    count, slots, width = block_tokens.shape
    local_width = weight_in.shape[2]
    local_heads = local_width // HD
    scale = HD ** (-0.5)
    start = block_tokens.astype(jnp.float32)
    normed_in, normed_one, inv_one = layer_norm(
        start, gain_one.astype(jnp.float32), shift_one.astype(jnp.float32)
    )
    hidden_one = normed_in.astype(jnp.bfloat16)
    projected = jnp.einsum(
        "bsd,dcf->bscf", hidden_one, weight_in, preferred_element_type=jnp.float32
    )
    biases = bias_pair.astype(jnp.float32).reshape(2, local_width)
    queries = (projected[:, :, 0] + biases[0]).astype(jnp.bfloat16)
    keys = projected[:, :, 1].astype(jnp.bfloat16)
    values = (projected[:, :, 2] + biases[1]).astype(jnp.bfloat16)
    all_keys, all_values = (
        lax.all_gather(keys, "ctx", axis=1, tiled=True),
        lax.all_gather(values, "ctx", axis=1, tiled=True),
    )
    query_heads = queries.reshape(count, slots, local_heads, HD)
    key_heads = all_keys.reshape(count, -1, local_heads, HD)
    value_heads = all_values.reshape(count, -1, local_heads, HD)
    scores = (
        jnp.einsum("bqhc,bkhc->bhqk", query_heads, key_heads, preferred_element_type=jnp.float32)
        * scale
    )
    scores = jnp.where(key_live, scores, neg_big)
    top = jnp.max(scores, axis=-1, keepdims=True)
    expo = jnp.exp(scores - top)
    total = jnp.sum(expo, axis=-1, keepdims=True)
    probs = (expo / total).astype(jnp.bfloat16)
    log_total = top + jnp.log(total)
    mixed = jnp.einsum("bhqk,bkhc->bqhc", probs, value_heads, preferred_element_type=jnp.float32)
    mixed = mixed.reshape(count, slots, local_width).astype(jnp.bfloat16)
    branch = lax.psum(row_product(mixed, weight_out).astype(jnp.bfloat16), "tensor").astype(
        jnp.float32
    )
    first = start + branch + bias_out.astype(jnp.float32)
    normed_mid, normed_two, inv_two = layer_norm(
        first, gain_two.astype(jnp.float32), shift_two.astype(jnp.float32)
    )
    hidden_two = normed_mid.astype(jnp.bfloat16)
    inner = row_product(hidden_two, weight_up) + bias_up.astype(jnp.float32).reshape(-1)
    activ = gelu_value(inner).astype(jnp.bfloat16)
    second_branch = lax.psum(row_product(activ, weight_down).astype(jnp.bfloat16), "tensor").astype(
        jnp.float32
    )
    second = first + second_branch + bias_down.astype(jnp.float32)
    output = jnp.where(live_rows[:, :, None], second, 0.0).astype(jnp.bfloat16)
    saved = (
        normed_one,
        inv_one,
        hidden_one,
        query_heads,
        key_heads,
        value_heads,
        log_total,
        mixed,
        normed_two,
        inv_two,
        hidden_two,
        inner,
        activ,
    )
    return (output, saved)


def backward_pass(grad_rows, key_live, whole, saved):
    (
        gain_one,
        shift_one,
        weight_in,
        bias_pair,
        weight_out,
        bias_out,
        gain_two,
        shift_two,
        weight_up,
        bias_up,
        weight_down,
        bias_down,
    ) = whole
    (
        normed_one,
        inv_one,
        hidden_one,
        query_heads,
        key_heads,
        value_heads,
        log_total,
        mixed,
        normed_two,
        inv_two,
        hidden_two,
        inner,
        activ,
    ) = saved
    count, slots, width = grad_rows.shape
    local_width = weight_in.shape[2]
    local_heads = local_width // HD
    scale = HD ** (-0.5)
    grad_bias_down = jnp.sum(grad_rows, axis=(0, 1))
    grad_down = grad_rows.astype(jnp.bfloat16)
    grad_weight_down = outer_sum(activ, grad_down)
    grad_activ = back_product(grad_down, weight_down)
    grad_inner = (grad_activ * gelu_slope(inner)).astype(jnp.bfloat16)
    grad_bias_up = jnp.sum(grad_inner.astype(jnp.float32), axis=(0, 1)).reshape(bias_up.shape)
    grad_weight_up = outer_sum(hidden_two, grad_inner)
    grad_hidden_two = lax.psum(
        back_product(grad_inner, weight_up).astype(jnp.bfloat16), "tensor"
    ).astype(jnp.float32)
    grad_gain_two = jnp.sum(grad_hidden_two * normed_two, axis=(0, 1))
    grad_shift_two = jnp.sum(grad_hidden_two, axis=(0, 1))
    grad_first = grad_rows + norm_back(
        grad_hidden_two, normed_two, inv_two, gain_two.astype(jnp.float32)
    )
    grad_bias_out = jnp.sum(grad_first, axis=(0, 1))
    grad_branch = grad_first.astype(jnp.bfloat16)
    grad_weight_out = outer_sum(mixed, grad_branch)
    grad_mixed = (
        back_product(grad_branch, weight_out)
        .astype(jnp.bfloat16)
        .reshape(count, slots, local_heads, HD)
    )
    scores = (
        jnp.einsum("bqhc,bkhc->bhqk", query_heads, key_heads, preferred_element_type=jnp.float32)
        * scale
    )
    scores = jnp.where(key_live, scores, neg_big)
    weights = jnp.exp(scores - log_total)
    grad_probs = jnp.einsum(
        "bqhc,bkhc->bhqk", grad_mixed, value_heads, preferred_element_type=jnp.float32
    )
    along = jnp.sum(grad_probs * weights, axis=-1, keepdims=True)
    grad_scores = (weights * (grad_probs - along)).astype(jnp.bfloat16)
    grad_queries = (
        jnp.einsum("bhqk,bkhc->bqhc", grad_scores, key_heads, preferred_element_type=jnp.float32)
        * scale
    )
    grad_queries = grad_queries.astype(jnp.bfloat16).reshape(count, slots, local_width)
    key_terms = (
        jnp.einsum("bhqk,bqhc->bkhc", grad_scores, query_heads, preferred_element_type=jnp.float32)
        * scale
    )
    value_terms = jnp.einsum(
        "bhqk,bqhc->bkhc",
        weights.astype(jnp.bfloat16),
        grad_mixed,
        preferred_element_type=jnp.float32,
    )
    key_sums, value_sums = (
        lax.psum_scatter(
            key_terms.astype(jnp.bfloat16), "ctx", scatter_dimension=1, tiled=True
        ).astype(jnp.float32),
        lax.psum_scatter(
            value_terms.astype(jnp.bfloat16), "ctx", scatter_dimension=1, tiled=True
        ).astype(jnp.float32),
    )
    grad_keys = key_sums.astype(jnp.bfloat16).reshape(count, slots, local_width)
    grad_values = value_sums.astype(jnp.bfloat16).reshape(count, slots, local_width)
    grad_projected = jnp.stack([grad_queries, grad_keys, grad_values], axis=2)
    query_total = jnp.sum(grad_queries.astype(jnp.float32), axis=(0, 1))
    value_total = jnp.sum(grad_values.astype(jnp.float32), axis=(0, 1))
    grad_bias_pair = jnp.stack([query_total, value_total]).reshape(bias_pair.shape)
    grad_weight_in = jnp.einsum(
        "bsd,bscf->dcf", hidden_one, grad_projected, preferred_element_type=jnp.float32
    )
    grad_hidden_one = lax.psum(
        jnp.einsum(
            "bscf,dcf->bsd", grad_projected, weight_in, preferred_element_type=jnp.float32
        ).astype(jnp.bfloat16),
        "tensor",
    ).astype(jnp.float32)
    grad_gain_one = jnp.sum(grad_hidden_one * normed_one, axis=(0, 1))
    grad_shift_one = jnp.sum(grad_hidden_one, axis=(0, 1))
    grad_start = grad_first + norm_back(
        grad_hidden_one, normed_one, inv_one, gain_one.astype(jnp.float32)
    )
    grads = (
        grad_gain_one,
        grad_shift_one,
        grad_weight_in,
        grad_bias_pair,
        grad_weight_out,
        grad_bias_out,
        grad_gain_two,
        grad_shift_two,
        grad_weight_up,
        grad_bias_up,
        grad_weight_down,
        grad_bias_down,
    )
    return (grad_start.astype(jnp.bfloat16), grads)


def on_device(
    tokens,
    keep_mask,
    cotangent,
    first_gain,
    first_shift,
    attend_in,
    attend_bias,
    attend_out,
    out_bias,
    second_gain,
    second_shift,
    expand_in,
    expand_bias,
    contract_out,
    contract_bias,
):
    per_micro = tokens.shape[0] // MICRO
    slots = tokens.shape[1]
    total_slots = slots * lax.axis_size("ctx")
    lengths = BUFFER + jnp.sum(keep_mask, axis=1)
    own_slots = lax.axis_index("ctx") * slots + lax.iota(jnp.int32, slots)
    every_slot = lax.iota(jnp.int32, total_slots)
    outputs = []
    input_grads = []
    owned = None
    for index in range(MICRO):
        lower = index * per_micro
        upper = lower + per_micro
        block_lengths = lengths[lower:upper]
        live_rows = own_slots[None, :] < block_lengths[:, None]
        key_live = (every_slot[None, :] < block_lengths[:, None])[:, None, None, :]
        whole = (
            lax.all_gather(first_gain, ("dp", "ctx"), axis=0, tiled=True),
            lax.all_gather(first_shift, ("dp", "ctx"), axis=0, tiled=True),
            lax.all_gather(attend_in, ("dp", "ctx"), axis=0, tiled=True),
            lax.all_gather(attend_bias, ("dp", "ctx"), axis=2, tiled=True),
            lax.all_gather(attend_out, ("dp", "ctx"), axis=1, tiled=True),
            lax.all_gather(out_bias, ("dp", "ctx"), axis=0, tiled=True),
            lax.all_gather(second_gain, ("dp", "ctx"), axis=0, tiled=True),
            lax.all_gather(second_shift, ("dp", "ctx"), axis=0, tiled=True),
            lax.all_gather(expand_in, ("dp", "ctx"), axis=0, tiled=True),
            lax.all_gather(expand_bias, ("dp", "ctx"), axis=1, tiled=True),
            lax.all_gather(contract_out, ("dp", "ctx"), axis=1, tiled=True),
            lax.all_gather(contract_bias, ("dp", "ctx"), axis=0, tiled=True),
        )
        output, saved = forward_pass(tokens[lower:upper], live_rows, key_live, whole)
        whole = (
            lax.all_gather(first_gain, ("dp", "ctx"), axis=0, tiled=True),
            lax.all_gather(first_shift, ("dp", "ctx"), axis=0, tiled=True),
            lax.all_gather(attend_in, ("dp", "ctx"), axis=0, tiled=True),
            lax.all_gather(attend_bias, ("dp", "ctx"), axis=2, tiled=True),
            lax.all_gather(attend_out, ("dp", "ctx"), axis=1, tiled=True),
            lax.all_gather(out_bias, ("dp", "ctx"), axis=0, tiled=True),
            lax.all_gather(second_gain, ("dp", "ctx"), axis=0, tiled=True),
            lax.all_gather(second_shift, ("dp", "ctx"), axis=0, tiled=True),
            lax.all_gather(expand_in, ("dp", "ctx"), axis=0, tiled=True),
            lax.all_gather(expand_bias, ("dp", "ctx"), axis=1, tiled=True),
            lax.all_gather(contract_out, ("dp", "ctx"), axis=1, tiled=True),
            lax.all_gather(contract_bias, ("dp", "ctx"), axis=0, tiled=True),
        )
        grad_rows = jnp.where(
            live_rows[:, :, None], cotangent[lower:upper].astype(jnp.float32), 0.0
        )
        input_grad, grads = backward_pass(grad_rows, key_live, whole, saved)
        outputs.append(output)
        input_grads.append(input_grad)
        shares = (
            lax.psum_scatter(grads[0], ("dp", "ctx"), scatter_dimension=0, tiled=True),
            lax.psum_scatter(grads[1], ("dp", "ctx"), scatter_dimension=0, tiled=True),
            lax.psum_scatter(grads[2], ("dp", "ctx"), scatter_dimension=0, tiled=True),
            lax.psum_scatter(grads[3], ("dp", "ctx"), scatter_dimension=2, tiled=True),
            lax.psum_scatter(grads[4], ("dp", "ctx"), scatter_dimension=1, tiled=True),
            lax.psum_scatter(grads[5], ("dp", "ctx"), scatter_dimension=0, tiled=True),
            lax.psum_scatter(grads[6], ("dp", "ctx"), scatter_dimension=0, tiled=True),
            lax.psum_scatter(grads[7], ("dp", "ctx"), scatter_dimension=0, tiled=True),
            lax.psum_scatter(grads[8], ("dp", "ctx"), scatter_dimension=0, tiled=True),
            lax.psum_scatter(grads[9], ("dp", "ctx"), scatter_dimension=1, tiled=True),
            lax.psum_scatter(grads[10], ("dp", "ctx"), scatter_dimension=1, tiled=True),
            lax.psum_scatter(grads[11], ("dp", "ctx"), scatter_dimension=0, tiled=True),
        )
        owned = (
            shares if owned is None else tuple((held + added for held, added in zip(owned, shares)))
        )
    block_out = jnp.concatenate(outputs, axis=0)
    tokens_grad = jnp.concatenate(input_grads, axis=0)
    return (
        block_out,
        tokens_grad,
        owned[0],
        owned[1],
        owned[2],
        owned[3],
        owned[4],
        owned[5],
        owned[6],
        owned[7],
        owned[8],
        owned[9],
        owned[10],
        owned[11],
    )


def solution(mesh):
    return jax.shard_map(
        on_device,
        mesh=mesh,
        in_specs=(
            P("dp", "ctx", None),
            P("dp", None),
            P("dp", "ctx", None),
            P(("dp", "ctx")),
            P(("dp", "ctx")),
            P(("dp", "ctx"), None, "tensor"),
            P(None, "tensor", ("dp", "ctx")),
            P("tensor", ("dp", "ctx")),
            P(("dp", "ctx")),
            P(("dp", "ctx")),
            P(("dp", "ctx")),
            P(("dp", "ctx"), "tensor"),
            P("tensor", ("dp", "ctx")),
            P("tensor", ("dp", "ctx")),
            P(("dp", "ctx")),
        ),
        out_specs=(
            P("dp", "ctx", None),
            P("dp", "ctx", None),
            P(("dp", "ctx")),
            P(("dp", "ctx")),
            P(("dp", "ctx"), None, "tensor"),
            P(None, "tensor", ("dp", "ctx")),
            P("tensor", ("dp", "ctx")),
            P(("dp", "ctx")),
            P(("dp", "ctx")),
            P(("dp", "ctx")),
            P(("dp", "ctx"), "tensor"),
            P("tensor", ("dp", "ctx")),
            P("tensor", ("dp", "ctx")),
            P(("dp", "ctx")),
        ),
        check_vma=False,
    )
```

profile of v0, /device:TPU:0, one launch (start us, length us, event | category | flops | bytes accessed | tf_op | source)
XLA Modules:
  0.0 616.9 jit_solution(4514457535441832308)
XLA Ops:
  8.0 10.3 %all-gather.2 = bf16[8,1,128]{2,1,0:T(2,128)(2,1)S(1)} all-gather(bf16[1,1,128]{2,1,0:T(2,128)(2,1)} %bitcast.311), channel_id=1, replica_groups=mesh['dp'=2,'ctx'=4,'tensor'=4] {'dp','ctx'}, dimensions={0}, use_global_device_ids=true | all-gather | bytes 2304 | tf_op jit(solution)/shard_map/all_gather | solution.py:309
  18.3 8.6 %all-gather.3 = bf16[8,1,128]{2,1,0:T(2,128)(2,1)S(1)} all-gather(bf16[1,1,128]{2,1,0:T(2,128)(2,1)} %bitcast.312), channel_id=1, replica_groups=mesh['dp'=2,'ctx'=4,'tensor'=4] {'dp','ctx'}, dimensions={0}, use_global_device_ids=true | all-gather | bytes 2304 | tf_op jit(solution)/shard_map/all_gather | solution.py:310
  27.7 8.2 %all_gather.35 = bf16[2,4,64]{1,0,2:T(2,128)(2,1)S(1)} all-gather(bf16[2,4,8]{1,0,2:T(2,128)(2,1)S(1)} %copy.156), channel_id=1, replica_groups=mesh['dp'=2,'ctx'=4,'tensor'=4] {'dp','ctx'}, dimensions={2}, use_global_device_ids=true | all-gather | bytes 1152 | tf_op jit(solution)/shard_map/all_gather | solution.py:312
  37.0 9.9 %all_gather.38 = bf16[256,1024]{1,0:T(8,128)(2,1)S(1)} all-gather(bf16[256,128]{1,0:T(8,128)(2,1)} %param.22), channel_id=1, replica_groups=mesh['dp'=2,'ctx'=4,'tensor'=4] {'dp','ctx'}, dimensions={1}, use_global_device_ids=true | all-gather | bytes 589824 | tf_op jit(solution)/shard_map/all_gather | solution.py:313
  52.4 6.2 %all-gather.1 = bf16[2,320,1,256]{3,1,2,0:T(8,128)(2,1)S(1)} all-gather(bf16[2,80,1,256]{3,1,2,0:T(8,128)(2,1)S(1)} %slice.156), channel_id=3, replica_groups=mesh['dp'=2,'ctx'=4,'tensor'=4] {'ctx'}, dimensions={1}, use_global_device_ids=true | all-gather | bytes 409600 | tf_op jit(solution)/shard_map/all_gather | solution.py:97
  59.7 6.2 %all-gather = bf16[2,320,1,256]{3,1,2,0:T(8,128)(2,1)S(1)} all-gather(bf16[2,80,1,256]{3,1,2,0:T(8,128)(2,1)S(1)} %slice.157), channel_id=2, replica_groups=mesh['dp'=2,'ctx'=4,'tensor'=4] {'ctx'}, dimensions={1}, use_global_device_ids=true | all-gather | bytes 409600 | tf_op jit(solution)/shard_map/all_gather | solution.py:97
  66.2 6.2 %all_gather.86 = bf16[2,320,256]{2,1,0:T(8,128)(2,1)S(1)} all-gather(bf16[2,80,256]{2,1,0:T(8,128)(2,1)S(1)} %get-tuple-element.144), channel_id=1, replica_groups=mesh['dp'=2,'ctx'=4,'tensor'=4] {'ctx'}, dimensions={1}, use_global_device_ids=true | all-gather | bytes 409600 | tf_op jit(solution)/shard_map/all_gather | solution.py:98
  73.3 6.2 %all_gather.36 = bf16[2,320,256]{2,1,0:T(8,128)(2,1)S(1)} all-gather(bf16[2,80,256]{2,1,0:T(8,128)(2,1)S(1)} %get-tuple-element.145), channel_id=1, replica_groups=mesh['dp'=2,'ctx'=4,'tensor'=4] {'ctx'}, dimensions={1}, use_global_device_ids=true | all-gather | bytes 409600 | tf_op jit(solution)/shard_map/all_gather | solution.py:98
  86.5 8.1 %all-gather.4 = bf16[8,1,128]{2,1,0:T(2,128)(2,1)S(1)} all-gather(bf16[1,1,128]{2,1,0:T(2,128)(2,1)S(1)} %bitcast.313), channel_id=1, replica_groups=mesh['dp'=2,'ctx'=4,'tensor'=4] {'dp','ctx'}, dimensions={0}, use_global_device_ids=true | all-gather | bytes 2304 | tf_op jit(solution)/shard_map/all_gather | solution.py:314
  94.6 8.4 %all-gather.5 = bf16[8,1,128]{2,1,0:T(2,128)(2,1)S(1)} all-gather(bf16[1,1,128]{2,1,0:T(2,128)(2,1)S(1)} %bitcast.314), channel_id=1, replica_groups=mesh['dp'=2,'ctx'=4,'tensor'=4] {'dp','ctx'}, dimensions={0}, use_global_device_ids=true | all-gather | bytes 2304 | tf_op jit(solution)/shard_map/all_gather | solution.py:315
  103.0 8.0 %all-gather.6 = bf16[8,1,128]{2,1,0:T(2,128)(2,1)S(1)} all-gather(bf16[1,1,128]{2,1,0:T(2,128)(2,1)S(1)} %bitcast.315), channel_id=1, replica_groups=mesh['dp'=2,'ctx'=4,'tensor'=4] {'dp','ctx'}, dimensions={0}, use_global_device_ids=true | all-gather | bytes 2304 | tf_op jit(solution)/shard_map/all_gather | solution.py:316
  111.1 8.8 %all_gather.83 = bf16[16,64]{0,1:T(8,128)(2,1)S(1)} all-gather(bf16[16,8]{0,1:T(8,128)(2,1)S(1)} %copy-done.87), channel_id=1, replica_groups=mesh['dp'=2,'ctx'=4,'tensor'=4] {'dp','ctx'}, dimensions={1}, use_global_device_ids=true | all-gather | bytes 2304 | tf_op jit(solution)/shard_map/all_gather | solution.py:318
  120.1 6.2 %all-reduce.20.cloned.1.call-done = (bf16[2,80,1024]{2,1,0:T(8,128)(2,1)}, bf16[2,80,1024]{2,1,0:T(8,128)(2,1)}) async-done(((bf16[2,80,1024]{2,1,0:T(8,128)(2,1)}, bf16[2,80,1024]{2,1,0:T(8,128)(2,1)}), (bf16[2,80,1024]{2,1,0:T(8,128)(2,1)}, bf16[2,80,1024]{2,1,0:T(8,128)(2,1)})) %all-reduce.20.cloned.1.call-update) | async-done | bytes 655376 | tf_op jit(solution)/shard_map/psum | solution.py:115
  129.3 26.3 %all-gather.14.cloned.1.call-done = bf16[1024,1024]{1,0:T(8,128)(2,1)} async-done(((bf16[128,1024]{1,0:T(8,128)(2,1)}), bf16[1024,1024]{1,0:T(8,128)(2,1)}) %all-gather.14.cloned.1.call-update) | async-done | bytes 2097168 | tf_op jit(solution)/shard_map/all_gather | solution.py:317
  155.6 3.1 fusion.36
  158.6 26.9 %all-gather.16.cloned.1.call-done = bf16[1024,1024]{1,0:T(8,128)(2,1)} async-done(((bf16[1024,128]{1,0:T(8,128)(2,1)}), bf16[1024,1024]{1,0:T(8,128)(2,1)}) %all-gather.16.cloned.1.call-update) | async-done | bytes 2097168 | tf_op jit(solution)/shard_map/all_gather | solution.py:319
  185.5 3.5 convert_reduce_fusion.6
  197.3 3.0 fusion.68
  200.3 37.8 %all-reduce.18.cloned.1.call-done = (bf16[2,80,1024]{2,1,0:T(8,128)(2,1)}, bf16[2,80,1024]{2,1,0:T(8,128)(2,1)}) async-done(((bf16[2,80,1024]{2,1,0:T(8,128)(2,1)}, bf16[2,80,1024]{2,1,0:T(8,128)(2,1)}), (bf16[2,80,1024]{2,1,0:T(8,128)(2,1)}, bf16[2,80,1024]{2,1,0:T(8,128)(2,1)})) %all-reduce.18.cloned.1.call-update) | async-done | bytes 655376 | tf_op jit(solution)/shard_map/psum | solution.py:189
  280.9 14.1 %reduce-scatter.33.cloned.1.call-done = bf16[80,512]{1,0:T(8,128)(2,1)} async-done(((bf16[320,512]{1,0:T(8,128)(2,1)}), bf16[80,512]{1,0:T(8,128)(2,1)}) %reduce-scatter.33.cloned.1.call-update) | async-done | bytes 81936
  296.3 21.7 %reduce-scatter.31.cloned.1.call-done = bf16[80,512]{1,0:T(8,128)(2,1)} async-done(((bf16[320,512]{1,0:T(8,128)(2,1)}), bf16[80,512]{1,0:T(8,128)(2,1)}) %reduce-scatter.31.cloned.1.call-update) | async-done | bytes 81936
  319.3 22.4 %reduce-scatter.27.cloned.1.call-done = bf16[80,512]{1,0:T(8,128)(2,1)} async-done(((bf16[320,512]{1,0:T(8,128)(2,1)}), bf16[80,512]{1,0:T(8,128)(2,1)}) %reduce-scatter.27.cloned.1.call-update) | async-done | bytes 81936
  343.0 2.8 fusion.53
  345.8 2.9 fusion.56
  368.2 8.7 %all-gather.7 = bf16[8,1,128]{2,1,0:T(2,128)(2,1)S(1)} all-gather(bf16[1,1,128]{2,1,0:T(2,128)(2,1)S(1)} %bitcast.316), channel_id=1, replica_groups=mesh['dp'=2,'ctx'=4,'tensor'=4] {'dp','ctx'}, dimensions={0}, use_global_device_ids=true | all-gather | bytes 2304 | tf_op jit(solution)/shard_map/all_gather | solution.py:320
  381.0 29.0 %all-reduce.16.cloned.1.call-done = (bf16[2,80,1024]{2,1,0:T(8,128)(2,1)}, bf16[2,80,1024]{2,1,0:T(8,128)(2,1)}, bf16[2,80,1024]{2,1,0:T(8,128)(2,1)}, bf16[2,80,1024]{2,1,0:T(8,128)(2,1)}) async-done(((bf16[2,80,1024]{2,1,0:T(8,128)(2,1)}, bf16[2,80,1024]{2,1,0:T(8,128)(2,1)}, bf16[2,80,1024]{2,1,0:T(8,128)(2,1)}, bf16[2,80,1024]{2,1,0:T(8,128)(2,1)}), (bf16[2,80,1024]{2,1,0:T(8,128)(2,1)}, ...) | async-done | bytes 1310736 | tf_op jit(solution)/shard_map/psum | solution.py:125
  410.0 3.1 fusion.132
  413.2 24.3 %all-reduce.8 = (f32[1024]{0:T(1024)S(1)}, f32[1024]{0:T(1024)S(1)}, f32[2,4,64]{2,1,0:T(4,128)S(1)}, f32[1024]{0:T(1024)S(1)}, f32[1024]{0:T(1024)S(1)}, /*inde...) all-reduce(f32[1024]{0:T(1024)S(1)} %add.375, ...), channel_id=20, replica_groups=mesh['dp'=2,'ctx'=4,'tensor'=4] {'dp','ctx'}, use_global_device_ids=true, to_apply=%region_36.37.clone | all-reduce | flops 7680 | bytes 61440
  445.5 4.0 reduce-scatter.21.cloned.1.call-done
  449.5 50.1 %reduce-scatter.19.cloned.1.call-done = f32[128,3,256]{2,0,1:T(8,128)} async-done(((f32[1024,3,256]{2,0,1:T(8,128)}), f32[128,3,256]{2,0,1:T(8,128)}) %reduce-scatter.19.cloned.1.call-update) | async-done | bytes 393232 | tf_op jit(solution)/shard_map/reduce_scatter | solution.py:346
  499.6 55.7 %reduce-scatter.23.cloned.1.call-done = f32[128,1024]{1,0:T(8,128)} async-done(((f32[1024,1024]{1,0:T(8,128)}), f32[128,1024]{1,0:T(8,128)}) %reduce-scatter.23.cloned.1.call-update) | async-done | bytes 524304 | tf_op jit(solution)/shard_map/reduce_scatter | solution.py:352
  555.2 55.1 %reduce-scatter.25.cloned.1.call-done = f32[1024,128]{1,0:T(8,128)} async-done(((f32[1024,1024]{1,0:T(8,128)}), f32[1024,128]{1,0:T(8,128)}) %reduce-scatter.25.cloned.1.call-update) | async-done | bytes 524304 | tf_op jit(solution)/shard_map/reduce_scatter | solution.py:354
  (356 shorter events, 104.6 us)
Async XLA Ops:
  7.2 41.0 %copy-start = (bf16[4,80,1024]{2,1,0:T(8,128)(2,1)S(1)}, bf16[4,80,1024]{2,1,0:T(8,128)(2,1)}, u32[]{:S(2)}) copy-start(bf16[4,80,1024]{2,1,0:T(8,128)(2,1)} %param.15) | copy-start | bytes 1966084
  7.2 41.6 %all-gather.12.cloned.1.call-start = ((), (), s32[]{:S(2)}) async-start(), calls=%async_computation.8 | async-start | bytes 1769472 | tf_op jit(solution)/shard_map/all_gather | solution.py:311
  7.9 118.4 %all-reduce.20.cloned.1.call-start = ((), (), s32[]{:S(2)}) async-start(), calls=%async_computation.21 | async-start | bytes 1310720 | tf_op jit(solution)/shard_map/psum | solution.py:115
  36.0 46.1 %copy-start.43 = (f32[4,64]{1,0:T(4,128)}, f32[4,64]{1,0:T(4,128)S(1)}, u32[]{:S(2)}) copy-start(f32[4,64]{1,0:T(4,128)S(1)} %copy.160) | copy-start | bytes 3076
  85.2 70.4 %all-gather.14.cloned.1.call-start = ((), (), s32[]{:S(2)}) async-start(), calls=%async_computation.9 | async-start | bytes 2359296 | tf_op jit(solution)/shard_map/all_gather | solution.py:317
  85.9 99.6 %all-gather.16.cloned.1.call-start = ((), (), s32[]{:S(2)}) async-start(), calls=%async_computation.10 | async-start | bytes 2359296 | tf_op jit(solution)/shard_map/all_gather | solution.py:319
  86.5 151.7 %all-reduce.18.cloned.1.call-start = ((), (), s32[]{:S(2)}) async-start(), calls=%async_computation.20 | async-start | bytes 1310720 | tf_op jit(solution)/shard_map/psum | solution.py:189
  111.1 80.3 %copy-start.48 = (f32[8,1,128]{2,1,0:T(1,128)}, f32[8,1,128]{2,1,0:T(1,128)S(1)}, u32[]{:S(2)}) copy-start(f32[8,1,128]{2,1,0:T(1,128)S(1)} %convert_element_type.357) | copy-start | bytes 12292
  120.1 120.7 %copy-start.83 = (pred[2,80]{1,0:T(4,128)(4,1)}, pred[2,80]{1,0:T(4,128)(4,1)S(1)}, u32[]{:S(2)}) copy-start(pred[2,80]{1,0:T(4,128)(4,1)S(1)} %get-tuple-element.146) | copy-start | bytes 484
  120.1 131.7 %copy-start.79 = (pred[2,80]{1,0:T(4,128)(4,1)}, pred[2,80]{1,0:T(4,128)(4,1)S(1)}, u32[]{:S(2)}) copy-start(pred[2,80]{1,0:T(4,128)(4,1)S(1)} %get-tuple-element.147) | copy-start | bytes 484
  127.7 113.1 %copy-start.59 = (f32[2,80]{1,0:T(2,128)}, f32[2,80]{1,0:T(2,128)S(1)}, u32[]{:S(2)}) copy-start(f32[2,80]{1,0:T(2,128)S(1)} %broadcast_multiply_fusion.10) | copy-start | bytes 1924
  127.8 124.1 %copy-start.57 = (f32[2,80]{1,0:T(2,128)}, f32[2,80]{1,0:T(2,128)S(1)}, u32[]{:S(2)}) copy-start(f32[2,80]{1,0:T(2,128)S(1)} %broadcast_multiply_fusion.8) | copy-start | bytes 1924
  129.3 111.6 %copy-start.78 = (f32[2,80]{1,0:T(2,128)}, f32[2,80]{1,0:T(2,128)S(1)}, u32[]{:S(2)}) copy-start(f32[2,80]{1,0:T(2,128)S(1)} %add_rsqrt_fusion.2) | copy-start | bytes 1924
  129.3 122.6 %copy-start.64 = (f32[2,80]{1,0:T(2,128)}, f32[2,80]{1,0:T(2,128)S(1)}, u32[]{:S(2)}) copy-start(f32[2,80]{1,0:T(2,128)S(1)} %add_rsqrt_fusion) | copy-start | bytes 1924
  197.2 82.4 %reduce-scatter.29.cloned.1.call-start = ((), (), s32[]{:S(2)}) async-start(), calls=%async_computation.16 | async-start | bytes 409600
  251.8 43.2 %reduce-scatter.33.cloned.1.call-start = ((), (), s32[]{:S(2)}) async-start(), calls=%async_computation.18 | async-start | bytes 409600
  262.2 55.7 %reduce-scatter.31.cloned.1.call-start = ((), (), s32[]{:S(2)}) async-start(), calls=%async_computation.17 | async-start | bytes 409600
  265.4 76.2 %reduce-scatter.27.cloned.1.call-start = ((), (), s32[]{:S(2)}) async-start(), calls=%async_computation.15 | async-start | bytes 409600
  273.8 136.2 %all-reduce.16.cloned.1.call-start = ((), (), s32[]{:S(2)}) async-start(), calls=%async_computation.19 | async-start | bytes 2621440 | tf_op jit(solution)/shard_map/psum | solution.py:125
  348.7 100.8 %reduce-scatter.21.cloned.1.call-start = ((), (), s32[]{:S(2)}) async-start(), calls=%async_computation.12 | async-start | bytes 1179648 | tf_op jit(solution)/shard_map/reduce_scatter | solution.py:348
  351.2 148.4 %reduce-scatter.19.cloned.1.call-start = ((), (), s32[]{:S(2)}) async-start(), calls=%async_computation.11 | async-start | bytes 3538944 | tf_op jit(solution)/shard_map/reduce_scatter | solution.py:346
  354.5 200.7 %reduce-scatter.23.cloned.1.call-start = ((), (), s32[]{:S(2)}) async-start(), calls=%async_computation.13 | async-start | bytes 4718592 | tf_op jit(solution)/shard_map/reduce_scatter | solution.py:352
  359.9 250.5 %reduce-scatter.25.cloned.1.call-start = ((), (), s32[]{:S(2)}) async-start(), calls=%async_computation.14 | async-start | bytes 4718592 | tf_op jit(solution)/shard_map/reduce_scatter | solution.py:354
  365.8 44.2 %copy-start.53 = (f32[2,80]{1,0:T(2,128)S(1)}, f32[2,80]{1,0:T(2,128)}, u32[]{:S(2)}) copy-start(f32[2,80]{1,0:T(2,128)} %copy-done.51) | copy-start | bytes 1924
  365.8 44.2 %copy-start.56 = (f32[2,80]{1,0:T(2,128)S(1)}, f32[2,80]{1,0:T(2,128)}, u32[]{:S(2)}) copy-start(f32[2,80]{1,0:T(2,128)} %copy-done.54) | copy-start | bytes 1924
  380.7 32.4 %copy-start.50 = (f32[16,64]{1,0:T(8,128)S(1)}, f32[16,64]{1,0:T(8,128)}, u32[]{:S(2)}) copy-start(f32[16,64]{1,0:T(8,128)} %reshape.320) | copy-start | bytes 12292
  380.8 32.4 %copy-start.74 = (f32[1024]{0:T(1024)S(1)}, f32[1024]{0:T(1024)}, u32[]{:S(2)}) copy-start(f32[1024]{0:T(1024)} %add.381) | copy-start | bytes 12292
  380.8 32.4 %copy-start.75 = (f32[1024]{0:T(1024)S(1)}, f32[1024]{0:T(1024)}, u32[]{:S(2)}) copy-start(f32[1024]{0:T(1024)} %add.382) | copy-start | bytes 12292
  380.8 32.4 %copy-start.76 = (f32[1024]{0:T(1024)S(1)}, f32[1024]{0:T(1024)}, u32[]{:S(2)}) copy-start(f32[1024]{0:T(1024)} %add.380) | copy-start | bytes 12292
  380.8 32.4 %copy-start.77 = (f32[1024]{0:T(1024)S(1)}, f32[1024]{0:T(1024)}, u32[]{:S(2)}) copy-start(f32[1024]{0:T(1024)} %add.386) | copy-start | bytes 12292
  410.0 32.4 %copy-start.32 = (bf16[2,80,1024]{2,1,0:T(8,128)(2,1)S(1)}, bf16[2,80,1024]{2,1,0:T(8,128)(2,1)}, u32[]{:S(2)}) copy-start(bf16[2,80,1024]{2,1,0:T(8,128)(2,1)} %get-tuple-element.124) | copy-start | bytes 983044
  410.0 32.4 %copy-start.33 = (bf16[2,80,1024]{2,1,0:T(8,128)(2,1)S(1)}, bf16[2,80,1024]{2,1,0:T(8,128)(2,1)}, u32[]{:S(2)}) copy-start(bf16[2,80,1024]{2,1,0:T(8,128)(2,1)} %get-tuple-element.125) | copy-start | bytes 983044
  (76 other events, 426.1 us)
Sparse Core Ops, SparseCore 0:
  9.9 28.5 all-gather.11
  85.3 40.9 all-reduce.19
  128.2 27.3 all-gather.13
  157.3 28.1 all-gather.15
  197.3 40.7 all-reduce.17
  251.9 19.8 reduce-scatter.28
  274.5 20.4 reduce-scatter.32
  297.5 20.4 reduce-scatter.30
  321.2 20.4 reduce-scatter.26
  348.8 61.1 all-reduce.15
  413.7 35.6 reduce-scatter.20
  453.3 46.2 reduce-scatter.18
  503.9 51.3 reduce-scatter.22
  559.0 51.3 reduce-scatter.24
where the time goes:
time: 618 us; the launch traced here: 617 us
  waiting for transfers between devices  351 us (57%)
  blocking collectives  128 us (21%)
  matrix products  54.7 us (9%)
  local copies, waits for them, and re-layouts  43.2 us (7%)
  other arithmetic  22.2 us (4%)
  between operations  16.5 us (3%)
    unnamed x18, waiting for transfers between devices  60.2 us
    reduce_scatter x1, waiting for transfers between devices, on_device(): lax.psum_scatter(grads[8], ('dp', 'ctx'), scatter_dimension=0, tiled=True)  55.7 us
    reduce_scatter x1, waiting for transfers between devices, on_device(): lax.psum_scatter(grads[10], ('dp', 'ctx'), scatter_dimension=1, tiled=True)  55.1 us
    reduce_scatter x1, waiting for transfers between devices, on_device(): lax.psum_scatter(grads[2], ('dp', 'ctx'), scatter_dimension=0, tiled=True)  50.1 us
    psum x1, waiting for transfers between devices, backward_pass(): lax.psum(back_product(grad_inner, weight_up).astype(jnp.bfloat16), 'tensor')  37.8 us
    unnamed x215, local copies, waits for them, and re-layouts  35.4 us
    psum x1, waiting for transfers between devices, forward_pass(): lax.psum(row_product(activ, weight_down).astype(jnp.bfloat16), 'tensor')  29 us
    all_gather x1, waiting for transfers between devices, on_device(): lax.all_gather(contract_out, ('dp', 'ctx'), axis=1, tiled=True)  26.9 us
  transfers between devices with their start and end apart: 14, of which 12 were waited for; matrix products, arithmetic and copies ran while one was open for 12% of the time, Pallas kernels for 0%

commit v1 on v0

v1 whole, which is shorter than its diff:
```python
import functools

import jax
import jax.numpy as jnp
from jax import lax
from jax.experimental import pallas as pl
from jax.experimental.pallas import tpu as pltpu
from jax.sharding import PartitionSpec as P

HD = 64
BUFFER = 64
LANES = 128
ROWS = 16
TILE = 256
MESH = pl.DeviceIdType.MESH
F32 = jnp.float32
BF16 = jnp.bfloat16

eps = 1e-06
neg_big = -1e30
root_half = 0.7071067811865476
inv_root_two_pi = 0.3989422804014327


def flip(index, bits):
    out, bit = index, 1
    while bit <= bits:
        if bits & bit:
            out = out + bit - 2 * bit * lax.rem(lax.div(index, bit), 2)
        bit *= 2
    return out


def nn(left, right):
    return jnp.dot(left, right, preferred_element_type=F32)


def nt(left, right):
    return lax.dot_general(left, right, (((1,), (1,)), ((), ())), preferred_element_type=F32)


def tn(left, right):
    return lax.dot_general(left, right, (((0,), (0,)), ((), ())), preferred_element_type=F32)


def norm_parts(values):
    mean = jnp.mean(values, axis=-1, keepdims=True)
    centered = values - mean
    spread = jnp.mean(centered * centered, axis=-1, keepdims=True)
    inv = lax.rsqrt(spread + eps)
    return centered * inv, inv


def block_kernel(
    sizes,
    tok,
    cot,
    keep,
    win,
    wot,
    wup,
    wdt,
    vec,
    out_block,
    out_tokens,
    out_win,
    out_wot,
    out_wup,
    out_wdt,
    out_vec,
    g_win,
    g_wot,
    g_wup,
    g_wdt,
    g_vec,
    vx,
    n1,
    h1,
    qkv,
    wq,
    wk,
    stat,
    alng,
    mixed,
    first,
    h2,
    ga,
    act,
    gi,
    part2,
    parts,
    part1,
    recv2,
    recvs,
    recv1,
    gfirst,
    gdown,
    gball,
    gm,
    do,
    dqkv,
    gv,
    vr_sib,
    vr_plane,
    vr_z,
    b_win,
    b_wot,
    b_wup,
    b_wdt,
    s_win,
    s_wot,
    s_wup,
    s_wdt,
    t_win,
    t_wot,
    t_wup,
    t_wdt,
    r_win,
    r_wot,
    r_wup,
    r_wdt,
    send_sem,
    recv_sem,
    local_sem,
):
    n_dp, n_ctx, n_t, images, slots, width, wide, hidden, part_rows, cut = sizes
    rows = images * slots
    total = slots * n_ctx
    heads = wide // HD
    half = n_ctx // 2
    group = n_dp * half
    scale = HD ** (-0.5)
    dp = lax.axis_index("dp")
    ctx = lax.axis_index("ctx")
    z = lax.axis_index("tensor")
    high, core = lax.div(ctx, 2), lax.rem(ctx, 2)
    me = dp * half + high
    sib = (dp, flip(ctx, 1), z)

    def plane(k):
        other = flip(me, k)
        return (lax.div(other, half), lax.rem(other, half) * 2 + core, z)

    def ctx_at(k):
        return flip(high, k) * 2 + core

    def zpeer(k):
        return (dp, ctx, flip(z, k))

    own = pl.ds(pl.multiple_of(ctx * slots, ROWS), slots)
    mine = pl.ds(pl.multiple_of(z * slots, ROWS), slots)

    def slot_at(index):
        return pl.ds(pl.multiple_of(index * slots, ROWS), slots)

    def lane_at(index, size):
        return pl.ds(pl.multiple_of(index * size, size), size)

    count = [0, 0]
    pending = []

    def send(src, dst, device):
        index = count[0]
        count[0] += 1
        copy = pltpu.make_async_remote_copy(
            src_ref=src,
            dst_ref=dst,
            send_sem=send_sem.at[index],
            recv_sem=recv_sem.at[index],
            device_id=device,
            device_id_type=MESH,
        )
        copy.start()
        pending.append(copy)
        return copy

    def complete(copy):
        pending[:] = [other for other in pending if other is not copy]
        copy.wait()

    def local(src, dst):
        index = count[1]
        count[1] += 1
        copy = pltpu.make_async_copy(src, dst, local_sem.at[index])
        copy.start()
        return copy

    planes = range(1, group)
    zs = range(1, n_t)

    barrier = pltpu.get_barrier_semaphore()
    for device in [plane(k) for k in planes] + [sib] + [zpeer(k) for k in zs]:
        pl.semaphore_signal(barrier, inc=1, device_id=device, device_id_type=MESH)
    pl.semaphore_wait(barrier, group + n_t - 1)

    def gather_start(src, at):
        keep_own = local(src, at(me, core))
        far = [send(src, at(me, core), plane(k)) for k in planes]
        near = send(src, at(me, core), sib)
        return keep_own, far, near

    def gather_forward(started, at):
        started[0].wait()
        out = []
        for k in planes:
            started[1][k - 1].wait_recv()
            there = at(flip(me, k), core)
            out.append(send(there, there, sib))
        return out

    def gather_finish(started, passed):
        started[2].wait_recv()
        for copy in passed:
            copy.wait_recv()

    def ctx_start(at):
        far = [send(at(ctx), at(ctx), (dp, ctx_at(k), z)) for k in range(1, half)]
        return far, send(at(ctx), at(ctx), sib)

    def ctx_forward(started, at):
        out = []
        for k in range(1, half):
            started[0][k - 1].wait_recv()
            out.append(send(at(ctx_at(k)), at(ctx_at(k)), sib))
        return out

    def ctx_finish(started, passed):
        started[1].wait_recv()
        for copy in passed:
            copy.wait_recv()

    def at_win(m, c):
        return g_win.at[m, c]

    def at_wot(m, c):
        return g_wot.at[m, c, :, lane_at(z, wide)]

    def at_wup(m, c):
        return g_wup.at[m, c]

    def at_wdt(m, c):
        return g_wdt.at[m, c]

    def at_vec(m, c):
        return g_vec.at[m, c]

    gv[...] = jnp.zeros_like(gv)
    vec_started = gather_start(vec, at_vec)
    win_started = gather_start(win, at_win)
    wot_started = gather_start(wot, at_wot)

    def first_norm(step, carry):
        at = pl.ds(pl.multiple_of(step * ROWS, ROWS), ROWS)
        normed, _ = norm_parts(tok[at, :].astype(F32))
        n1[at, :] = normed
        return carry

    lax.fori_loop(0, rows // ROWS, first_norm, 0)
    wup_started = gather_start(wup, at_wup)

    vec_passed = gather_forward(vec_started, at_vec)
    gather_finish(vec_started, vec_passed)
    piece = width // (2 * group)
    source = lax.broadcasted_iota(jnp.int32, (LANES, width), 0)
    target = lax.broadcasted_iota(jnp.int32, (LANES, width), 1)
    unit = (target // HD == source // cut).astype(jnp.int32)
    inside = target % HD - source % cut

    def place(index, carry):
        by_width, by_unit = carry
        shares = g_vec[lax.div(index, 2), lax.rem(index, 2)]
        one = jnp.where(target - source == index * piece, 1.0, 0.0).astype(BF16)
        two = jnp.where((unit == 1) & (inside == index * cut), 1.0, 0.0).astype(BF16)
        return by_width + nn(shares, one), by_unit + nn(shares, two)

    zero = jnp.zeros((ROWS, width), F32)
    by_width, by_unit = lax.fori_loop(0, 2 * group, place, (zero, zero))
    row_id = lax.broadcasted_iota(jnp.int32, (ROWS, width), 0)
    vx[...] = jnp.where(row_id < 6, by_width, by_unit)

    def first_hidden(step, carry):
        at = pl.ds(pl.multiple_of(step * ROWS, ROWS), ROWS)
        h1[at, :] = (n1[at, :] * vx[0:1, :] + vx[1:2, :]).astype(BF16)
        return carry

    lax.fori_loop(0, rows // ROWS, first_hidden, 0)

    lengths = BUFFER + jnp.sum(keep[...], axis=1, keepdims=True)
    slot_id = lax.broadcasted_iota(jnp.int32, (slots, 1), 0) + ctx * slots
    key_id = lax.broadcasted_iota(jnp.int32, (1, total), 1)
    head_of = lax.broadcasted_iota(jnp.int32, (slots, wide), 1) // HD
    spot = lax.broadcasted_iota(jnp.int32, (slots, total), 1) == slot_id

    def stack_heads(block):
        wider = block.astype(F32)
        return jnp.concatenate(
            [jnp.where(head_of == h, wider, 0.0).astype(BF16) for h in range(heads)], axis=0
        )

    def pick_heads(block):
        out = jnp.where(head_of == 0, block[0:slots], 0.0)
        for h in range(1, heads):
            out = jnp.where(head_of == h, block[h * slots : (h + 1) * slots], out)
        return out

    def put_rows(ref, image, column):
        for h in range(heads):
            part = jnp.where(spot, column[h * slots : (h + 1) * slots], 0.0)
            line = image * heads + h
            ref[ctx, line : line + 1, :] = jnp.sum(part, axis=0, keepdims=True)

    win_passed = gather_forward(win_started, at_win)
    wot_passed = gather_forward(wot_started, at_wot)
    def wot_half(index, c):
        return g_wot.at[:, c, :, lane_at(index, wide)]

    wot_z = [send(wot_half(z, core), wot_half(z, core), zpeer(k)) for k in zs]
    gather_finish(win_started, win_passed)

    def project(j, bias):
        weight = g_win[:, :, :, j * wide : (j + 1) * wide].reshape(width, wide)
        out = nn(h1[...], weight)
        if bias is not None:
            out = out + vx[bias : bias + 1, 0:wide]
        qkv[:, own, j * wide : (j + 1) * wide] = out.astype(BF16).reshape(images, slots, wide)

    project(1, None)
    project(2, 8)

    def at_kv(index):
        return qkv.at[:, slot_at(index), wide : 3 * wide]

    def at_q(index):
        return qkv.at[:, slot_at(index), 0:wide]

    kv_started = ctx_start(at_kv)
    project(0, 7)
    q_started = ctx_start(at_q)
    wdt_started = gather_start(wdt, at_wdt)
    kv_passed = ctx_forward(kv_started, at_kv)
    ctx_finish(kv_started, kv_passed)

    def at_mixed(index, image):
        return mixed.at[image * slots : (image + 1) * slots, lane_at(index, wide)]

    mixed_sent = []
    for image in range(images):
        key_live = key_id < lengths[image : image + 1, :]
        stacked = stack_heads(qkv[image, own, 0:wide])
        scores = nt(stacked, qkv[image, :, wide : 2 * wide]) * scale
        scores = jnp.where(key_live, scores, neg_big)
        top = jnp.max(scores, axis=-1, keepdims=True)
        expo = jnp.exp(scores - top)
        whole = jnp.sum(expo, axis=-1, keepdims=True)
        probs = expo / whole
        wq[image] = probs
        put_rows(stat, image, top + jnp.log(whole))
        out = nn(probs.astype(BF16), qkv[image, :, 2 * wide : 3 * wide])
        mixed[image * slots : (image + 1) * slots, lane_at(z, wide)] = pick_heads(out).astype(BF16)
        mixed_sent.append(
            [send(at_mixed(z, image), at_mixed(z, image), zpeer(k)) for k in zs]
        )

    def at_stat(index):
        return stat.at[index]

    stat_started = ctx_start(at_stat)
    q_passed = ctx_forward(q_started, at_q)
    stat_passed = ctx_forward(stat_started, at_stat)
    gather_finish(wot_started, wot_passed)
    wup_passed = gather_forward(wup_started, at_wup)
    wot_more = []
    for k in zs:
        wot_z[k - 1].wait_recv()
        there = wot_half(flip(z, k), core)
        wot_more.append(send(there, there, sib))
    wdt_passed = gather_forward(wdt_started, at_wdt)

    row_live = []
    for image in range(images):
        row_live.append(slot_id < lengths[image : image + 1, :])
        at = slice(image * slots, (image + 1) * slots)
        gdown[at, :] = jnp.where(row_live[image], cot[at, :].astype(F32), 0.0).astype(BF16)
    gather_finish(wdt_started, wdt_passed)

    def down_back(step, carry):
        at = lane_at(step, TILE)
        ga[:, at] = nn(gdown[...], g_wdt[:, :, :, at].reshape(width, TILE))
        return carry

    lax.fori_loop(0, hidden // TILE, down_back, 0)

    ctx_finish(q_started, q_passed)
    ctx_finish(stat_started, stat_passed)
    for image in range(images):
        stacked = stack_heads(qkv[image, own, wide : 2 * wide])
        scores = nt(stacked, qkv[image, :, 0:wide]) * scale
        for h in range(heads):
            line = image * heads + h
            level = stat[0, line : line + 1, :]
            for other in range(1, n_ctx):
                level = level + stat[other, line : line + 1, :]
            block = scores[h * slots : (h + 1) * slots]
            block = jnp.where(row_live[image], block, neg_big)
            wk[image, h * slots : (h + 1) * slots, :] = jnp.exp(block - level)

    for copies in mixed_sent:
        for copy in copies:
            copy.wait_recv()
    for copy in wot_more:
        copy.wait_recv()

    def project_out(step, carry):
        some = group // (width // TILE)
        weight = g_wot[pl.ds(step * some, some)].reshape(TILE, n_t * wide)
        first[:, lane_at(step, TILE)] = nt(mixed[...], weight)
        return carry

    lax.fori_loop(0, width // TILE, project_out, 0)

    def second_norm(step, carry):
        at = pl.ds(pl.multiple_of(step * ROWS, ROWS), ROWS)
        value = tok[at, :].astype(F32) + first[at, :] + vx[2:3, :]
        first[at, :] = value
        normed, _ = norm_parts(value)
        h2[at, :] = (normed * vx[3:4, :] + vx[4:5, :]).astype(BF16)
        return carry

    lax.fori_loop(0, rows // ROWS, second_norm, 0)

    gather_finish(wup_started, wup_passed)

    def expand(step, carry):
        at = lane_at(step, TILE)
        inner = nn(h2[...], g_wup[:, :, :, at].reshape(width, TILE)) + vx[6:7, at]
        share = 0.5 * (1.0 + lax.erf(inner * root_half))
        act[:, at] = (inner * share).astype(BF16)
        slope = share + inner * jnp.exp(-0.5 * inner * inner) * inv_root_two_pi
        grad = (ga[:, at] * slope).astype(BF16)
        gi[:, at] = grad
        gv[8:9, at] = jnp.sum(grad.astype(F32), axis=0, keepdims=True)
        return carry

    lax.fori_loop(0, hidden // TILE, expand, 0)

    def up_back(step, carry):
        some = group // (width // TILE)
        weight = g_wup[pl.ds(step * some, some)].reshape(TILE, hidden)
        part2[:, lane_at(step, TILE)] = nt(gi[...], weight).astype(BF16)
        return carry

    lax.fori_loop(0, width // TILE, up_back, 0)

    def scatter(part, recv):
        return [
            send(part.at[slot_at(flip(z, k)), :], recv.at[k - 1], zpeer(k)) for k in reversed(zs)
        ]

    def arrived(part, recv, at):
        out = part[pl.ds(pl.multiple_of(z * slots + at, ROWS), ROWS), :].astype(F32)
        for k in zs:
            out = out + recv[k - 1, pl.ds(pl.multiple_of(at, ROWS), ROWS), :].astype(F32)
        return out

    sent2 = scatter(part2, recv2)

    def wide_grad(buf, left, right, lanes):
        def one(step, carry):
            at = lane_at(step, TILE)
            out = tn(left[...], right[:, at]).astype(BF16)
            buf[:, :, :, at] = out.reshape(group, 2, piece, TILE)
            return carry

        lax.fori_loop(0, lanes // TILE, one, 0)

    def grad_near(buf, near):
        return send(buf.at[:, 1 - core], near, sib)

    def grad_far(copy, buf, near, both, recv):
        copy.wait_recv()

        def one(m, carry):
            both[m] = (buf[m, core].astype(F32) + near[m].astype(F32)).astype(BF16)
            return carry

        lax.fori_loop(0, group, one, 0)
        return [send(both.at[flip(me, k)], recv.at[k - 1], plane(k)) for k in planes]

    def grad_last(copies, both, recv, out):
        for copy in copies:
            copy.wait_recv()
        value = both[me].astype(F32)
        for k in planes:
            value = value + recv[k - 1].astype(F32)
        out[...] = value

    def contract(step, carry):
        some = group // (width // TILE)
        weight = g_wdt[pl.ds(step * some, some)].reshape(TILE, hidden)
        parts[:, lane_at(step, TILE)] = nt(act[...], weight).astype(BF16)
        return carry

    lax.fori_loop(0, width // TILE, contract, 0)
    sents = scatter(parts, recvs)
    wide_grad(b_wdt, gdown, act, hidden)
    wdt_near = grad_near(b_wdt, s_wdt)
    wide_grad(b_wup, h2, gi, hidden)
    wup_near = grad_near(b_wup, s_wup)
    wdt_far = grad_far(wdt_near, b_wdt, s_wdt, t_wdt, r_wdt)
    wup_far = grad_far(wup_near, b_wup, s_wup, t_wup, r_wup)

    for copy in sent2:
        copy.wait_recv()
    own_live = slot_id < jnp.sum(
        jnp.where(lax.broadcasted_iota(jnp.int32, (images, 1), 0) == z, lengths, 0),
        axis=0,
        keepdims=True,
    )

    def add_line(line, value):
        gv[line : line + 1, :] += jnp.sum(value, axis=0, keepdims=True)

    def second_back(step, carry):
        at = step * ROWS
        here = pl.ds(pl.multiple_of(z * slots + at, ROWS), ROWS)
        grad = arrived(part2, recv2, at)
        normed, inv = norm_parts(first[here, :])
        add_line(3, grad * normed)
        add_line(4, grad)
        scaled = grad * vx[3:4, :]
        inner = (
            scaled
            - jnp.mean(scaled, axis=-1, keepdims=True)
            - normed * jnp.mean(scaled * normed, axis=-1, keepdims=True)
        )
        rows_grad = gdown[here, :].astype(F32)
        add_line(5, rows_grad)
        value = rows_grad + inner * inv
        add_line(2, value)
        gfirst[pl.ds(pl.multiple_of(at, ROWS), ROWS), :] = value
        return carry

    lax.fori_loop(0, slots // ROWS, second_back, 0)
    gball[mine, :] = gfirst[...].astype(BF16)

    def mixed_back(step, carry):
        at = lane_at(step, wide)
        weight = g_wot[:, :, :, at].reshape(width, wide)
        gm[:, at] = nn(gball[mine, :], weight).astype(BF16)
        return carry

    lax.fori_loop(0, n_t, mixed_back, 0)
    to_heads = [
        send(gm.at[:, lane_at(flip(z, k), wide)], do.at[z, own, :], zpeer(k)) for k in reversed(zs)
    ]
    do[z, own, :] = gm[:, lane_at(z, wide)]

    rows_sent = [send(gball.at[mine, :], gball.at[mine, :], zpeer(k)) for k in zs]
    for copy in to_heads:
        copy.wait_recv()

    def at_do(index):
        return do.at[:, slot_at(index), :]

    do_started = ctx_start(at_do)

    for image in range(images):
        stacked = stack_heads(do[image, own, :])
        grad_probs = nt(stacked, qkv[image, :, 2 * wide : 3 * wide])
        weights = wq[image]
        along = jnp.sum(grad_probs * weights, axis=-1, keepdims=True)
        put_rows(alng, image, along)
        grad_scores = (weights * (grad_probs - along)).astype(BF16)
        out = pick_heads(nn(grad_scores, qkv[image, :, wide : 2 * wide])) * scale
        dqkv[image * slots : (image + 1) * slots, 0:wide] = out.astype(BF16)

    def at_along(index):
        return alng.at[index]

    along_started = ctx_start(at_along)
    do_passed = ctx_forward(do_started, at_do)
    along_passed = ctx_forward(along_started, at_along)
    ctx_finish(do_started, do_passed)
    ctx_finish(along_started, along_passed)

    for image in range(images):
        stacked = stack_heads(qkv[image, own, 2 * wide : 3 * wide])
        grad_probs = nt(stacked, do[image])
        weights = wk[image]
        lines = []
        for h in range(heads):
            line = image * heads + h
            level = alng[0, line : line + 1, :]
            for other in range(1, n_ctx):
                level = level + alng[other, line : line + 1, :]
            lines.append(grad_probs[h * slots : (h + 1) * slots] - level)
        grad_scores = (weights * jnp.concatenate(lines, axis=0)).astype(BF16)
        at = slice(image * slots, (image + 1) * slots)
        out = pick_heads(nn(grad_scores, qkv[image, :, 0:wide])) * scale
        dqkv[at, wide : 2 * wide] = out.astype(BF16)
        out = pick_heads(nn(weights.astype(BF16), do[image]))
        dqkv[at, 2 * wide : 3 * wide] = out.astype(BF16)

    def in_back(step, carry):
        some = group // (width // TILE)
        weight = g_win[pl.ds(step * some, some)].reshape(TILE, 3 * wide)
        part1[:, lane_at(step, TILE)] = nt(dqkv[...], weight).astype(BF16)
        return carry

    lax.fori_loop(0, width // TILE, in_back, 0)
    sent1 = scatter(part1, recv1)

    wide_grad(b_win, h1, dqkv, 3 * wide)
    win_near = grad_near(b_win, s_win)
    for copy in rows_sent:
        copy.wait_recv()

    out = tn(gball[...], mixed[:, lane_at(z, wide)]).astype(BF16)
    b_wot[...] = out.reshape(group, 2, piece, wide)
    wot_near = grad_near(b_wot, s_wot)
    gv[9:10, 0:wide] = jnp.sum(dqkv[:, 0:wide].astype(F32), axis=0, keepdims=True)
    gv[10:11, 0:wide] = jnp.sum(dqkv[:, 2 * wide : 3 * wide].astype(F32), axis=0, keepdims=True)
    win_far = grad_far(win_near, b_win, s_win, t_win, r_win)
    wot_far = grad_far(wot_near, b_wot, s_wot, t_wot, r_wot)

    for copy in sents:
        copy.wait_recv()

    def block_rows(step, carry):
        at = step * ROWS
        here = pl.ds(pl.multiple_of(z * slots + at, ROWS), ROWS)
        value = first[here, :] + arrived(parts, recvs, at) + vx[5:6, :]
        out_block[here, :] = value.astype(BF16)
        return carry

    lax.fori_loop(0, slots // ROWS, block_rows, 0)
    out_block[mine, :] = jnp.where(own_live, out_block[mine, :].astype(F32), 0.0).astype(BF16)

    for copy in sent1:
        copy.wait_recv()

    def first_back(step, carry):
        at = step * ROWS
        here = pl.ds(pl.multiple_of(z * slots + at, ROWS), ROWS)
        grad = arrived(part1, recv1, at)
        normed, inv = norm_parts(tok[here, :].astype(F32))
        add_line(0, grad * normed)
        add_line(1, grad)
        scaled = grad * vx[0:1, :]
        inner = (
            scaled
            - jnp.mean(scaled, axis=-1, keepdims=True)
            - normed * jnp.mean(scaled * normed, axis=-1, keepdims=True)
        )
        value = gfirst[pl.ds(pl.multiple_of(at, ROWS), ROWS), :] + inner * inv
        out_tokens[here, :] = value.astype(BF16)
        return carry

    lax.fori_loop(0, slots // ROWS, first_back, 0)
    tail = [send(out_tokens.at[mine, :], out_tokens.at[mine, :], zpeer(k)) for k in reversed(zs)]
    tail += [send(out_block.at[mine, :], out_block.at[mine, :], zpeer(k)) for k in reversed(zs)]

    near = send(gv, vr_sib, sib)
    complete(near)
    gv[...] = gv[...] + vr_sib[...]
    far = [send(gv, vr_plane.at[k - 1], plane(k)) for k in planes]
    for copy in far:
        complete(copy)
    value = gv[...]
    for k in planes:
        value = value + vr_plane[k - 1]
    gv[...] = value
    far = [send(gv.at[0:8], vr_z.at[k - 1], zpeer(k)) for k in zs]

    grad_last(wdt_far, t_wdt, r_wdt, out_wdt)
    grad_last(wup_far, t_wup, r_wup, out_wup)
    grad_last(win_far, t_win, r_win, out_win)
    grad_last(wot_far, t_wot, r_wot, out_wot)

    for copy in far:
        copy.wait_recv()
    value = gv[0:8, :]
    for k in zs:
        value = value + vr_z[k - 1]
    out_vec[0:8, :] = value
    out_vec[8:16, :] = gv[8:16, :]
    for copy in tail:
        copy.wait_recv()
    for copy in pending:
        copy.wait_send()


def on_device(
    mesh_shape,
    tokens,
    keep_mask,
    cotangent,
    first_gain,
    first_shift,
    attend_in,
    attend_bias,
    attend_out,
    out_bias,
    second_gain,
    second_shift,
    expand_in,
    expand_bias,
    contract_out,
    contract_bias,
):
    n_dp, n_ctx, n_t = mesh_shape
    images, slots, width = tokens.shape
    piece, _, wide = attend_in.shape
    hidden = expand_in.shape[1]
    cut = expand_bias.shape[1]
    rows = images * slots
    group = n_dp * n_ctx // 2
    total = slots * n_ctx
    heads = wide // HD

    def line(values):
        values = values.reshape(-1)
        return jnp.pad(values, (0, LANES - values.shape[0]))

    lines = [
        first_gain,
        first_shift,
        out_bias,
        second_gain,
        second_shift,
        contract_bias,
        expand_bias,
        attend_bias[0],
        attend_bias[1],
    ]
    vec = jnp.stack([line(v) for v in lines])
    vec = jnp.pad(vec, ((0, ROWS - len(lines)), (0, 0)))
    sizes = (n_dp, n_ctx, n_t, images, slots, width, wide, hidden, piece, cut)
    widths = (3 * wide, wide, hidden, hidden)
    vmem = pl.BlockSpec(memory_space=pltpu.VMEM)
    scratch = [
        pltpu.VMEM((group, 2, piece, 3 * wide), BF16),
        pltpu.VMEM((group, 2, piece, n_t * wide), BF16),
        pltpu.VMEM((group, 2, piece, hidden), BF16),
        pltpu.VMEM((group, 2, piece, hidden), BF16),
        pltpu.VMEM((group, 2, ROWS, LANES), BF16),
        pltpu.VMEM((ROWS, width), F32),
        pltpu.VMEM((rows, width), F32),
        pltpu.VMEM((rows, width), BF16),
        pltpu.VMEM((images, total, 3 * wide), BF16),
        pltpu.VMEM((images, heads * slots, total), F32),
        pltpu.VMEM((images, heads * slots, total), F32),
        pltpu.VMEM((n_ctx, images * heads, total), F32),
        pltpu.VMEM((n_ctx, images * heads, total), F32),
        pltpu.VMEM((rows, n_t * wide), BF16),
        pltpu.VMEM((rows, width), F32),
        pltpu.VMEM((rows, width), BF16),
        pltpu.VMEM((rows, hidden), F32),
        pltpu.VMEM((rows, hidden), BF16),
        pltpu.VMEM((rows, hidden), BF16),
        pltpu.VMEM((rows, width), BF16),
        pltpu.VMEM((rows, width), BF16),
        pltpu.VMEM((rows, width), BF16),
        pltpu.VMEM((n_t - 1, slots, width), BF16),
        pltpu.VMEM((n_t - 1, slots, width), BF16),
        pltpu.VMEM((n_t - 1, slots, width), BF16),
        pltpu.VMEM((slots, width), F32),
        pltpu.VMEM((rows, width), BF16),
        pltpu.VMEM((rows, width), BF16),
        pltpu.VMEM((slots, n_t * wide), BF16),
        pltpu.VMEM((images, total, wide), BF16),
        pltpu.VMEM((rows, 3 * wide), BF16),
        pltpu.VMEM((ROWS, width), F32),
        pltpu.VMEM((ROWS, width), F32),
        pltpu.VMEM((group - 1, ROWS, width), F32),
        pltpu.VMEM((n_t - 1, 8, width), F32),
    ]
    scratch += [pltpu.VMEM((group, 2, piece, n), BF16) for n in widths]
    scratch += [pltpu.VMEM((group, piece, n), BF16) for n in widths]
    scratch += [pltpu.VMEM((group, piece, n), BF16) for n in widths]
    scratch += [pltpu.VMEM((group - 1, piece, n), BF16) for n in widths]
    copies = 80 + 16 * group
    scratch += [
        pltpu.SemaphoreType.DMA((copies,)),
        pltpu.SemaphoreType.DMA((copies,)),
        pltpu.SemaphoreType.DMA((8,)),
    ]
    outs = pl.pallas_call(
        functools.partial(block_kernel, sizes),
        out_shape=(
            jax.ShapeDtypeStruct((rows, width), BF16),
            jax.ShapeDtypeStruct((rows, width), BF16),
            *[jax.ShapeDtypeStruct((piece, n), F32) for n in widths],
            jax.ShapeDtypeStruct((ROWS, width), F32),
        ),
        in_specs=[vmem] * 8,
        out_specs=(vmem,) * 7,
        scratch_shapes=scratch,
        compiler_params=pltpu.CompilerParams(
            collective_id=0, has_side_effects=True, vmem_limit_bytes=62 << 20
        ),
    )(
        tokens.reshape(rows, width),
        cotangent.reshape(rows, width),
        keep_mask,
        attend_in.reshape(piece, 3 * wide),
        attend_out.T,
        expand_in,
        contract_out.T,
        vec,
    )
    block_out, tokens_grad, d_win, d_wot, d_wup, d_wdt, d_vec = outs
    shard = lax.axis_index("dp") * n_ctx + lax.axis_index("ctx")

    def own(row):
        return lax.dynamic_slice(d_vec, (row, shard * piece), (1, piece)).reshape(piece)

    def own_units(row, units):
        grid = d_vec[row, : units * HD].reshape(units, HD)
        return lax.dynamic_slice(grid, (0, shard * cut), (units, cut))

    return (
        block_out.reshape(tokens.shape),
        tokens_grad.reshape(tokens.shape),
        own(0),
        own(1),
        d_win.reshape(attend_in.shape),
        jnp.stack([own_units(9, heads), own_units(10, heads)]),
        d_wot.T,
        own(2),
        own(3),
        own(4),
        d_wup,
        own_units(8, hidden // HD),
        d_wdt.T,
        own(5),
    )


def solution(mesh):
    shape = (mesh.shape["dp"], mesh.shape["ctx"], mesh.shape["tensor"])
    vector = P(("dp", "ctx"))
    params = (
        vector,
        vector,
        P(("dp", "ctx"), None, "tensor"),
        P(None, "tensor", ("dp", "ctx")),
        P("tensor", ("dp", "ctx")),
        vector,
        vector,
        vector,
        P(("dp", "ctx"), "tensor"),
        P("tensor", ("dp", "ctx")),
        P("tensor", ("dp", "ctx")),
        vector,
    )
    rows = P("dp", "ctx", None)
    return jax.shard_map(
        functools.partial(on_device, shape),
        mesh=mesh,
        in_specs=(rows, P("dp", None), rows, *params),
        out_specs=(rows, rows, *params),
        check_vma=False,
    )
```

time: 618 us -> 185 us (0.30)
  waiting for transfers between devices: 351 us -> 0 us
  Pallas kernels: 0 us -> 165 us
  blocking collectives: 128 us -> 0 us
  matrix products: 54.7 us -> 0 us
  local copies, waits for them, and re-layouts: 43.2 us -> 18.2 us
  other arithmetic: 22.2 us -> 0.6 us
  between operations: 16.5 us -> 0.78 us
    pallas_call x0 -> x1, Pallas kernels: none -> 165 us  [on_device(): pl.pallas_call(functools.partial(block_kernel, sizes), out_shape=(jax.Sha...]
    reduce_scatter x4 -> x0, waiting for transfers between devices: 165 us -> none  [the longest x1 55.7 us: on_device(): lax.psum_scatter(grads[8], ('dp', 'ctx'), scatter_dimension=0, tiled=True)]
    all_gather x13 -> x0, blocking collectives: 104 us -> none  [the longest x2 12.4 us: forward_pass(): lax.all_gather(keys, 'ctx', axis=1, tiled=True)]
    psum x3 -> x0, waiting for transfers between devices: 73 us -> none  [the longest x1 37.8 us: backward_pass(): lax.psum(back_product(grad_inner, weight_up).astype(jnp.bfloat16), 'tensor')]
    unnamed x18 -> x0, waiting for transfers between devices: 60.2 us -> none
    dot_general x36 -> x0, matrix products: 54.7 us -> none  [the longest x6 11.2 us: row_product(): return jnp.dot(left, right, preferred_element_type=jnp.float32)]
    all_gather x3 -> x0, waiting for transfers between devices: 53.2 us -> none  [the longest x1 26.9 us: on_device(): lax.all_gather(contract_out, ('dp', 'ctx'), axis=1, tiled=True)]
    unnamed x1 -> x0, blocking collectives: 24.3 us -> none
  transfers between devices with their start and end apart: 14 -> 0, of which waited for: 12 -> 0; matrix products, arithmetic and copies ran while one was open for 12% -> 0% of each run, Pallas kernels for 0% -> 0%
where the time goes in v1:
time: 185 us
  Pallas kernels  165 us (89%)
  local copies, waits for them, and re-layouts  18.2 us (10%)
    pallas_call x1, Pallas kernels, on_device(): pl.pallas_call(functools.partial(block_kernel, sizes), out_shape=(jax.Sha...  165 us
    unnamed x41, local copies, waits for them, and re-layouts  11.8 us

profile of v1, /device:TPU:0, one launch (start us, length us, event | category | flops | bytes accessed | tf_op | source)
XLA Modules:
  0.0 184.6 jit_solution(17993029285256785724)
XLA Ops:
  0.7 0.7 copy-done.8
  1.3 0.1 reshape_squeeze.15
  1.4 0.1 reshape_squeeze.16
  1.5 0.7 copy-done.7
  2.2 0.1 copy.40
  2.3 0.1 stack.45
  2.5 0.6 copy-done.12
  3.2 0.6 pad.13.vec
  3.8 1.1 copy.37
  4.9 0.8 copy.41.win
  5.7 0.1 copy-done.4
  5.8 0.8 copy.39
  6.7 0.7 copy.38
  7.4 165.0 %shard_map.254 = (bf16[320,1024]{1,0:T(8,128)(2,1)}, bf16[320,1024]{1,0:T(8,128)(2,1)}, f32[128,768]{1,0:T(8,128)}, f32[128,256]{1,0:T(8,128)}, f32[128,1024]{1,...) custom-call(bf16[320,1024]{1,0:T(8,128)(2,1)} %bitcast.39, bf16[320,1024]{1,0:T(8,128)(2,1)} %bitcast.40, ...), custom_call_target="tpu_custom_call" | custom-call | tf_op jit(solution)/shard_map/pallas_call | solution.py:788
  172.4 0.8 slice_reduce_fusion.2
  173.2 0.1 reshape_squeeze.18
  173.3 0.1 reshape_squeeze.17
  173.5 0.6 pad_maximum_fusion
  174.1 1.5 dynamic-slice_bitcast_fusion.2
  175.6 0.8 slice_reduce_fusion
  176.4 0.1 constant_dynamic-slice_fusion
  176.5 0.7 copy.47
  177.2 1.1 copy.42
  178.4 0.9 copy.44
  179.3 0.1 copy-done.3
  179.4 1.0 copy.46
  180.4 0.8 copy.45
  181.2 0.8 copy.51
  182.0 0.5 copy-done
  182.5 0.8 copy.52
  183.3 0.4 copy-done.2
  183.8 0.8 copy.53
  (29 shorter events, 0.4 us)
Async XLA Ops:
  0.7 0.7 copy-start.8
  1.5 0.7 copy-start.7
  2.4 0.7 copy-start.12
  2.4 0.7 copy-start.13
  2.4 0.7 copy-start.14
  2.4 0.7 copy-start.9
  2.4 0.7 copy-start.10
  2.4 0.7 copy-start.11
  4.9 1.0 copy-start.4
  5.8 0.9 copy-start.6
  178.3 1.0 copy-start.3
  179.4 1.0 copy-start.5
  179.4 1.8 copy-start.1
  181.2 1.3 copy-start
  182.5 1.3 copy-start.2

commit v2 on v1

v2 whole, which is shorter than its diff:
```python
import functools

import jax
import jax.numpy as jnp
from jax import lax
from jax.experimental import pallas as pl
from jax.experimental.pallas import tpu as pltpu
from jax.sharding import PartitionSpec as P

HD = 64
BUFFER = 64
LANES = 128
ROWS = 16
TILE = 256
BLOCK = 32
MESH = pl.DeviceIdType.MESH
F32 = jnp.float32
BF16 = jnp.bfloat16

eps = 1e-06
neg_big = -1e30
root_half = 0.7071067811865476
inv_root_two_pi = 0.3989422804014327


def flip(index, bits):
    out, bit = index, 1
    while bit <= bits:
        if bits & bit:
            out = out + bit - 2 * bit * lax.rem(lax.div(index, bit), 2)
        bit *= 2
    return out


def nn(left, right):
    return jnp.dot(left, right, preferred_element_type=F32)


def nt(left, right):
    return lax.dot_general(left, right, (((1,), (1,)), ((), ())), preferred_element_type=F32)


def tn(left, right):
    return lax.dot_general(left, right, (((0,), (0,)), ((), ())), preferred_element_type=F32)


def turned(value, ref):
    return value if value.shape == ref.shape else value.T


def norm_parts(values):
    mean = jnp.mean(values, axis=-1, keepdims=True)
    centered = values - mean
    spread = jnp.mean(centered * centered, axis=-1, keepdims=True)
    inv = lax.rsqrt(spread + eps)
    return centered * inv, inv


def block_kernel(
    sizes,
    tok_in,
    cot_in,
    keep,
    win,
    attend_out,
    wup,
    contract_out,
    first_gain,
    first_shift,
    out_bias,
    second_gain,
    second_shift,
    contract_bias,
    expand_bias,
    attend_bias,
    out_block,
    out_tokens,
    out_win,
    out_wot,
    out_wup,
    out_wdt,
    out_vec,
    tok,
    cot,
    a_out,
    c_out,
    vec,
    g_win,
    g_wot,
    g_wup,
    g_wdt,
    g_vec,
    vx,
    n1,
    h1,
    qkv,
    wq,
    wk,
    stat,
    alng,
    mixed,
    first,
    h2,
    ga,
    act,
    gi,
    part2,
    parts,
    part1,
    recv2,
    recvs,
    recv1,
    gfirst,
    gdown,
    gown,
    gm,
    do,
    dqkv,
    block_own,
    tokens_own,
    gv,
    vr_sib,
    vr_plane,
    vr_z,
    b_win,
    b_wot,
    b_wup,
    b_wdt,
    s_win,
    s_wot,
    s_wup,
    s_wdt,
    t_win,
    t_wot,
    t_wup,
    t_wdt,
    r_win,
    r_wot,
    r_wup,
    r_wdt,
    o_wot,
    z_wot,
    f_win,
    f_wot,
    f_wup,
    f_wdt,
    send_sem,
    recv_sem,
    local_sem,
):
    n_dp, n_ctx, n_t, images, slots, width, wide, hidden, piece, cut = sizes
    rows = images * slots
    total = slots * n_ctx
    heads = wide // HD
    half = n_ctx // 2
    group = n_dp * half
    scale = HD ** (-0.5)
    dp = lax.axis_index("dp")
    ctx = lax.axis_index("ctx")
    z = lax.axis_index("tensor")
    high, core = lax.div(ctx, 2), lax.rem(ctx, 2)
    me = dp * half + high
    shard = me * 2 + core
    sib = (dp, flip(ctx, 1), z)

    def plane(k):
        other = flip(me, k)
        return (lax.div(other, half), lax.rem(other, half) * 2 + core, z)

    def ctx_at(k):
        return flip(high, k) * 2 + core

    def zpeer(k):
        return (dp, ctx, flip(z, k))

    def slot_at(index):
        return pl.ds(pl.multiple_of(index * slots, ROWS), slots)

    def lane_at(index, size):
        return pl.ds(pl.multiple_of(index * size, size), size)

    own = slot_at(ctx)
    mine = slot_at(z)

    count = [0, 0]
    pending = []

    def send(src, dst, device):
        index = count[0]
        count[0] += 1
        copy = pltpu.make_async_remote_copy(
            src_ref=src,
            dst_ref=dst,
            send_sem=send_sem.at[index],
            recv_sem=recv_sem.at[index],
            device_id=device,
            device_id_type=MESH,
        )
        copy.start()
        pending.append(copy)
        return copy

    def complete(copy):
        pending[:] = [other for other in pending if other is not copy]
        copy.wait()

    def local(src, dst):
        index = count[1]
        count[1] += 1
        copy = pltpu.make_async_copy(src, dst, local_sem.at[index])
        copy.start()
        return copy

    planes = range(1, group)
    zs = range(1, n_t)

    def at_win(m, c):
        return g_win.at[:, m, c]

    def at_wot(m, c):
        return g_wot.at[m, c, :, lane_at(z, wide)]

    def at_wup(m, c):
        return g_wup.at[m, c]

    def at_wdt(m, c):
        return g_wdt.at[m, c]

    def at_vec(m, c):
        return g_vec.at[m, c]

    barrier = pltpu.get_barrier_semaphore()
    for device in [plane(k) for k in planes] + [sib] + [zpeer(k) for k in zs]:
        pl.semaphore_signal(barrier, inc=1, device_id=device, device_id_type=MESH)
    a_out_load = local(attend_out, a_out)
    tok_load = local(tok_in, tok)
    win_own = local(win, at_win(me, core))
    c_out_load = local(contract_out, c_out)
    cot_load = local(cot_in, cot)
    wup_own = local(wup, at_wup(me, core))

    vec[...] = jnp.zeros_like(vec)
    for line, ref in enumerate(
        (first_gain, first_shift, out_bias, second_gain, second_shift, contract_bias)
    ):
        vec[line : line + 1, 0:piece] = ref[...].astype(F32)
    vec[8 : 8 + cut, 0 : hidden // HD] = expand_bias[...].astype(F32)
    for j in range(2):
        vec[16 + j * heads : 16 + (j + 1) * heads, 0:cut] = attend_bias[j].astype(F32)
    g_vec[me, core] = vec[...]
    gv[...] = jnp.zeros_like(gv)
    unit_one = (
        lax.broadcasted_iota(jnp.int32, (piece, piece), 0)
        == lax.broadcasted_iota(jnp.int32, (piece, piece), 1)
    ).astype(F32)
    unit_one = unit_one.astype(BF16)
    a_out_load.wait()
    g_wot[me, core, :, lane_at(z, wide)] = nt(unit_one, a_out[...]).astype(BF16)
    pl.semaphore_wait(barrier, group + n_t - 1)

    def gather_start(src, at):
        far = [send(src, at(me, core), plane(k)) for k in planes]
        return far, send(src, at(me, core), sib)

    def gather_forward(started, at):
        out = []
        for k in planes:
            started[0][k - 1].wait_recv()
            there = at(flip(me, k), core)
            out.append(send(there, there, sib))
        return out

    def gather_finish(started, passed):
        started[1].wait_recv()
        for copy in passed:
            copy.wait_recv()

    def ctx_start(at):
        far = [send(at(ctx), at(ctx), (dp, ctx_at(k), z)) for k in range(1, half)]
        return far, send(at(ctx), at(ctx), sib)

    def ctx_forward(started, at):
        out = []
        for k in range(1, half):
            started[0][k - 1].wait_recv()
            out.append(send(at(ctx_at(k)), at(ctx_at(k)), sib))
        return out

    def ctx_finish(started, passed):
        started[1].wait_recv()
        for copy in passed:
            copy.wait_recv()

    def wot_piece(m, index):
        return g_wot.at[m, core, :, lane_at(index, wide)]

    vec_started = gather_start(vec, at_vec)
    win_started = gather_start(win, at_win)
    wot_started = gather_start(at_wot(me, core), at_wot)
    wot_z = [[send(wot_piece(me, z), wot_piece(me, z), zpeer(k)) for k in zs]]

    tok_load.wait()

    def first_norm(step, carry):
        at = pl.ds(pl.multiple_of(step * BLOCK, BLOCK), BLOCK)
        normed, _ = norm_parts(tok[at, :].astype(F32))
        n1[at, :] = normed
        return carry

    lax.fori_loop(0, rows // BLOCK, first_norm, 0)

    vec_passed = gather_forward(vec_started, at_vec)
    gather_finish(vec_started, vec_passed)
    shape = (2 * ROWS, width)
    line_id = lax.broadcasted_iota(jnp.int32, shape, 0)
    lane_id = lax.broadcasted_iota(jnp.int32, shape, 1)
    source = lax.broadcasted_iota(jnp.int32, (LANES, width), 0)
    target = lax.broadcasted_iota(jnp.int32, (LANES, width), 1)
    by_unit = jnp.where(target // HD == source, 1.0, 0.0).astype(BF16)
    for_unit = lane_id % HD - (line_id - 8)
    for_head = lane_id // HD == (line_id - 16) % heads

    def place(index, carry):
        one, two, three = carry
        shares = g_vec[lax.div(index, 2), lax.rem(index, 2)].astype(BF16)
        by_width = jnp.where(target - source == index * piece, 1.0, 0.0).astype(BF16)
        by_channel = jnp.where(target % HD - source == index * cut, 1.0, 0.0).astype(BF16)
        one = one + nn(shares, by_width)
        two = two + jnp.where(for_unit == index * cut, nn(shares, by_unit), 0.0)
        three = three + jnp.where(for_head, nn(shares, by_channel), 0.0)
        return one, two, three

    zero = jnp.zeros(shape, F32)
    one, two, three = lax.fori_loop(0, 2 * group, place, (zero, zero, zero))
    vx[0:8, :] = one[0:8]
    vx[8:9, :] = jnp.sum(two[8 : 8 + cut], axis=0, keepdims=True)
    vx[9:10, :] = jnp.sum(three[16 : 16 + heads], axis=0, keepdims=True)
    vx[10:11, :] = jnp.sum(three[16 + heads : 16 + 2 * heads], axis=0, keepdims=True)

    def first_hidden(step, carry):
        at = pl.ds(pl.multiple_of(step * BLOCK, BLOCK), BLOCK)
        h1[at, :] = (n1[at, :] * vx[0:1, :] + vx[1:2, :]).astype(BF16)
        return carry

    lax.fori_loop(0, rows // BLOCK, first_hidden, 0)

    c_out_load.wait()

    def turn(step, carry):
        at = lane_at(step, TILE)
        g_wdt[me, core, :, at] = nt(unit_one, c_out[at, :]).astype(BF16)
        return carry

    lax.fori_loop(0, hidden // TILE, turn, 0)

    lengths = BUFFER + jnp.sum(keep[...], axis=1, keepdims=True)
    slot_id = lax.broadcasted_iota(jnp.int32, (slots, 1), 0) + ctx * slots
    key_id = lax.broadcasted_iota(jnp.int32, (1, total), 1)
    head_of = lax.broadcasted_iota(jnp.int32, (slots, wide), 1) // HD
    spot = lax.broadcasted_iota(jnp.int32, (slots, total), 1) == slot_id

    def stack_heads(block):
        wider = block.astype(F32)
        return jnp.concatenate(
            [jnp.where(head_of == h, wider, 0.0).astype(BF16) for h in range(heads)], axis=0
        )

    def pick_heads(block):
        out = jnp.where(head_of == 0, block[0:slots], 0.0)
        for h in range(1, heads):
            out = jnp.where(head_of == h, block[h * slots : (h + 1) * slots], out)
        return out

    def put_rows(ref, image, column):
        for h in range(heads):
            part = jnp.where(spot, column[h * slots : (h + 1) * slots], 0.0)
            line = image * heads + h
            ref[ctx, line : line + 1, :] = jnp.sum(part, axis=0, keepdims=True)

    win_passed = gather_forward(win_started, at_win)
    win_own.wait()
    gather_finish(win_started, win_passed)

    def project(j, bias):
        out = nn(h1[...], g_win[j].reshape(width, wide))
        if bias is not None:
            out = out + vx[bias : bias + 1, 0:wide]
        qkv[:, own, j * wide : (j + 1) * wide] = out.astype(BF16).reshape(images, slots, wide)

    def at_kv(index):
        return qkv.at[:, slot_at(index), wide : 3 * wide]

    def at_q(index):
        return qkv.at[:, slot_at(index), 0:wide]

    project(1, None)
    project(2, 10)
    kv_started = ctx_start(at_kv)
    wup_started = gather_start(wup, at_wup)
    wdt_started = gather_start(at_wdt(me, core), at_wdt)
    wot_passed = []
    for k in planes:
        wot_started[0][k - 1].wait_recv()
        there = wot_piece(flip(me, k), z)
        wot_z.append([send(there, there, zpeer(j)) for j in zs])
        wot_passed.append(send(there, there, sib))
    project(0, 9)
    q_started = ctx_start(at_q)
    kv_passed = ctx_forward(kv_started, at_kv)
    ctx_finish(kv_started, kv_passed)

    def at_mixed(index, image):
        return mixed.at[image * slots : (image + 1) * slots, lane_at(index, wide)]

    mixed_sent = []
    for image in range(images):
        key_live = key_id < lengths[image : image + 1, :]
        stacked = stack_heads(qkv[image, own, 0:wide])
        scores = nt(stacked, qkv[image, :, wide : 2 * wide]) * scale
        scores = jnp.where(key_live, scores, neg_big)
        top = jnp.max(scores, axis=-1, keepdims=True)
        expo = jnp.exp(scores - top)
        whole = jnp.sum(expo, axis=-1, keepdims=True)
        probs = expo / whole
        wq[image] = probs
        put_rows(stat, image, top + jnp.log(whole))
        out = nn(probs.astype(BF16), qkv[image, :, 2 * wide : 3 * wide])
        mixed[image * slots : (image + 1) * slots, lane_at(z, wide)] = pick_heads(out).astype(BF16)
        mixed_sent.append(
            [send(at_mixed(z, image), at_mixed(z, image), zpeer(k)) for k in reversed(zs)]
        )

    def at_stat(index):
        return stat.at[index]

    stat_started = ctx_start(at_stat)

    cot_load.wait()
    row_live = []
    for image in range(images):
        row_live.append(slot_id < lengths[image : image + 1, :])
        at = slice(image * slots, (image + 1) * slots)
        gdown[at, :] = jnp.where(row_live[image], cot[at, :].astype(F32), 0.0).astype(BF16)

    gather_finish(wot_started, wot_passed)
    wot_more = []
    for order, block in enumerate(wot_z):
        for k in zs:
            block[k - 1].wait_recv()
            there = wot_piece(flip(me, order), flip(z, k))
            wot_more.append(send(there, there, sib))
    wup_passed = gather_forward(wup_started, at_wup)
    wup_own.wait()
    wdt_passed = gather_forward(wdt_started, at_wdt)
    gather_finish(wdt_started, wdt_passed)

    def down_back(step, carry):
        at = lane_at(step, TILE)
        ga[:, at] = nn(gdown[...], g_wdt[:, :, :, at].reshape(width, TILE))
        return carry

    lax.fori_loop(0, hidden // TILE, down_back, 0)

    gather_finish(wup_started, wup_passed)
    for copy in wot_more:
        copy.wait_recv()
    for copies in mixed_sent:
        for copy in copies:
            copy.wait_recv()

    some = group // (width // TILE)

    def project_out(step, carry):
        weight = g_wot[pl.ds(step * some, some)].reshape(TILE, n_t * wide)
        first[:, lane_at(step, TILE)] = nt(mixed[...], weight)
        return carry

    lax.fori_loop(0, width // TILE, project_out, 0)

    def second_norm(step, carry):
        at = pl.ds(pl.multiple_of(step * BLOCK, BLOCK), BLOCK)
        value = tok[at, :].astype(F32) + first[at, :] + vx[2:3, :]
        first[at, :] = value
        normed, _ = norm_parts(value)
        h2[at, :] = (normed * vx[3:4, :] + vx[4:5, :]).astype(BF16)
        return carry

    lax.fori_loop(0, rows // BLOCK, second_norm, 0)

    def expand(step, carry):
        at = lane_at(step, TILE)
        inner = nn(h2[...], g_wup[:, :, :, at].reshape(width, TILE)) + vx[8:9, at]
        share = 0.5 * (1.0 + lax.erf(inner * root_half))
        act[:, at] = (inner * share).astype(BF16)
        slope = share + inner * jnp.exp(-0.5 * inner * inner) * inv_root_two_pi
        grad = (ga[:, at] * slope).astype(BF16)
        gi[:, at] = grad
        gv[8:9, at] = jnp.sum(grad.astype(F32), axis=0, keepdims=True)
        return carry

    lax.fori_loop(0, hidden // TILE, expand, 0)

    def up_back(step, carry):
        weight = g_wup[pl.ds(step * some, some)].reshape(TILE, hidden)
        part2[:, lane_at(step, TILE)] = nt(gi[...], weight).astype(BF16)
        return carry

    lax.fori_loop(0, width // TILE, up_back, 0)

    def scatter(part, recv, start, size):
        return [
            send(
                part.at[pl.ds(pl.multiple_of(flip(z, k) * slots + start, ROWS), size), :],
                recv.at[k - 1, start : start + size, :],
                zpeer(k),
            )
            for k in reversed(zs)
        ]

    def arrived(part, recv, at, size):
        out = part[pl.ds(pl.multiple_of(z * slots + at, ROWS), size), :].astype(F32)
        for k in zs:
            out = out + recv[k - 1, pl.ds(pl.multiple_of(at, ROWS), size), :].astype(F32)
        return out

    sent2 = scatter(part2, recv2, 0, slots)

    def contract(step, carry):
        weight = g_wdt[pl.ds(step * some, some)].reshape(TILE, hidden)
        parts[:, lane_at(step, TILE)] = nt(act[...], weight).astype(BF16)
        return carry

    lax.fori_loop(0, width // TILE, contract, 0)
    early = 2 * ROWS
    sents = [scatter(parts, recvs, 0, early)]

    def wide_grad(buf, left, right, lanes):
        def one(step, carry):
            at = lane_at(step, TILE)
            out = tn(left[...], right[:, at]).astype(BF16)
            buf[:, :, :, at] = out.reshape(group, 2, piece, TILE)
            return carry

        lax.fori_loop(0, lanes // TILE, one, 0)

    def grad_near(buf, near):
        return send(buf.at[:, 1 - core], near, sib)

    def grad_far(copy, buf, near, both, recv):
        copy.wait_recv()

        def one(m, carry):
            both[m] = (buf[m, core].astype(F32) + near[m].astype(F32)).astype(BF16)
            return carry

        lax.fori_loop(0, group, one, 0)
        return [send(both.at[flip(me, k)], recv.at[k - 1], plane(k)) for k in reversed(planes)]

    def grad_sum(copies, both, recv):
        for copy in copies:
            copy.wait_recv()
        value = both[me].astype(F32)
        for k in planes:
            value = value + recv[k - 1].astype(F32)
        return value

    wide_grad(b_wdt, gdown, act, hidden)
    wdt_near = grad_near(b_wdt, s_wdt)
    wide_grad(b_wup, h2, gi, hidden)
    wup_near = grad_near(b_wup, s_wup)
    wdt_far = grad_far(wdt_near, b_wdt, s_wdt, t_wdt, r_wdt)

    q_passed = ctx_forward(q_started, at_q)
    stat_passed = ctx_forward(stat_started, at_stat)
    ctx_finish(q_started, q_passed)
    ctx_finish(stat_started, stat_passed)
    for image in range(images):
        stacked = stack_heads(qkv[image, own, wide : 2 * wide])
        scores = nt(stacked, qkv[image, :, 0:wide]) * scale
        for h in range(heads):
            line = image * heads + h
            level = stat[0, line : line + 1, :]
            for other in range(1, n_ctx):
                level = level + stat[other, line : line + 1, :]
            block = scores[h * slots : (h + 1) * slots]
            block = jnp.where(row_live[image], block, neg_big)
            wk[image, h * slots : (h + 1) * slots, :] = jnp.exp(block - level)

    own_live = slot_id < jnp.sum(
        jnp.where(lax.broadcasted_iota(jnp.int32, (images, 1), 0) == z, lengths, 0),
        axis=0,
        keepdims=True,
    )

    def add_line(line, value):
        gv[line : line + 1, :] += jnp.sum(value, axis=0, keepdims=True)

    def norm_back(grad, normed, inv, gain):
        scaled = grad * gain
        inner = (
            scaled
            - jnp.mean(scaled, axis=-1, keepdims=True)
            - normed * jnp.mean(scaled * normed, axis=-1, keepdims=True)
        )
        return inner * inv

    for copy in sent2:
        copy.wait_recv()

    def second_back(step, carry):
        at = step * ROWS
        here = pl.ds(pl.multiple_of(z * slots + at, ROWS), ROWS)
        grad = arrived(part2, recv2, at, ROWS)
        normed, inv = norm_parts(first[here, :])
        rows_grad = gdown[here, :].astype(F32)
        value = rows_grad + norm_back(grad, normed, inv, vx[3:4, :])
        there = pl.ds(pl.multiple_of(at, ROWS), ROWS)
        gfirst[there, :] = value
        gown[there, :] = value.astype(BF16)
        add_line(3, grad * normed)
        add_line(4, grad)
        add_line(5, rows_grad)
        add_line(2, value)
        return carry

    lax.fori_loop(0, slots // ROWS, second_back, 0)

    def mixed_back(step, carry):
        at = lane_at(step, wide)
        weight = g_wot[:, :, :, at].reshape(width, wide)
        gm[:, at] = nn(gown[...], weight).astype(BF16)
        return carry

    lax.fori_loop(0, n_t, mixed_back, 0)
    to_heads = [
        send(gm.at[:, lane_at(flip(z, k), wide)], do.at[z, own, :], zpeer(k)) for k in reversed(zs)
    ]
    sents.append(scatter(parts, recvs, early, slots - early))
    do[z, own, :] = gm[:, lane_at(z, wide)]
    def out_grad(step, carry):
        at = lane_at(step, TILE)
        out = tn(gown[...], mixed[mine, at]).astype(BF16)
        b_wot[:, :, :, at] = out.reshape(group, 2, piece, TILE)
        return carry

    lax.fori_loop(0, n_t * wide // TILE, out_grad, 0)
    wot_near = grad_near(b_wot, s_wot)

    def block_rows(start, size, copies):
        for copy in copies:
            copy.wait_recv()
        here = pl.ds(pl.multiple_of(z * slots + start, ROWS), size)
        value = first[here, :] + arrived(parts, recvs, start, size) + vx[5:6, :]
        value = jnp.where(own_live[start : start + size], value, 0.0)
        block_own[start : start + size, :] = value.astype(BF16)
        source = block_own.at[start : start + size, :]
        keep_own = local(source, out_block.at[here, :])
        return [send(source, out_block.at[here, :], zpeer(k)) for k in reversed(zs)], keep_own

    block_early, block_kept = block_rows(0, early, sents[0])
    tail = block_early
    stays = [block_kept]

    for copy in to_heads:
        copy.wait_recv()

    def at_do(index):
        return do.at[:, slot_at(index), :]

    do_started = ctx_start(at_do)

    for image in range(images):
        stacked = stack_heads(do[image, own, :])
        grad_probs = nt(stacked, qkv[image, :, 2 * wide : 3 * wide])
        weights = wq[image]
        along = jnp.sum(grad_probs * weights, axis=-1, keepdims=True)
        put_rows(alng, image, along)
        grad_scores = (weights * (grad_probs - along)).astype(BF16)
        out = pick_heads(nn(grad_scores, qkv[image, :, wide : 2 * wide])) * scale
        dqkv[image * slots : (image + 1) * slots, 0:wide] = out.astype(BF16)

    def at_along(index):
        return alng.at[index]

    along_started = ctx_start(at_along)
    wot_far = grad_far(wot_near, b_wot, s_wot, t_wot, r_wot)
    wup_far = grad_far(wup_near, b_wup, s_wup, t_wup, r_wup)
    do_passed = ctx_forward(do_started, at_do)
    along_passed = ctx_forward(along_started, at_along)
    ctx_finish(do_started, do_passed)
    ctx_finish(along_started, along_passed)

    for image in range(images):
        stacked = stack_heads(qkv[image, own, 2 * wide : 3 * wide])
        grad_probs = nt(stacked, do[image])
        weights = wk[image]
        lines = []
        for h in range(heads):
            line = image * heads + h
            level = alng[0, line : line + 1, :]
            for other in range(1, n_ctx):
                level = level + alng[other, line : line + 1, :]
            lines.append(grad_probs[h * slots : (h + 1) * slots] - level)
        grad_scores = (weights * jnp.concatenate(lines, axis=0)).astype(BF16)
        at = slice(image * slots, (image + 1) * slots)
        out = pick_heads(nn(grad_scores, qkv[image, :, 0:wide])) * scale
        dqkv[at, wide : 2 * wide] = out.astype(BF16)
        out = pick_heads(nn(weights.astype(BF16), do[image]))
        dqkv[at, 2 * wide : 3 * wide] = out.astype(BF16)

    def in_back(step, carry):
        out = None
        for j in range(3):
            weight = g_win[j, pl.ds(step * some, some)].reshape(TILE, wide)
            term = nt(dqkv[:, j * wide : (j + 1) * wide], weight)
            out = term if out is None else out + term
        part1[:, lane_at(step, TILE)] = out.astype(BF16)
        return carry

    lax.fori_loop(0, width // TILE, in_back, 0)
    sent1 = scatter(part1, recv1, 0, slots)

    block_late, block_kept = block_rows(early, slots - early, sents[1])
    tail += block_late
    stays.append(block_kept)
    for j in range(3):
        out = tn(h1[...], dqkv[:, j * wide : (j + 1) * wide]).astype(BF16)
        b_win[j] = out.reshape(group, 2, piece, wide)
    win_near = send(b_win.at[:, :, 1 - core], s_win, sib)
    gv[9:10, 0:wide] = jnp.sum(dqkv[:, 0:wide].astype(F32), axis=0, keepdims=True)
    gv[10:11, 0:wide] = jnp.sum(dqkv[:, 2 * wide : 3 * wide].astype(F32), axis=0, keepdims=True)
    f_wdt[...] = turned(grad_sum(wdt_far, t_wdt, r_wdt), f_wdt)
    stays.append(local(f_wdt, out_wdt))
    win_near.wait_recv()
    for j in range(3):
        both = b_win[j, :, pl.ds(core, 1)].reshape(group, piece, wide).astype(F32)
        t_win[:, j] = (both + s_win[j].astype(F32)).astype(BF16)
    win_far = [send(t_win.at[flip(me, k)], r_win.at[k - 1], plane(k)) for k in reversed(planes)]

    whole_rows = grad_sum(wot_far, t_wot, r_wot)
    o_wot[...] = whole_rows.astype(BF16)
    to_owner = [
        send(o_wot.at[:, lane_at(flip(z, k), wide)], z_wot.at[k - 1], zpeer(k))
        for k in reversed(zs)
    ]
    f_wup[...] = grad_sum(wup_far, t_wup, r_wup)
    stays.append(local(f_wup, out_wup))

    for copy in sent1:
        copy.wait_recv()

    def first_back(step, carry):
        at = step * ROWS
        here = pl.ds(pl.multiple_of(z * slots + at, ROWS), ROWS)
        grad = arrived(part1, recv1, at, ROWS)
        normed, inv = norm_parts(tok[here, :].astype(F32))
        there = pl.ds(pl.multiple_of(at, ROWS), ROWS)
        value = gfirst[there, :] + norm_back(grad, normed, inv, vx[0:1, :])
        tokens_own[there, :] = value.astype(BF16)
        add_line(0, grad * normed)
        add_line(1, grad)
        return carry

    lax.fori_loop(0, slots // ROWS, first_back, 0)
    tail += [send(tokens_own, out_tokens.at[mine, :], zpeer(k)) for k in reversed(zs)]
    stays.append(local(tokens_own, out_tokens.at[mine, :]))

    near = send(gv, vr_sib, sib)
    complete(near)
    gv[...] = gv[...] + vr_sib[...]
    far = [send(gv, vr_plane.at[k - 1], plane(k)) for k in planes]
    f_win[...] = grad_sum(win_far, t_win, r_win)
    stays.append(local(f_win, out_win))
    for copy in far:
        complete(copy)
    value = gv[...]
    for k in planes:
        value = value + vr_plane[k - 1]
    gv[...] = value
    lanes = lane_at(lax.div(shard * piece, LANES), LANES)
    far = [send(gv.at[0:8, lanes], vr_z.at[k - 1], zpeer(k)) for k in zs]
    for copy in to_owner:
        copy.wait_recv()
    value = o_wot[:, lane_at(z, wide)].astype(F32)
    for k in zs:
        value = value + z_wot[k - 1].astype(F32)
    f_wot[...] = turned(value, f_wot)
    stays.append(local(f_wot, out_wot))
    for copy in far:
        complete(copy)
    value = gv[0:8, lanes]
    for k in zs:
        value = value + vr_z[k - 1]
    gv[0:8, lanes] = value
    stays.append(local(gv, out_vec))
    for copy in tail:
        copy.wait_recv()
    for copy in pending:
        copy.wait_send()
    for copy in stays:
        copy.wait()


def finish_call(sizes, *refs):
    finish_kernel(sizes, *refs[:13], refs[13:19], *refs[19:])


def finish_kernel(
    sizes,
    in_block,
    in_tokens,
    in_win,
    in_wot,
    in_wup,
    in_wdt,
    in_vec,
    block,
    tokens,
    win,
    wot,
    wup,
    wdt,
    vectors,
    units,
    biases,
    sems,
):
    n_ctx, piece, cut, wide, hidden, width = sizes
    shard = lax.axis_index("dp") * n_ctx + lax.axis_index("ctx")
    pairs = [(in_block, block), (in_tokens, tokens), (in_win, win)]
    pairs += [(in_wot, wot), (in_wup, wup), (in_wdt, wdt)]
    copies = [pltpu.make_async_copy(a, b, sems.at[i]) for i, (a, b) in enumerate(pairs)]
    for copy in copies:
        copy.start()

    def exact(left, right):
        return jnp.dot(left, right, precision=lax.Precision.HIGHEST, preferred_element_type=F32)

    heads = wide // HD
    lane = lax.broadcasted_iota(jnp.int32, (width, piece), 0)
    slot = lax.broadcasted_iota(jnp.int32, (width, piece), 1)
    part = exact(in_vec[0:8, :], jnp.where(lane - slot == shard * piece, 1.0, 0.0))
    for line in range(6):
        vectors[line][...] = part[line : line + 1]
    channel = lax.broadcasted_iota(jnp.int32, (cut, hidden), 0)
    lane = lax.broadcasted_iota(jnp.int32, (cut, hidden), 1)
    chosen = jnp.where(lane % HD - channel == shard * cut, in_vec[8:9, 0:hidden], 0.0)
    lane = lax.broadcasted_iota(jnp.int32, (hidden, hidden // HD), 0)
    slot = lax.broadcasted_iota(jnp.int32, (hidden, hidden // HD), 1)
    units[...] = exact(chosen, jnp.where(lane // HD == slot, 1.0, 0.0))
    lane = lax.broadcasted_iota(jnp.int32, (wide, cut), 0)
    slot = lax.broadcasted_iota(jnp.int32, (wide, cut), 1)
    pick = jnp.where(lane % HD - slot == shard * cut, 1.0, 0.0)
    head = lax.broadcasted_iota(jnp.int32, (heads, wide), 0)
    lane = lax.broadcasted_iota(jnp.int32, (heads, wide), 1)
    for j in range(2):
        chosen = jnp.where(lane // HD == head, in_vec[9 + j : 10 + j, 0:wide], 0.0)
        biases[j] = exact(chosen, pick)
    for copy in copies:
        copy.wait()


def on_device(
    mesh_shape,
    tokens,
    keep_mask,
    cotangent,
    first_gain,
    first_shift,
    attend_in,
    attend_bias,
    attend_out,
    out_bias,
    second_gain,
    second_shift,
    expand_in,
    expand_bias,
    contract_out,
    contract_bias,
):
    n_dp, n_ctx, n_t = mesh_shape
    images, slots, width = tokens.shape
    piece, _, wide = attend_in.shape
    hidden = expand_in.shape[1]
    cut = expand_bias.shape[1]
    rows = images * slots
    group = n_dp * n_ctx // 2
    total = slots * n_ctx
    heads = wide // HD
    turn = piece % LANES == 0
    sizes = (n_dp, n_ctx, n_t, images, slots, width, wide, hidden, piece, cut)
    vmem = pl.BlockSpec(memory_space=pltpu.VMEM)
    hbm = pl.BlockSpec(memory_space=pl.ANY)
    scratch = [
        pltpu.VMEM((rows, width), BF16),
        pltpu.VMEM((rows, width), BF16),
        pltpu.VMEM((wide, piece), BF16),
        pltpu.VMEM((hidden, piece), BF16),
        pltpu.VMEM((2 * ROWS, LANES), F32),
        pltpu.VMEM((3, group, 2, piece, wide), BF16),
        pltpu.VMEM((group, 2, piece, n_t * wide), BF16),
        pltpu.VMEM((group, 2, piece, hidden), BF16),
        pltpu.VMEM((group, 2, piece, hidden), BF16),
        pltpu.VMEM((group, 2, 2 * ROWS, LANES), F32),
        pltpu.VMEM((ROWS, width), F32),
        pltpu.VMEM((rows, width), F32),
        pltpu.VMEM((rows, width), BF16),
        pltpu.VMEM((images, total, 3 * wide), BF16),
        pltpu.VMEM((images, heads * slots, total), F32),
        pltpu.VMEM((images, heads * slots, total), F32),
        pltpu.VMEM((n_ctx, images * heads, total), F32),
        pltpu.VMEM((n_ctx, images * heads, total), F32),
        pltpu.VMEM((rows, n_t * wide), BF16),
        pltpu.VMEM((rows, width), F32),
        pltpu.VMEM((rows, width), BF16),
        pltpu.VMEM((rows, hidden), F32),
        pltpu.VMEM((rows, hidden), BF16),
        pltpu.VMEM((rows, hidden), BF16),
        pltpu.VMEM((rows, width), BF16),
        pltpu.VMEM((rows, width), BF16),
        pltpu.VMEM((rows, width), BF16),
        pltpu.VMEM((n_t - 1, slots, width), BF16),
        pltpu.VMEM((n_t - 1, slots, width), BF16),
        pltpu.VMEM((n_t - 1, slots, width), BF16),
        pltpu.VMEM((slots, width), F32),
        pltpu.VMEM((rows, width), BF16),
        pltpu.VMEM((slots, width), BF16),
        pltpu.VMEM((slots, n_t * wide), BF16),
        pltpu.VMEM((images, total, wide), BF16),
        pltpu.VMEM((rows, 3 * wide), BF16),
        pltpu.VMEM((slots, width), BF16),
        pltpu.VMEM((slots, width), BF16),
        pltpu.VMEM((ROWS, width), F32),
        pltpu.VMEM((ROWS, width), F32),
        pltpu.VMEM((group - 1, ROWS, width), F32),
        pltpu.VMEM((n_t - 1, 8, LANES), F32),
        pltpu.VMEM((3, group, 2, piece, wide), BF16),
        pltpu.VMEM((group, 2, piece, n_t * wide), BF16),
        pltpu.VMEM((group, 2, piece, hidden), BF16),
        pltpu.VMEM((group, 2, piece, hidden), BF16),
        pltpu.VMEM((3, group, piece, wide), BF16),
        pltpu.VMEM((group, piece, n_t * wide), BF16),
        pltpu.VMEM((group, piece, hidden), BF16),
        pltpu.VMEM((group, piece, hidden), BF16),
        pltpu.VMEM((group, 3, piece, wide), BF16),
        pltpu.VMEM((group, piece, n_t * wide), BF16),
        pltpu.VMEM((group, piece, hidden), BF16),
        pltpu.VMEM((group, piece, hidden), BF16),
        pltpu.VMEM((group - 1, 3, piece, wide), BF16),
        pltpu.VMEM((group - 1, piece, n_t * wide), BF16),
        pltpu.VMEM((group - 1, piece, hidden), BF16),
        pltpu.VMEM((group - 1, piece, hidden), BF16),
        pltpu.VMEM((piece, n_t * wide), BF16),
        pltpu.VMEM((n_t - 1, piece, wide), BF16),
    ]
    shapes = (
        (3, piece, wide),
        (wide, piece) if turn else (piece, wide),
        (piece, hidden),
        (hidden, piece) if turn else (piece, hidden),
    )
    scratch += [pltpu.VMEM(shape, F32) for shape in shapes]
    copies = 120 + 20 * group
    scratch += [
        pltpu.SemaphoreType.DMA((copies,)),
        pltpu.SemaphoreType.DMA((copies,)),
        pltpu.SemaphoreType.DMA((24,)),
    ]
    results = [jax.ShapeDtypeStruct((rows, width), BF16)] * 2
    results += [jax.ShapeDtypeStruct(shape, F32) for shape in shapes]
    outs = pl.pallas_call(
        functools.partial(block_kernel, sizes),
        out_shape=(*results, jax.ShapeDtypeStruct((ROWS, width), F32)),
        in_specs=[hbm, hbm, vmem, hbm, hbm, hbm, hbm] + [vmem] * 8,
        out_specs=(hbm,) * 7,
        scratch_shapes=scratch,
        compiler_params=pltpu.CompilerParams(
            collective_id=0, has_side_effects=True, vmem_limit_bytes=63 << 20
        ),
    )(
        tokens.reshape(rows, width),
        cotangent.reshape(rows, width),
        keep_mask,
        jnp.transpose(attend_in, (1, 0, 2)),
        attend_out,
        expand_in,
        contract_out,
        *[
            v.reshape(1, piece)
            for v in (first_gain, first_shift, out_bias, second_gain, second_shift, contract_bias)
        ],
        expand_bias.T,
        attend_bias,
    )
    vector = jax.ShapeDtypeStruct((1, piece), F32)
    placed = pl.pallas_call(
        functools.partial(finish_call, (n_ctx, piece, cut, wide, hidden, width)),
        out_shape=(
            *results,
            *[vector] * 6,
            jax.ShapeDtypeStruct((cut, hidden // HD), F32),
            jax.ShapeDtypeStruct((2, heads, cut), F32),
        ),
        in_specs=[hbm] * 6 + [vmem],
        out_specs=(vmem,) * 14,
        scratch_shapes=[pltpu.SemaphoreType.DMA((6,))],
        compiler_params=pltpu.CompilerParams(vmem_limit_bytes=32 << 20),
    )(*outs)
    block_out, tokens_grad, d_win, d_wot, d_wup, d_wdt = placed[:6]
    vectors = [v.reshape(piece) for v in placed[6:12]]
    return (
        block_out.reshape(tokens.shape),
        tokens_grad.reshape(tokens.shape),
        vectors[0],
        vectors[1],
        jnp.transpose(d_win, (1, 0, 2)),
        placed[13],
        d_wot if turn else d_wot.T,
        vectors[2],
        vectors[3],
        vectors[4],
        d_wup,
        placed[12].T,
        d_wdt if turn else d_wdt.T,
        vectors[5],
    )


def solution(mesh):
    shape = (mesh.shape["dp"], mesh.shape["ctx"], mesh.shape["tensor"])
    vector = P(("dp", "ctx"))
    params = (
        vector,
        vector,
        P(("dp", "ctx"), None, "tensor"),
        P(None, "tensor", ("dp", "ctx")),
        P("tensor", ("dp", "ctx")),
        vector,
        vector,
        vector,
        P(("dp", "ctx"), "tensor"),
        P("tensor", ("dp", "ctx")),
        P("tensor", ("dp", "ctx")),
        vector,
    )
    rows = P("dp", "ctx", None)
    return jax.shard_map(
        functools.partial(on_device, shape),
        mesh=mesh,
        in_specs=(rows, P("dp", None), rows, *params),
        out_specs=(rows, rows, *params),
        check_vma=False,
    )
```

time: 185 us -> 159 us (0.86)
  Pallas kernels: 165 us -> 150 us
  local copies, waits for them, and re-layouts: 18.2 us -> 6.99 us
    pallas_call x1 -> x2, Pallas kernels: 165 us -> 150 us  [the longest x1 147 us: on_device(): pl.pallas_call(functools.partial(block_kernel, sizes), out_shape=(*result...]
    unnamed x41 -> x14, local copies, waits for them, and re-layouts: 11.8 us -> 6.99 us
    reshape x2 -> x0, local copies, waits for them, and re-layouts: 2.33 us -> none  [the longest x1 1.5 us: own(): lax.dynamic_slice(d_vec, (row, shard * piece), (1, piece)).reshape(piece)]
where the time goes in v2:
time: 159 us; the launch traced here: 158 us
  Pallas kernels  150 us (94%)
  local copies, waits for them, and re-layouts  6.99 us (4%)
    pallas_call x1, Pallas kernels, on_device(): pl.pallas_call(functools.partial(block_kernel, sizes), out_shape=(*result...  147 us
    unnamed x14, local copies, waits for them, and re-layouts  6.99 us
    pallas_call x1, Pallas kernels, on_device(): pl.pallas_call(functools.partial(finish_call, (n_ctx, piece, cut, wide, h...  3.33 us

profile of v2, /device:TPU:0, one launch (start us, length us, event | category | flops | bytes accessed | tf_op | source)
XLA Modules:
  0.0 158.1 jit_solution(9299078659187612566)
XLA Ops:
  0.7 147.1 %shard_map.254 = (bf16[320,1024]{1,0:T(8,128)(2,1)}, bf16[320,1024]{1,0:T(8,128)(2,1)}, f32[3,128,256]{2,1,0:T(8,128)}, f32[256,128]{1,0:T(8,128)}, f32[128,1024...) custom-call(bf16[320,1024]{1,0:T(8,128)(2,1)} %bitcast.20, bf16[320,1024]{1,0:T(8,128)(2,1)} %bitcast.21, ...), custom_call_target="tpu_custom_call" | custom-call | tf_op jit(solution)/shard_map/pallas_call | solution.py:971
  147.7 0.0 copy-start
  147.7 1.1 copy-done
  148.8 0.0 copy-start.1
  148.8 1.1 copy-done.1
  149.9 0.0 copy-start.2
  149.9 1.0 copy-done.2
  151.0 0.0 copy-start.3
  151.0 1.0 copy-done.3
  152.0 0.0 copy-start.4
  152.0 1.0 copy-done.4
  153.0 0.0 copy-start.5
  153.0 0.9 copy-done.5
  153.9 0.0 copy-start.6
  153.9 0.8 copy-done.6
  154.7 3.3 %shard_map.255 = (bf16[320,1024]{1,0:T(8,128)(2,1)}, bf16[320,1024]{1,0:T(8,128)(2,1)}, f32[3,128,256]{2,1,0:T(8,128)}, f32[256,128]{1,0:T(8,128)}, f32[128,1024...) custom-call(bf16[320,1024]{1,0:T(8,128)(2,1)S(1)} %copy-done, ...), custom_call_target="tpu_custom_call" | custom-call | tf_op jit(solution)/shard_map/pallas_call | solution.py:996
Async XLA Ops:
  147.7 1.1 copy-start
  148.8 1.1 copy-start.1
  149.9 1.0 copy-start.2
  151.0 1.0 copy-start.3
  152.0 1.0 copy-start.4
  153.0 0.9 copy-start.5
  153.9 0.8 copy-start.6

commit v3 on v2

--- a/solution.py
+++ b/solution.py
@@ -108,8 +108,11 @@
     parts,
     part1,
     recv2,
+    relay2,
     recvs,
+    relays,
     recv1,
+    relay1,
     gfirst,
     gdown,
     gown,
@@ -182,6 +185,25 @@
     own = slot_at(ctx)
     mine = slot_at(z)
 
+    cut_at = ROWS * ((slots // ROWS + 1) // 2)
+    starts = (0, cut_at)
+    sizes_of = (cut_at, slots - cut_at)
+    bases = (0, images * cut_at)
+
+    def chunk(c):
+        return slice(bases[c], bases[c] + images * sizes_of[c])
+
+    def rows_at(c, image):
+        first_row = bases[c] + image * sizes_of[c]
+        return pl.ds(pl.multiple_of(first_row, ROWS), sizes_of[c])
+
+    def slot_part(c):
+        return slice(starts[c], starts[c] + sizes_of[c])
+
+    def split_rows(ref, image, lanes, value):
+        for c in range(2):
+            ref[rows_at(c, image), lanes] = value[slot_part(c)]
+
     count = [0, 0]
     pending = []
 
@@ -200,6 +222,31 @@
         pending.append(copy)
         return copy
 
+    inside = lax.rem(z - lax.div(z, 2), 2) == 1
+    at_end = lax.rem(z - lax.div(z, 2), 2) == 0
+    guarded = []
+
+    def fresh():
+        count[0] += 1
+        return count[0] - 1
+
+    def remote(src, dst, device, out_index, in_index):
+        return pltpu.make_async_remote_copy(
+            src_ref=src,
+            dst_ref=dst,
+            send_sem=send_sem.at[out_index],
+            recv_sem=recv_sem.at[in_index],
+            device_id=device,
+            device_id_type=MESH,
+        )
+
+    def send_if(flag, make):
+        guarded.append((flag, make))
+
+        @pl.when(flag)
+        def _():
+            make().start()
+
     def complete(copy):
         pending[:] = [other for other in pending if other is not copy]
         copy.wait()
@@ -233,10 +280,20 @@
     for device in [plane(k) for k in planes] + [sib] + [zpeer(k) for k in zs]:
         pl.semaphore_signal(barrier, inc=1, device_id=device, device_id_type=MESH)
     a_out_load = local(attend_out, a_out)
-    tok_load = local(tok_in, tok)
+    def load_rows(source, ref):
+        return [
+            local(
+                source.at[image * slots + starts[c] : image * slots + starts[c] + sizes_of[c], :],
+                ref.at[rows_at(c, image), :],
+            )
+            for c in range(2)
+            for image in range(images)
+        ]
+
+    tok_load = load_rows(tok_in, tok)
     win_own = local(win, at_win(me, core))
     c_out_load = local(contract_out, c_out)
-    cot_load = local(cot_in, cot)
+    cot_load = load_rows(cot_in, cot)
     wup_own = local(wup, at_wup(me, core))
 
     vec[...] = jnp.zeros_like(vec)
@@ -299,7 +356,8 @@
     wot_started = gather_start(at_wot(me, core), at_wot)
     wot_z = [[send(wot_piece(me, z), wot_piece(me, z), zpeer(k)) for k in zs]]
 
-    tok_load.wait()
+    for copy in tok_load:
+        copy.wait()
 
     def first_norm(step, carry):
         at = pl.ds(pl.multiple_of(step * BLOCK, BLOCK), BLOCK)
@@ -385,7 +443,11 @@
         out = nn(h1[...], g_win[j].reshape(width, wide))
         if bias is not None:
             out = out + vx[bias : bias + 1, 0:wide]
-        qkv[:, own, j * wide : (j + 1) * wide] = out.astype(BF16).reshape(images, slots, wide)
+        out = out.astype(BF16)
+        for c in range(2):
+            place_at = pl.ds(pl.multiple_of(ctx * slots + starts[c], ROWS), sizes_of[c])
+            block = out[chunk(c)].reshape(images, sizes_of[c], wide)
+            qkv[:, place_at, j * wide : (j + 1) * wide] = block
 
     def at_kv(index):
         return qkv.at[:, slot_at(index), wide : 3 * wide]
@@ -409,10 +471,9 @@
     kv_passed = ctx_forward(kv_started, at_kv)
     ctx_finish(kv_started, kv_passed)
 
-    def at_mixed(index, image):
-        return mixed.at[image * slots : (image + 1) * slots, lane_at(index, wide)]
-
-    mixed_sent = []
+    def at_mixed(index, c):
+        return mixed.at[chunk(c), lane_at(index, wide)]
+
     for image in range(images):
         key_live = key_id < lengths[image : image + 1, :]
         stacked = stack_heads(qkv[image, own, 0:wide])
@@ -425,22 +486,25 @@
         wq[image] = probs
         put_rows(stat, image, top + jnp.log(whole))
         out = nn(probs.astype(BF16), qkv[image, :, 2 * wide : 3 * wide])
-        mixed[image * slots : (image + 1) * slots, lane_at(z, wide)] = pick_heads(out).astype(BF16)
-        mixed_sent.append(
-            [send(at_mixed(z, image), at_mixed(z, image), zpeer(k)) for k in reversed(zs)]
-        )
+        split_rows(mixed, image, lane_at(z, wide), pick_heads(out).astype(BF16))
+    mixed_sent = [
+        [send(at_mixed(z, c), at_mixed(z, c), zpeer(k)) for k in reversed(zs)] for c in range(2)
+    ]
 
     def at_stat(index):
         return stat.at[index]
 
     stat_started = ctx_start(at_stat)
 
-    cot_load.wait()
+    for copy in cot_load:
+        copy.wait()
     row_live = []
     for image in range(images):
         row_live.append(slot_id < lengths[image : image + 1, :])
-        at = slice(image * slots, (image + 1) * slots)
-        gdown[at, :] = jnp.where(row_live[image], cot[at, :].astype(F32), 0.0).astype(BF16)
+        for c in range(2):
+            at = rows_at(c, image)
+            live = row_live[image][slot_part(c)]
+            gdown[at, :] = jnp.where(live, cot[at, :].astype(F32), 0.0).astype(BF16)
 
     gather_finish(wot_started, wot_passed)
     wot_more = []
@@ -451,7 +515,148 @@
             wot_more.append(send(there, there, sib))
     wup_passed = gather_forward(wup_started, at_wup)
     wup_own.wait()
+    for copy in wot_more:
+        copy.wait_recv()
+
+    some = group // (width // TILE)
+
+    def scatter(part, recv, relay, c):
+        marks = [fresh() for _ in range(4)]
+
+        def onward(j):
+            return remote(
+                part.at[rows_at(c, flip(z, 3 - j)), :],
+                relay.at[j, slot_part(c), :],
+                zpeer(1),
+                marks[j],
+                marks[j],
+            )
+
+        def passed(j):
+            return remote(
+                relay.at[j, slot_part(c), :],
+                recv.at[1, slot_part(c), :],
+                zpeer(2 + j),
+                marks[2 + j],
+                marks[2],
+            )
+
+        for j in range(2):
+            send_if(at_end, functools.partial(onward, j))
+        near = send(
+            part.at[rows_at(c, flip(z, 1)), :], recv.at[0, slot_part(c), :], zpeer(1)
+        )
+
+        def pass_on():
+            for j in range(2):
+
+                @pl.when(inside)
+                def _():
+                    onward(j).wait_recv()
+                    value = part[rows_at(c, flip(z, 2 + j)), :].astype(F32)
+                    value = value + relay[j, slot_part(c), :].astype(F32)
+                    relay[j, slot_part(c), :] = value.astype(BF16)
+
+                send_if(inside, functools.partial(passed, j))
+
+        def finish():
+            near.wait_recv()
+            passed(0).wait_recv()
+
+        return pass_on, finish
+
+    def spread(source, at):
+        marks = [fresh() for _ in range(4)]
+        near = send(source, at(z), zpeer(1))
+
+        def far(k):
+            return remote(source, at(z), zpeer(k), marks[k - 2], marks[k - 2])
+
+        def passed(k):
+            block = at(flip(z, k))
+            return remote(block, block, zpeer(1), marks[k], marks[3 - k])
+
+        send_if(at_end, functools.partial(far, 2))
+        send_if(inside, functools.partial(far, 3))
+
+        def pass_on():
+            for k in (3, 2):
+
+                @pl.when(inside)
+                def _():
+                    far(k).wait_recv()
+
+                send_if(inside, functools.partial(passed, k))
+
+        def finish():
+            near.wait_recv()
+
+            @pl.when(at_end)
+            def _():
+                far(2).wait_recv()
+                far(3).wait_recv()
+
+        return pass_on, finish
+
+    def arrived(part, recv, c, at, size):
+        here = pl.ds(pl.multiple_of(bases[c] + z * sizes_of[c] + at, ROWS), size)
+        there = pl.ds(pl.multiple_of(starts[c] + at, ROWS), size)
+        out = part[here, :].astype(F32)
+        for j in range(2):
+            out = out + recv[j, there, :].astype(F32)
+        return out
+
+    def attended(c):
+        at_rows = chunk(c)
+        for copy in mixed_sent[c]:
+            copy.wait_recv()
+
+        def project_out(step, carry):
+            weight = g_wot[pl.ds(step * some, some)].reshape(TILE, n_t * wide)
+            first[at_rows, lane_at(step, TILE)] = nt(mixed[at_rows, :], weight)
+            return carry
+
+        lax.fori_loop(0, width // TILE, project_out, 0)
+
+        def second_norm(step, carry):
+            at = pl.ds(pl.multiple_of(bases[c] + step * BLOCK, BLOCK), BLOCK)
+            value = tok[at, :].astype(F32) + first[at, :] + vx[2:3, :]
+            first[at, :] = value
+            normed, _ = norm_parts(value)
+            h2[at, :] = (normed * vx[3:4, :] + vx[4:5, :]).astype(BF16)
+            return carry
+
+        lax.fori_loop(0, images * sizes_of[c] // BLOCK, second_norm, 0)
+
+    def feed_forward(c):
+        at_rows = chunk(c)
+
+        def expand(step, carry):
+            at = lane_at(step, TILE)
+            weight = g_wup[:, :, :, at].reshape(width, TILE)
+            inner = nn(h2[at_rows, :], weight) + vx[8:9, at]
+            share = 0.5 * (1.0 + lax.erf(inner * root_half))
+            act[at_rows, at] = (inner * share).astype(BF16)
+            slope = share + inner * jnp.exp(-0.5 * inner * inner) * inv_root_two_pi
+            grad = (ga[at_rows, at] * slope).astype(BF16)
+            gi[at_rows, at] = grad
+            gv[8:9, at] += jnp.sum(grad.astype(F32), axis=0, keepdims=True)
+            return carry
+
+        lax.fori_loop(0, hidden // TILE, expand, 0)
+
+        def up_back(step, carry):
+            weight = g_wup[pl.ds(step * some, some)].reshape(TILE, hidden)
+            part2[at_rows, lane_at(step, TILE)] = nt(gi[at_rows, :], weight).astype(BF16)
+            return carry
+
+        lax.fori_loop(0, width // TILE, up_back, 0)
+        return scatter(part2, recv2, relay2, c)
+
+    for c in range(2):
+        attended(c)
     wdt_passed = gather_forward(wdt_started, at_wdt)
+    gather_finish(wup_started, wup_passed)
     gather_finish(wdt_started, wdt_passed)
 
     def down_back(step, carry):
@@ -460,70 +665,7 @@
         return carry
 
     lax.fori_loop(0, hidden // TILE, down_back, 0)
-
-    gather_finish(wup_started, wup_passed)
-    for copy in wot_more:
-        copy.wait_recv()
-    for copies in mixed_sent:
-        for copy in copies:
-            copy.wait_recv()
-
-    some = group // (width // TILE)
-
-    def project_out(step, carry):
-        weight = g_wot[pl.ds(step * some, some)].reshape(TILE, n_t * wide)
-        first[:, lane_at(step, TILE)] = nt(mixed[...], weight)
-        return carry
-
-    lax.fori_loop(0, width // TILE, project_out, 0)
-
-    def second_norm(step, carry):
-        at = pl.ds(pl.multiple_of(step * BLOCK, BLOCK), BLOCK)
-        value = tok[at, :].astype(F32) + first[at, :] + vx[2:3, :]
-        first[at, :] = value
-        normed, _ = norm_parts(value)
-        h2[at, :] = (normed * vx[3:4, :] + vx[4:5, :]).astype(BF16)
-        return carry
-
-    lax.fori_loop(0, rows // BLOCK, second_norm, 0)
-
-    def expand(step, carry):
-        at = lane_at(step, TILE)
-        inner = nn(h2[...], g_wup[:, :, :, at].reshape(width, TILE)) + vx[8:9, at]
-        share = 0.5 * (1.0 + lax.erf(inner * root_half))
-        act[:, at] = (inner * share).astype(BF16)
-        slope = share + inner * jnp.exp(-0.5 * inner * inner) * inv_root_two_pi
-        grad = (ga[:, at] * slope).astype(BF16)
-        gi[:, at] = grad
-        gv[8:9, at] = jnp.sum(grad.astype(F32), axis=0, keepdims=True)
-        return carry
-
-    lax.fori_loop(0, hidden // TILE, expand, 0)
-
-    def up_back(step, carry):
-        weight = g_wup[pl.ds(step * some, some)].reshape(TILE, hidden)
-        part2[:, lane_at(step, TILE)] = nt(gi[...], weight).astype(BF16)
-        return carry
-
-    lax.fori_loop(0, width // TILE, up_back, 0)
-
-    def scatter(part, recv, start, size):
-        return [
-            send(
-                part.at[pl.ds(pl.multiple_of(flip(z, k) * slots + start, ROWS), size), :],
-                recv.at[k - 1, start : start + size, :],
-                zpeer(k),
-            )
-            for k in reversed(zs)
-        ]
-
-    def arrived(part, recv, at, size):
-        out = part[pl.ds(pl.multiple_of(z * slots + at, ROWS), size), :].astype(F32)
-        for k in zs:
-            out = out + recv[k - 1, pl.ds(pl.multiple_of(at, ROWS), size), :].astype(F32)
-        return out
-
-    sent2 = scatter(part2, recv2, 0, slots)
+    sent2 = [feed_forward(c) for c in range(2)]
 
     def contract(step, carry):
         weight = g_wdt[pl.ds(step * some, some)].reshape(TILE, hidden)
@@ -531,8 +673,6 @@
         return carry
 
     lax.fori_loop(0, width // TILE, contract, 0)
-    early = 2 * ROWS
-    sents = [scatter(parts, recvs, 0, early)]
 
     def wide_grad(buf, left, right, lanes):
         def one(step, carry):
@@ -566,8 +706,10 @@
 
     wide_grad(b_wdt, gdown, act, hidden)
     wdt_near = grad_near(b_wdt, s_wdt)
+    sent2[0][0]()
     wide_grad(b_wup, h2, gi, hidden)
     wup_near = grad_near(b_wup, s_wup)
+    sent2[1][0]()
     wdt_far = grad_far(wdt_near, b_wdt, s_wdt, t_wdt, r_wdt)
 
     q_passed = ctx_forward(q_started, at_q)
@@ -604,70 +746,89 @@
         )
         return inner * inv
 
-    for copy in sent2:
-        copy.wait_recv()
-
-    def second_back(step, carry):
-        at = step * ROWS
-        here = pl.ds(pl.multiple_of(z * slots + at, ROWS), ROWS)
-        grad = arrived(part2, recv2, at, ROWS)
-        normed, inv = norm_parts(first[here, :])
-        rows_grad = gdown[here, :].astype(F32)
-        value = rows_grad + norm_back(grad, normed, inv, vx[3:4, :])
-        there = pl.ds(pl.multiple_of(at, ROWS), ROWS)
-        gfirst[there, :] = value
-        gown[there, :] = value.astype(BF16)
-        add_line(3, grad * normed)
-        add_line(4, grad)
-        add_line(5, rows_grad)
-        add_line(2, value)
-        return carry
-
-    lax.fori_loop(0, slots // ROWS, second_back, 0)
-
-    def mixed_back(step, carry):
-        at = lane_at(step, wide)
-        weight = g_wot[:, :, :, at].reshape(width, wide)
-        gm[:, at] = nn(gown[...], weight).astype(BF16)
-        return carry
-
-    lax.fori_loop(0, n_t, mixed_back, 0)
-    to_heads = [
-        send(gm.at[:, lane_at(flip(z, k), wide)], do.at[z, own, :], zpeer(k)) for k in reversed(zs)
-    ]
-    sents.append(scatter(parts, recvs, early, slots - early))
-    do[z, own, :] = gm[:, lane_at(z, wide)]
+    def second_back(c):
+        sent2[c][1]()
+
+        def one(step, carry):
+            at = step * ROWS
+            here = pl.ds(pl.multiple_of(bases[c] + z * sizes_of[c] + at, ROWS), ROWS)
+            grad = arrived(part2, recv2, c, at, ROWS)
+            normed, inv = norm_parts(first[here, :])
+            rows_grad = gdown[here, :].astype(F32)
+            value = rows_grad + norm_back(grad, normed, inv, vx[3:4, :])
+            there = pl.ds(pl.multiple_of(starts[c] + at, ROWS), ROWS)
+            gfirst[there, :] = value
+            gown[there, :] = value.astype(BF16)
+            add_line(3, grad * normed)
+            add_line(4, grad)
+            add_line(5, rows_grad)
+            add_line(2, value)
+            return carry
+
+        lax.fori_loop(0, sizes_of[c] // ROWS, one, 0)
+
+        def mixed_back(step, carry):
+            at = lane_at(step, wide)
+            weight = g_wot[:, :, :, at].reshape(width, wide)
+            gm[slot_part(c), at] = nn(gown[slot_part(c), :], weight).astype(BF16)
+            return carry
+
+        lax.fori_loop(0, n_t, mixed_back, 0)
+        place_at = pl.ds(pl.multiple_of(ctx * slots + starts[c], ROWS), sizes_of[c])
+        sent = [
+            send(
+                gm.at[slot_part(c), lane_at(flip(z, k), wide)],
+                do.at[z, place_at, :],
+                zpeer(k),
+            )
+            for k in reversed(zs)
+        ]
+        do[z, place_at, :] = gm[slot_part(c), lane_at(z, wide)]
+        return sent
+
+    to_heads = [second_back(c) for c in range(2)]
+    sents = [scatter(parts, recvs, relays, c) for c in range(2)]
+
     def out_grad(step, carry):
         at = lane_at(step, TILE)
-        out = tn(gown[...], mixed[mine, at]).astype(BF16)
+        part = jnp.concatenate([mixed[rows_at(c, z), at] for c in range(2)], axis=0)
+        out = tn(gown[...], part).astype(BF16)
         b_wot[:, :, :, at] = out.reshape(group, 2, piece, TILE)
         return carry
 
     lax.fori_loop(0, n_t * wide // TILE, out_grad, 0)
     wot_near = grad_near(b_wot, s_wot)
 
-    def block_rows(start, size, copies):
-        for copy in copies:
+    stays = []
+
+    def block_rows(c):
+        sents[c][1]()
+        value = first[rows_at(c, z), :] + arrived(parts, recvs, c, 0, sizes_of[c]) + vx[5:6, :]
+        value = jnp.where(own_live[slot_part(c)], value, 0.0)
+        block_own[slot_part(c), :] = value.astype(BF16)
+        return to_all(block_own, out_block, c)
+
+    def to_all(source, target, c):
+        def at(index):
+            here = pl.ds(pl.multiple_of(index * slots + starts[c], ROWS), sizes_of[c])
+            return target.at[here, :]
+
+        part = source.at[slot_part(c), :]
+        stays.append(local(part, at(z)))
+        return spread(part, at)
+
+    def at_do(c):
+        def at(index):
+            first_row = index * slots + starts[c]
+            return do.at[:, pl.ds(pl.multiple_of(first_row, ROWS), sizes_of[c]), :]
+
+        return at
+
+    do_started = []
+    for c in range(2):
+        for copy in to_heads[c]:
             copy.wait_recv()
-        here = pl.ds(pl.multiple_of(z * slots + start, ROWS), size)
-        value = first[here, :] + arrived(parts, recvs, start, size) + vx[5:6, :]
-        value = jnp.where(own_live[start : start + size], value, 0.0)
-        block_own[start : start + size, :] = value.astype(BF16)
-        source = block_own.at[start : start + size, :]
-        keep_own = local(source, out_block.at[here, :])
-        return [send(source, out_block.at[here, :], zpeer(k)) for k in reversed(zs)], keep_own
-
-    block_early, block_kept = block_rows(0, early, sents[0])
-    tail = block_early
-    stays = [block_kept]
-
-    for copy in to_heads:
-        copy.wait_recv()
-
-    def at_do(index):
-        return do.at[:, slot_at(index), :]
-
-    do_started = ctx_start(at_do)
+        do_started.append(ctx_start(at_do(c)))
 
     for image in range(images):
         stacked = stack_heads(do[image, own, :])
@@ -677,7 +838,7 @@
         put_rows(alng, image, along)
         grad_scores = (weights * (grad_probs - along)).astype(BF16)
         out = pick_heads(nn(grad_scores, qkv[image, :, wide : 2 * wide])) * scale
-        dqkv[image * slots : (image + 1) * slots, 0:wide] = out.astype(BF16)
+        split_rows(dqkv, image, slice(0, wide), out.astype(BF16))
 
     def at_along(index):
         return alng.at[index]
@@ -685,9 +846,11 @@
     along_started = ctx_start(at_along)
     wot_far = grad_far(wot_near, b_wot, s_wot, t_wot, r_wot)
     wup_far = grad_far(wup_near, b_wup, s_wup, t_wup, r_wup)
-    do_passed = ctx_forward(do_started, at_do)
+    sents[0][0]()
+    do_passed = [ctx_forward(do_started[c], at_do(c)) for c in range(2)]
     along_passed = ctx_forward(along_started, at_along)
-    ctx_finish(do_started, do_passed)
+    for c in range(2):
+        ctx_finish(do_started[c], do_passed[c])
     ctx_finish(along_started, along_passed)
 
     for image in range(images):
@@ -702,31 +865,35 @@
                 level = level + alng[other, line : line + 1, :]
             lines.append(grad_probs[h * slots : (h + 1) * slots] - level)
         grad_scores = (weights * jnp.concatenate(lines, axis=0)).astype(BF16)
-        at = slice(image * slots, (image + 1) * slots)
         out = pick_heads(nn(grad_scores, qkv[image, :, 0:wide])) * scale
-        dqkv[at, wide : 2 * wide] = out.astype(BF16)
+        split_rows(dqkv, image, slice(wide, 2 * wide), out.astype(BF16))
         out = pick_heads(nn(weights.astype(BF16), do[image]))
-        dqkv[at, 2 * wide : 3 * wide] = out.astype(BF16)
-
-    def in_back(step, carry):
-        out = None
-        for j in range(3):
-            weight = g_win[j, pl.ds(step * some, some)].reshape(TILE, wide)
-            term = nt(dqkv[:, j * wide : (j + 1) * wide], weight)
-            out = term if out is None else out + term
-        part1[:, lane_at(step, TILE)] = out.astype(BF16)
-        return carry
-
-    lax.fori_loop(0, width // TILE, in_back, 0)
-    sent1 = scatter(part1, recv1, 0, slots)
-
-    block_late, block_kept = block_rows(early, slots - early, sents[1])
-    tail += block_late
-    stays.append(block_kept)
+        split_rows(dqkv, image, slice(2 * wide, 3 * wide), out.astype(BF16))
+
+    def in_back(c):
+        at_rows = chunk(c)
+
+        def one(step, carry):
+            out = None
+            for j in range(3):
+                weight = g_win[j, pl.ds(step * some, some)].reshape(TILE, wide)
+                term = nt(dqkv[at_rows, j * wide : (j + 1) * wide], weight)
+                out = term if out is None else out + term
+            part1[at_rows, lane_at(step, TILE)] = out.astype(BF16)
+            return carry
+
+        lax.fori_loop(0, width // TILE, one, 0)
+        return scatter(part1, recv1, relay1, c)
+
+    sent1 = [in_back(c) for c in range(2)]
+    sents[1][0]()
+
     for j in range(3):
         out = tn(h1[...], dqkv[:, j * wide : (j + 1) * wide]).astype(BF16)
         b_win[j] = out.reshape(group, 2, piece, wide)
     win_near = send(b_win.at[:, :, 1 - core], s_win, sib)
+    sent1[0][0]()
+    tail = [block_rows(0)]
     gv[9:10, 0:wide] = jnp.sum(dqkv[:, 0:wide].astype(F32), axis=0, keepdims=True)
     gv[10:11, 0:wide] = jnp.sum(dqkv[:, 2 * wide : 3 * wide].astype(F32), axis=0, keepdims=True)
     f_wdt[...] = turned(grad_sum(wdt_far, t_wdt, r_wdt), f_wdt)
@@ -737,6 +904,8 @@
         t_win[:, j] = (both + s_win[j].astype(F32)).astype(BF16)
     win_far = [send(t_win.at[flip(me, k)], r_win.at[k - 1], plane(k)) for k in reversed(planes)]
 
+    sent1[1][0]()
+    tail.append(block_rows(1))
     whole_rows = grad_sum(wot_far, t_wot, r_wot)
     o_wot[...] = whole_rows.astype(BF16)
     to_owner = [
@@ -746,29 +915,35 @@
     f_wup[...] = grad_sum(wup_far, t_wup, r_wup)
     stays.append(local(f_wup, out_wup))
 
-    for copy in sent1:
-        copy.wait_recv()
-
-    def first_back(step, carry):
-        at = step * ROWS
-        here = pl.ds(pl.multiple_of(z * slots + at, ROWS), ROWS)
-        grad = arrived(part1, recv1, at, ROWS)
-        normed, inv = norm_parts(tok[here, :].astype(F32))
-        there = pl.ds(pl.multiple_of(at, ROWS), ROWS)
-        value = gfirst[there, :] + norm_back(grad, normed, inv, vx[0:1, :])
-        tokens_own[there, :] = value.astype(BF16)
-        add_line(0, grad * normed)
-        add_line(1, grad)
-        return carry
-
-    lax.fori_loop(0, slots // ROWS, first_back, 0)
-    tail += [send(tokens_own, out_tokens.at[mine, :], zpeer(k)) for k in reversed(zs)]
-    stays.append(local(tokens_own, out_tokens.at[mine, :]))
+    def first_back(c):
+        sent1[c][1]()
+
+        def one(step, carry):
+            at = step * ROWS
+            here = pl.ds(pl.multiple_of(bases[c] + z * sizes_of[c] + at, ROWS), ROWS)
+            grad = arrived(part1, recv1, c, at, ROWS)
+            normed, inv = norm_parts(tok[here, :].astype(F32))
+            there = pl.ds(pl.multiple_of(starts[c] + at, ROWS), ROWS)
+            value = gfirst[there, :] + norm_back(grad, normed, inv, vx[0:1, :])
+            tokens_own[there, :] = value.astype(BF16)
+            add_line(0, grad * normed)
+            add_line(1, grad)
+            return carry
+
+        lax.fori_loop(0, sizes_of[c] // ROWS, one, 0)
+        return to_all(tokens_own, out_tokens, c)
+
+    for c in range(2):
+        tail[c][0]()
+    for c in range(2):
+        tail.append(first_back(c))
 
     near = send(gv, vr_sib, sib)
+    tail[2][0]()
     complete(near)
     gv[...] = gv[...] + vr_sib[...]
     far = [send(gv, vr_plane.at[k - 1], plane(k)) for k in planes]
+    tail[3][0]()
     f_win[...] = grad_sum(win_far, t_win, r_win)
     stays.append(local(f_win, out_win))
     for copy in far:
@@ -793,10 +968,16 @@
         value = value + vr_z[k - 1]
     gv[0:8, lanes] = value
     stays.append(local(gv, out_vec))
-    for copy in tail:
-        copy.wait_recv()
+    for _, finish in tail:
+        finish()
     for copy in pending:
         copy.wait_send()
+    for flag, make in guarded:
+
+        @pl.when(flag)
+        def _():
+            make().wait_send()
+
     for copy in stays:
         copy.wait()
 
@@ -919,9 +1100,12 @@
         pltpu.VMEM((rows, width), BF16),
         pltpu.VMEM((rows, width), BF16),
         pltpu.VMEM((rows, width), BF16),
-        pltpu.VMEM((n_t - 1, slots, width), BF16),
-        pltpu.VMEM((n_t - 1, slots, width), BF16),
-        pltpu.VMEM((n_t - 1, slots, width), BF16),
+        pltpu.VMEM((2, slots, width), BF16),
+        pltpu.VMEM((2, slots, width), BF16),
+        pltpu.VMEM((2, slots, width), BF16),
+        pltpu.VMEM((2, slots, width), BF16),
+        pltpu.VMEM((2, slots, width), BF16),
+        pltpu.VMEM((2, slots, width), BF16),
         pltpu.VMEM((slots, width), F32),
         pltpu.VMEM((rows, width), BF16),
         pltpu.VMEM((slots, width), BF16),
@@ -960,11 +1144,11 @@
         (hidden, piece) if turn else (piece, hidden),
     )
     scratch += [pltpu.VMEM(shape, F32) for shape in shapes]
-    copies = 120 + 20 * group
+    copies = 160 + 20 * group
     scratch += [
         pltpu.SemaphoreType.DMA((copies,)),
         pltpu.SemaphoreType.DMA((copies,)),
-        pltpu.SemaphoreType.DMA((24,)),
+        pltpu.SemaphoreType.DMA((48,)),
     ]
     results = [jax.ShapeDtypeStruct((rows, width), BF16)] * 2
     results += [jax.ShapeDtypeStruct(shape, F32) for shape in shapes]
@@ -1004,7 +1188,7 @@
         in_specs=[hbm] * 6 + [vmem],
         out_specs=(vmem,) * 14,
         scratch_shapes=[pltpu.SemaphoreType.DMA((6,))],
-        compiler_params=pltpu.CompilerParams(vmem_limit_bytes=32 << 20),
+        compiler_params=pltpu.CompilerParams(vmem_limit_bytes=63 << 20),
     )(*outs)
     block_out, tokens_grad, d_win, d_wot, d_wup, d_wdt = placed[:6]
     vectors = [v.reshape(piece) for v in placed[6:12]]

time: 159 us -> 145 us (0.912)
  local copies, waits for them, and re-layouts: 6.99 us -> 0 us
  Pallas kernels: 150 us -> 144 us
    pallas_call x1, Pallas kernels: 147 us -> 140 us  [on_device(): pl.pallas_call(functools.partial(block_kernel, sizes), out_shape=(*result...]
    unnamed x14 -> x0, local copies, waits for them, and re-layouts: 6.99 us -> none
where the time goes in v3:
time: 145 us
  Pallas kernels  144 us (99%)
    pallas_call x1, Pallas kernels, on_device(): pl.pallas_call(functools.partial(block_kernel, sizes), out_shape=(*result...  140 us
    pallas_call x1, Pallas kernels, on_device(): pl.pallas_call(functools.partial(finish_call, (n_ctx, piece, cut, wide, h...  4.3 us

profile of v3, /device:TPU:0, one launch (start us, length us, event | category | flops | bytes accessed | tf_op | source)
XLA Modules:
  0.0 144.8 jit_solution(3006418704792010928)
XLA Ops:
  0.7 139.6 %shard_map.254 = (bf16[320,1024]{1,0:T(8,128)(2,1)}, bf16[320,1024]{1,0:T(8,128)(2,1)}, f32[3,128,256]{2,1,0:T(8,128)}, f32[256,128]{1,0:T(8,128)}, f32[128,1024...) custom-call(bf16[320,1024]{1,0:T(8,128)(2,1)} %bitcast.20, bf16[320,1024]{1,0:T(8,128)(2,1)} %bitcast.21, ...), custom_call_target="tpu_custom_call" | custom-call | tf_op jit(solution)/shard_map/pallas_call | solution.py:1155
  140.3 4.3 %shard_map.255 = (bf16[320,1024]{1,0:T(8,128)(2,1)}, bf16[320,1024]{1,0:T(8,128)(2,1)}, f32[3,128,256]{2,1,0:T(8,128)}, f32[256,128]{1,0:T(8,128)}, f32[128,1024...) custom-call(bf16[320,1024]{1,0:T(8,128)(2,1)} %get-tuple-element.35., ...), custom_call_target="tpu_custom_call" | custom-call | tf_op jit(solution)/shard_map/pallas_call | solution.py:1180

commit v4 on v3

--- a/solution.py
+++ b/solution.py
@@ -122,9 +122,14 @@
     block_own,
     tokens_own,
     gv,
-    vr_sib,
-    vr_plane,
-    vr_z,
+    early,
+    early_sib,
+    early_plane,
+    early_z,
+    late,
+    late_sib,
+    late_plane,
+    late_z,
     b_win,
     b_wot,
     b_wup,
@@ -185,7 +190,7 @@
     own = slot_at(ctx)
     mine = slot_at(z)
 
-    cut_at = ROWS * ((slots // ROWS + 1) // 2)
+    cut_at = ROWS * (slots // ROWS // 2)
     starts = (0, cut_at)
     sizes_of = (cut_at, slots - cut_at)
     bases = (0, images * cut_at)
@@ -261,8 +266,11 @@
     planes = range(1, group)
     zs = range(1, n_t)
 
-    def at_win(m, c):
-        return g_win.at[:, m, c]
+    def at_win_kv(m, c):
+        return g_win.at[1:3, m, c]
+
+    def at_win_q(m, c):
+        return g_win.at[0:1, m, c]
 
     def at_wot(m, c):
         return g_wot.at[m, c, :, lane_at(z, wide)]
@@ -291,7 +299,7 @@
         ]
 
     tok_load = load_rows(tok_in, tok)
-    win_own = local(win, at_win(me, core))
+    win_own = local(win, g_win.at[:, me, core])
     c_out_load = local(contract_out, c_out)
     cot_load = load_rows(cot_in, cot)
     wup_own = local(wup, at_wup(me, core))
@@ -332,6 +340,34 @@
         for copy in passed:
             copy.wait_recv()
 
+    relayed = group == 4 and piece % (2 * ROWS) == 0
+
+    def relay_start(src, at):
+        if not relayed:
+            return gather_start(src, at)
+        far = [send(src, at(me, core), plane(k)) for k in (1, 2)]
+        return far, send(src, at(me, core), sib)
+
+    def relay_forward(started, at):
+        if not relayed:
+            return gather_forward(started, at), []
+        out, halves = [], []
+        for k in (1, 2):
+            started[0][k - 1].wait_recv()
+            there = at(flip(me, k), core)
+            part = there.at[pl.ds((k - 1) * (piece // 2), piece // 2)]
+            halves.append(send(part, part, plane(3 - k)))
+            out.append(send(there, there, sib))
+        return out, halves
+
+    def relay_last(halves, at):
+        if not halves:
+            return []
+        for copy in halves:
+            copy.wait_recv()
+        there = at(flip(me, 3), core)
+        return [send(there, there, sib)]
+
     def ctx_start(at):
         far = [send(at(ctx), at(ctx), (dp, ctx_at(k), z)) for k in range(1, half)]
         return far, send(at(ctx), at(ctx), sib)
@@ -352,7 +388,8 @@
         return g_wot.at[m, core, :, lane_at(index, wide)]
 
     vec_started = gather_start(vec, at_vec)
-    win_started = gather_start(win, at_win)
+    kv_win_started = gather_start(win.at[1:3], at_win_kv)
+    q_win_started = gather_start(win.at[0:1], at_win_q)
     wot_started = gather_start(at_wot(me, core), at_wot)
     wot_z = [[send(wot_piece(me, z), wot_piece(me, z), zpeer(k)) for k in zs]]
 
@@ -435,9 +472,9 @@
             line = image * heads + h
             ref[ctx, line : line + 1, :] = jnp.sum(part, axis=0, keepdims=True)
 
-    win_passed = gather_forward(win_started, at_win)
+    win_passed = gather_forward(kv_win_started, at_win_kv)
     win_own.wait()
-    gather_finish(win_started, win_passed)
+    gather_finish(kv_win_started, win_passed)
 
     def project(j, bias):
         out = nn(h1[...], g_win[j].reshape(width, wide))
@@ -449,32 +486,42 @@
             block = out[chunk(c)].reshape(images, sizes_of[c], wide)
             qkv[:, place_at, j * wide : (j + 1) * wide] = block
 
-    def at_kv(index):
-        return qkv.at[:, slot_at(index), wide : 3 * wide]
+    def at_kv(images_of):
+        def at(index):
+            return qkv.at[images_of, slot_at(index), wide : 3 * wide]
+
+        return at
 
     def at_q(index):
         return qkv.at[:, slot_at(index), 0:wide]
 
     project(1, None)
     project(2, 10)
-    kv_started = ctx_start(at_kv)
-    wup_started = gather_start(wup, at_wup)
-    wdt_started = gather_start(at_wdt(me, core), at_wdt)
+    middle = images // 2
+    image_parts = (slice(0, middle), slice(middle, images))
+    kv_started = [ctx_start(at_kv(part)) for part in image_parts]
+    wup_started = relay_start(wup, at_wup)
+    wdt_started = relay_start(at_wdt(me, core), at_wdt)
+    win_passed = gather_forward(q_win_started, at_win_q)
+    gather_finish(q_win_started, win_passed)
+    project(0, 9)
+    q_started = ctx_start(at_q)
     wot_passed = []
     for k in planes:
         wot_started[0][k - 1].wait_recv()
         there = wot_piece(flip(me, k), z)
         wot_z.append([send(there, there, zpeer(j)) for j in zs])
         wot_passed.append(send(there, there, sib))
-    project(0, 9)
-    q_started = ctx_start(at_q)
-    kv_passed = ctx_forward(kv_started, at_kv)
-    ctx_finish(kv_started, kv_passed)
 
     def at_mixed(index, c):
         return mixed.at[chunk(c), lane_at(index, wide)]
 
     for image in range(images):
+        for part in range(2):
+            if image == image_parts[part].start:
+                kv_at = at_kv(image_parts[part])
+                kv_passed = ctx_forward(kv_started[part], kv_at)
+                ctx_finish(kv_started[part], kv_passed)
         key_live = key_id < lengths[image : image + 1, :]
         stacked = stack_heads(qkv[image, own, 0:wide])
         scores = nt(stacked, qkv[image, :, wide : 2 * wide]) * scale
@@ -506,6 +553,7 @@
             live = row_live[image][slot_part(c)]
             gdown[at, :] = jnp.where(live, cot[at, :].astype(F32), 0.0).astype(BF16)
 
+    wup_passed, wup_halves = relay_forward(wup_started, at_wup)
     gather_finish(wot_started, wot_passed)
     wot_more = []
     for order, block in enumerate(wot_z):
@@ -513,15 +561,16 @@
             block[k - 1].wait_recv()
             there = wot_piece(flip(me, order), flip(z, k))
             wot_more.append(send(there, there, sib))
-    wup_passed = gather_forward(wup_started, at_wup)
     wup_own.wait()
+    wdt_passed, wdt_halves = relay_forward(wdt_started, at_wdt)
+    wup_passed += relay_last(wup_halves, at_wup)
     for copy in wot_more:
         copy.wait_recv()
 
     some = group // (width // TILE)
 
     def scatter(part, recv, relay, c):
-        marks = [fresh() for _ in range(4)]
+        marks = [fresh() for _ in range(5)]
 
         def onward(j):
             return remote(
@@ -543,9 +592,11 @@
 
         for j in range(2):
             send_if(at_end, functools.partial(onward, j))
-        near = send(
-            part.at[rows_at(c, flip(z, 1)), :], recv.at[0, slot_part(c), :], zpeer(1)
-        )
+        near = []
+
+        def send_near():
+            source = part.at[rows_at(c, flip(z, 1)), :]
+            near.append(send(source, recv.at[0, slot_part(c), :], zpeer(1)))
 
         def pass_on():
             for j in range(2):
@@ -560,10 +611,10 @@
                 send_if(inside, functools.partial(passed, j))
 
         def finish():
-            near.wait_recv()
+            near[0].wait_recv()
             passed(0).wait_recv()
 
-        return pass_on, finish
+        return pass_on, finish, send_near
 
     def spread(source, at):
         marks = [fresh() for _ in range(4)]
@@ -618,15 +669,12 @@
 
         lax.fori_loop(0, width // TILE, project_out, 0)
 
-        def second_norm(step, carry):
-            at = pl.ds(pl.multiple_of(bases[c] + step * BLOCK, BLOCK), BLOCK)
+        for row in range(bases[c], bases[c] + images * sizes_of[c], ROWS):
+            at = slice(row, row + ROWS)
             value = tok[at, :].astype(F32) + first[at, :] + vx[2:3, :]
             first[at, :] = value
             normed, _ = norm_parts(value)
             h2[at, :] = (normed * vx[3:4, :] + vx[4:5, :]).astype(BF16)
-            return carry
-
-        lax.fori_loop(0, images * sizes_of[c] // BLOCK, second_norm, 0)
 
     def feed_forward(c):
         at_rows = chunk(c)
@@ -653,19 +701,29 @@
         lax.fori_loop(0, width // TILE, up_back, 0)
         return scatter(part2, recv2, relay2, c)
 
-    for c in range(2):
-        attended(c)
-    wdt_passed = gather_forward(wdt_started, at_wdt)
+    attended(0)
+    wdt_passed += relay_last(wdt_halves, at_wdt)
     gather_finish(wup_started, wup_passed)
     gather_finish(wdt_started, wdt_passed)
 
-    def down_back(step, carry):
-        at = lane_at(step, TILE)
-        ga[:, at] = nn(gdown[...], g_wdt[:, :, :, at].reshape(width, TILE))
-        return carry
-
-    lax.fori_loop(0, hidden // TILE, down_back, 0)
-    sent2 = [feed_forward(c) for c in range(2)]
+    def down_back(c):
+        at_rows = chunk(c)
+
+        def one(step, carry):
+            at = lane_at(step, TILE)
+            weight = g_wdt[:, :, :, at].reshape(width, TILE)
+            ga[at_rows, at] = nn(gdown[at_rows, :], weight)
+            return carry
+
+        lax.fori_loop(0, hidden // TILE, one, 0)
+
+    down_back(0)
+    sent2 = [feed_forward(0)]
+    sent2[0][2]()
+    down_back(1)
+    attended(1)
+    sent2.append(feed_forward(1))
+    sent2[1][2]()
 
     def contract(step, carry):
         weight = g_wdt[pl.ds(step * some, some)].reshape(TILE, hidden)
@@ -673,6 +731,8 @@
         return carry
 
     lax.fori_loop(0, width // TILE, contract, 0)
+    sents = [scatter(parts, recvs, relays, 0)]
+    sents[0][2]()
 
     def wide_grad(buf, left, right, lanes):
         def one(step, carry):
@@ -734,9 +794,6 @@
         keepdims=True,
     )
 
-    def add_line(line, value):
-        gv[line : line + 1, :] += jnp.sum(value, axis=0, keepdims=True)
-
     def norm_back(grad, normed, inv, gain):
         scaled = grad * gain
         inner = (
@@ -749,23 +806,20 @@
     def second_back(c):
         sent2[c][1]()
 
-        def one(step, carry):
-            at = step * ROWS
+        sums = [0.0, 0.0, 0.0, 0.0]
+        for at in range(0, sizes_of[c], ROWS):
             here = pl.ds(pl.multiple_of(bases[c] + z * sizes_of[c] + at, ROWS), ROWS)
             grad = arrived(part2, recv2, c, at, ROWS)
             normed, inv = norm_parts(first[here, :])
             rows_grad = gdown[here, :].astype(F32)
             value = rows_grad + norm_back(grad, normed, inv, vx[3:4, :])
-            there = pl.ds(pl.multiple_of(starts[c] + at, ROWS), ROWS)
+            there = slice(starts[c] + at, starts[c] + at + ROWS)
             gfirst[there, :] = value
             gown[there, :] = value.astype(BF16)
-            add_line(3, grad * normed)
-            add_line(4, grad)
-            add_line(5, rows_grad)
-            add_line(2, value)
-            return carry
-
-        lax.fori_loop(0, sizes_of[c] // ROWS, one, 0)
+            terms = (value, grad * normed, grad, rows_grad)
+            sums = [old + jnp.sum(term, axis=0, keepdims=True) for old, term in zip(sums, terms)]
+        for line, value in enumerate(sums):
+            gv[2 + line : 3 + line, :] += value
 
         def mixed_back(step, carry):
             at = lane_at(step, wide)
@@ -787,7 +841,49 @@
         return sent
 
     to_heads = [second_back(c) for c in range(2)]
-    sents = [scatter(parts, recvs, relays, c) for c in range(2)]
+
+    per = width // LANES
+
+    def pack(ref, row, value):
+        for i in range(value.shape[1] // LANES):
+            ref[row + i : row + i + 1, :] = value[:, i * LANES : (i + 1) * LANES]
+
+    def unpack(ref, row, size):
+        return jnp.concatenate([ref[row + i : row + i + 1, :] for i in range(size // LANES)], axis=1)
+
+    for line in range(4):
+        pack(early, line * per, gv[2 + line : 3 + line, :])
+    pack(early, 4 * per, gv[8:9, 0:hidden])
+
+    def vector_z(ref, recv, size):
+        return [send(ref.at[0:size], recv.at[k - 1], zpeer(k)) for k in reversed(zs)]
+
+    def vector_near(copies, ref, recv, size, near):
+        for copy in copies:
+            complete(copy)
+        value = ref[0:size]
+        for k in zs:
+            value = value + recv[k - 1]
+        ref[0:size] = value
+        return send(ref, near, sib)
+
+    def vector_far(copy, ref, near, recv):
+        complete(copy)
+        ref[...] = ref[...] + near[...]
+        return [send(ref, recv.at[k - 1], plane(k)) for k in planes]
+
+    def vector_last(copies, ref, recv):
+        for copy in copies:
+            complete(copy)
+        value = ref[...]
+        for k in planes:
+            value = value + recv[k - 1]
+        ref[...] = value
+
+    vector_copies = vector_z(early, early_z, 4 * per)
+    sents.append(scatter(parts, recvs, relays, 1))
+    sents[1][2]()
+    sents[0][0]()
 
     def out_grad(step, carry):
         at = lane_at(step, TILE)
@@ -844,9 +940,11 @@
         return alng.at[index]
 
     along_started = ctx_start(at_along)
+    vector_copy = vector_near(vector_copies, early, early_z, 4 * per, early_sib)
     wot_far = grad_far(wot_near, b_wot, s_wot, t_wot, r_wot)
+    early_far = vector_far(vector_copy, early, early_sib, early_plane)
     wup_far = grad_far(wup_near, b_wup, s_wup, t_wup, r_wup)
-    sents[0][0]()
+    sents[1][0]()
     do_passed = [ctx_forward(do_started[c], at_do(c)) for c in range(2)]
     along_passed = ctx_forward(along_started, at_along)
     for c in range(2):
@@ -885,17 +983,21 @@
         lax.fori_loop(0, width // TILE, one, 0)
         return scatter(part1, recv1, relay1, c)
 
+    tail = [block_rows(0)]
     sent1 = [in_back(c) for c in range(2)]
-    sents[1][0]()
+    for c in range(2):
+        sent1[c][2]()
+    tail.append(block_rows(1))
 
     for j in range(3):
         out = tn(h1[...], dqkv[:, j * wide : (j + 1) * wide]).astype(BF16)
         b_win[j] = out.reshape(group, 2, piece, wide)
     win_near = send(b_win.at[:, :, 1 - core], s_win, sib)
     sent1[0][0]()
-    tail = [block_rows(0)]
-    gv[9:10, 0:wide] = jnp.sum(dqkv[:, 0:wide].astype(F32), axis=0, keepdims=True)
-    gv[10:11, 0:wide] = jnp.sum(dqkv[:, 2 * wide : 3 * wide].astype(F32), axis=0, keepdims=True)
+    late[2 * per :, :] = jnp.zeros((late.shape[0] - 2 * per, LANES), F32)
+    for j, start in enumerate((0, 2 * wide)):
+        value = jnp.sum(dqkv[:, start : start + wide].astype(F32), axis=0, keepdims=True)
+        pack(late, 2 * per + j * (wide // LANES), value)
     f_wdt[...] = turned(grad_sum(wdt_far, t_wdt, r_wdt), f_wdt)
     stays.append(local(f_wdt, out_wdt))
     win_near.wait_recv()
@@ -905,55 +1007,45 @@
     win_far = [send(t_win.at[flip(me, k)], r_win.at[k - 1], plane(k)) for k in reversed(planes)]
 
     sent1[1][0]()
-    tail.append(block_rows(1))
     whole_rows = grad_sum(wot_far, t_wot, r_wot)
     o_wot[...] = whole_rows.astype(BF16)
     to_owner = [
         send(o_wot.at[:, lane_at(flip(z, k), wide)], z_wot.at[k - 1], zpeer(k))
         for k in reversed(zs)
     ]
-    f_wup[...] = grad_sum(wup_far, t_wup, r_wup)
-    stays.append(local(f_wup, out_wup))
 
     def first_back(c):
         sent1[c][1]()
 
-        def one(step, carry):
-            at = step * ROWS
+        sums = [0.0, 0.0]
+        for at in range(0, sizes_of[c], ROWS):
             here = pl.ds(pl.multiple_of(bases[c] + z * sizes_of[c] + at, ROWS), ROWS)
             grad = arrived(part1, recv1, c, at, ROWS)
             normed, inv = norm_parts(tok[here, :].astype(F32))
-            there = pl.ds(pl.multiple_of(starts[c] + at, ROWS), ROWS)
+            there = slice(starts[c] + at, starts[c] + at + ROWS)
             value = gfirst[there, :] + norm_back(grad, normed, inv, vx[0:1, :])
             tokens_own[there, :] = value.astype(BF16)
-            add_line(0, grad * normed)
-            add_line(1, grad)
-            return carry
-
-        lax.fori_loop(0, sizes_of[c] // ROWS, one, 0)
-        return to_all(tokens_own, out_tokens, c)
+            terms = (grad * normed, grad)
+            sums = [old + jnp.sum(term, axis=0, keepdims=True) for old, term in zip(sums, terms)]
+        return sums
 
     for c in range(2):
         tail[c][0]()
-    for c in range(2):
-        tail.append(first_back(c))
-
-    near = send(gv, vr_sib, sib)
+    sums = first_back(0)
+    tail.append(to_all(tokens_own, out_tokens, 0))
+    for line, (one, two) in enumerate(zip(sums, first_back(1))):
+        pack(late, line * per, one + two)
+    vector_copies = vector_z(late, late_z, 2 * per)
+    tail.append(to_all(tokens_own, out_tokens, 1))
+    f_wup[...] = grad_sum(wup_far, t_wup, r_wup)
+    stays.append(local(f_wup, out_wup))
+    vector_last(early_far, early, early_plane)
     tail[2][0]()
-    complete(near)
-    gv[...] = gv[...] + vr_sib[...]
-    far = [send(gv, vr_plane.at[k - 1], plane(k)) for k in planes]
+    vector_copy = vector_near(vector_copies, late, late_z, 2 * per, late_sib)
     tail[3][0]()
+    late_far = vector_far(vector_copy, late, late_sib, late_plane)
     f_win[...] = grad_sum(win_far, t_win, r_win)
     stays.append(local(f_win, out_win))
-    for copy in far:
-        complete(copy)
-    value = gv[...]
-    for k in planes:
-        value = value + vr_plane[k - 1]
-    gv[...] = value
-    lanes = lane_at(lax.div(shard * piece, LANES), LANES)
-    far = [send(gv.at[0:8, lanes], vr_z.at[k - 1], zpeer(k)) for k in zs]
     for copy in to_owner:
         copy.wait_recv()
     value = o_wot[:, lane_at(z, wide)].astype(F32)
@@ -961,15 +1053,17 @@
         value = value + z_wot[k - 1].astype(F32)
     f_wot[...] = turned(value, f_wot)
     stays.append(local(f_wot, out_wot))
-    for copy in far:
-        complete(copy)
-    value = gv[0:8, lanes]
-    for k in zs:
-        value = value + vr_z[k - 1]
-    gv[0:8, lanes] = value
+    vector_last(late_far, late, late_plane)
+    for line in range(2):
+        gv[line : line + 1, :] = unpack(late, line * per, width)
+        row = 2 * per + line * (wide // LANES)
+        gv[9 + line : 10 + line, 0:wide] = unpack(late, row, wide)
+    for line in range(4):
+        gv[2 + line : 3 + line, :] = unpack(early, line * per, width)
+    gv[8:9, 0:hidden] = unpack(early, 4 * per, hidden)
     stays.append(local(gv, out_vec))
-    for _, finish in tail:
-        finish()
+    for passing in tail:
+        passing[1]()
     for copy in pending:
         copy.wait_send()
     for flag, make in guarded:
@@ -983,7 +1077,7 @@
 
 
 def finish_call(sizes, *refs):
-    finish_kernel(sizes, *refs[:13], refs[13:19], *refs[19:])
+    finish_kernel(sizes, *refs[:13], refs[13:19], *refs[19:21], refs[21:27], refs[27])
 
 
 def finish_kernel(
@@ -1004,18 +1098,29 @@
     vectors,
     units,
     biases,
+    held,
     sems,
 ):
     n_ctx, piece, cut, wide, hidden, width = sizes
     shard = lax.axis_index("dp") * n_ctx + lax.axis_index("ctx")
     pairs = [(in_block, block), (in_tokens, tokens), (in_win, win)]
     pairs += [(in_wot, wot), (in_wup, wup), (in_wdt, wdt)]
-    copies = [pltpu.make_async_copy(a, b, sems.at[i]) for i, (a, b) in enumerate(pairs)]
-    for copy in copies:
+    ins = [pltpu.make_async_copy(a, h, sems.at[0, i]) for i, ((a, _), h) in enumerate(zip(pairs, held))]
+    outs = [pltpu.make_async_copy(h, b, sems.at[1, i]) for i, ((_, b), h) in enumerate(zip(pairs, held))]
+    for copy in ins:
         copy.start()
+    for into, out_of in zip(ins, outs):
+        into.wait()
+        out_of.start()
 
     def exact(left, right):
-        return jnp.dot(left, right, precision=lax.Precision.HIGHEST, preferred_element_type=F32)
+        parts, rest = [], left
+        for _ in range(3):
+            parts.append(rest.astype(BF16).astype(F32))
+            rest = rest - parts[-1]
+        count = left.shape[0]
+        product = nn(jnp.concatenate(parts, axis=0).astype(BF16), right.astype(BF16))
+        return product[0:count] + product[count : 2 * count] + product[2 * count :]
 
     heads = wide // HD
     lane = lax.broadcasted_iota(jnp.int32, (width, piece), 0)
@@ -1037,7 +1142,7 @@
     for j in range(2):
         chosen = jnp.where(lane // HD == head, in_vec[9 + j : 10 + j, 0:wide], 0.0)
         biases[j] = exact(chosen, pick)
-    for copy in copies:
+    for copy in outs:
         copy.wait()
 
 
@@ -1069,6 +1174,9 @@
     total = slots * n_ctx
     heads = wide // HD
     turn = piece % LANES == 0
+    per = width // LANES
+    early_rows = 4 * per + hidden // LANES
+    late_rows = 2 * per + 8 * ((2 * wide // LANES + 7) // 8)
     sizes = (n_dp, n_ctx, n_t, images, slots, width, wide, hidden, piece, cut)
     vmem = pl.BlockSpec(memory_space=pltpu.VMEM)
     hbm = pl.BlockSpec(memory_space=pl.ANY)
@@ -1115,9 +1223,14 @@
         pltpu.VMEM((slots, width), BF16),
         pltpu.VMEM((slots, width), BF16),
         pltpu.VMEM((ROWS, width), F32),
-        pltpu.VMEM((ROWS, width), F32),
-        pltpu.VMEM((group - 1, ROWS, width), F32),
-        pltpu.VMEM((n_t - 1, 8, LANES), F32),
+        pltpu.VMEM((early_rows, LANES), F32),
+        pltpu.VMEM((early_rows, LANES), F32),
+        pltpu.VMEM((group - 1, early_rows, LANES), F32),
+        pltpu.VMEM((n_t - 1, 4 * per, LANES), F32),
+        pltpu.VMEM((late_rows, LANES), F32),
+        pltpu.VMEM((late_rows, LANES), F32),
+        pltpu.VMEM((group - 1, late_rows, LANES), F32),
+        pltpu.VMEM((n_t - 1, 2 * per, LANES), F32),
         pltpu.VMEM((3, group, 2, piece, wide), BF16),
         pltpu.VMEM((group, 2, piece, n_t * wide), BF16),
         pltpu.VMEM((group, 2, piece, hidden), BF16),
@@ -1186,8 +1299,9 @@
             jax.ShapeDtypeStruct((2, heads, cut), F32),
         ),
         in_specs=[hbm] * 6 + [vmem],
-        out_specs=(vmem,) * 14,
-        scratch_shapes=[pltpu.SemaphoreType.DMA((6,))],
+        out_specs=(hbm,) * 6 + (vmem,) * 8,
+        scratch_shapes=[pltpu.VMEM(r.shape, r.dtype) for r in results]
+        + [pltpu.SemaphoreType.DMA((2, 6))],
         compiler_params=pltpu.CompilerParams(vmem_limit_bytes=63 << 20),
     )(*outs)
     block_out, tokens_grad, d_win, d_wot, d_wup, d_wdt = placed[:6]

time: 145 us -> 135 us (0.931)
  Pallas kernels: 144 us -> 134 us
    pallas_call x1, Pallas kernels: 140 us -> 130 us  [on_device(): pl.pallas_call(functools.partial(block_kernel, sizes), out_shape=(*result...]
where the time goes in v4:
time: 135 us
  Pallas kernels  134 us (99%)
    pallas_call x1, Pallas kernels, on_device(): pl.pallas_call(functools.partial(block_kernel, sizes), out_shape=(*result...  130 us
    pallas_call x1, Pallas kernels, on_device(): pl.pallas_call(functools.partial(finish_call, (n_ctx, piece, cut, wide, h...  4.23 us

profile of v4, /device:TPU:0, one launch (start us, length us, event | category | flops | bytes accessed | tf_op | source)
XLA Modules:
  0.0 135.0 jit_solution(9639661121445988078)
XLA Ops:
  0.7 130.0 %shard_map.254 = (bf16[320,1024]{1,0:T(8,128)(2,1)}, bf16[320,1024]{1,0:T(8,128)(2,1)}, f32[3,128,256]{2,1,0:T(8,128)}, f32[256,128]{1,0:T(8,128)}, f32[128,1024...) custom-call(bf16[320,1024]{1,0:T(8,128)(2,1)} %bitcast.20, bf16[320,1024]{1,0:T(8,128)(2,1)} %bitcast.21, ...), custom_call_target="tpu_custom_call" | custom-call | tf_op jit(solution)/shard_map/pallas_call | solution.py:1268
  130.7 4.2 %shard_map.255 = (bf16[320,1024]{1,0:T(8,128)(2,1)}, bf16[320,1024]{1,0:T(8,128)(2,1)}, f32[3,128,256]{2,1,0:T(8,128)}, f32[256,128]{1,0:T(8,128)}, f32[128,1024...) custom-call(bf16[320,1024]{1,0:T(8,128)(2,1)} %get-tuple-element.35., ...), custom_call_target="tpu_custom_call" | custom-call | tf_op jit(solution)/shard_map/pallas_call | solution.py:1293

commit v5 on v4

--- a/solution.py
+++ b/solution.py
@@ -210,6 +210,7 @@
             ref[rows_at(c, image), lanes] = value[slot_part(c)]
 
     count = [0, 0]
+    stays = []
     pending = []
 
     def send(src, dst, device):
@@ -245,12 +246,13 @@
             device_id_type=MESH,
         )
 
-    def send_if(flag, make):
-        guarded.append((flag, make))
+    def send_if(flag, makes):
+        guarded.append((flag, makes))
 
         @pl.when(flag)
         def _():
-            make().start()
+            for make in makes:
+                make().start()
 
     def complete(copy):
         pending[:] = [other for other in pending if other is not copy]
@@ -388,9 +390,12 @@
         return g_wot.at[m, core, :, lane_at(index, wide)]
 
     vec_started = gather_start(vec, at_vec)
+    wot_own = at_wot(me, core)
+    wot_far = [send(wot_own, wot_own, plane(k)) for k in planes if k < 3]
     kv_win_started = gather_start(win.at[1:3], at_win_kv)
+    wot_far += [send(wot_own, wot_own, plane(k)) for k in planes if k >= 3]
+    wot_started = (wot_far, send(wot_own, wot_own, sib))
     q_win_started = gather_start(win.at[0:1], at_win_q)
-    wot_started = gather_start(at_wot(me, core), at_wot)
     wot_z = [[send(wot_piece(me, z), wot_piece(me, z), zpeer(k)) for k in zs]]
 
     for copy in tok_load:
@@ -439,6 +444,18 @@
 
     lax.fori_loop(0, rows // BLOCK, first_hidden, 0)
 
+    wot_passed = []
+
+    def wot_onward(k):
+        wot_started[0][k - 1].wait_recv()
+        there = wot_piece(flip(me, k), z)
+        wot_z.append([send(there, there, zpeer(j)) for j in reversed(zs)][::-1])
+        wot_passed.append(send(there, there, sib))
+
+    for k in planes:
+        if k < 3:
+            wot_onward(k)
+
     c_out_load.wait()
 
     def turn(step, carry):
@@ -502,20 +519,19 @@
     kv_started = [ctx_start(at_kv(part)) for part in image_parts]
     wup_started = relay_start(wup, at_wup)
     wdt_started = relay_start(at_wdt(me, core), at_wdt)
+    for k in planes:
+        if k >= 3:
+            wot_onward(k)
     win_passed = gather_forward(q_win_started, at_win_q)
     gather_finish(q_win_started, win_passed)
     project(0, 9)
-    q_started = ctx_start(at_q)
-    wot_passed = []
-    for k in planes:
-        wot_started[0][k - 1].wait_recv()
-        there = wot_piece(flip(me, k), z)
-        wot_z.append([send(there, there, zpeer(j)) for j in zs])
-        wot_passed.append(send(there, there, sib))
-
-    def at_mixed(index, c):
-        return mixed.at[chunk(c), lane_at(index, wide)]
-
+
+    def at_mixed(index, c, part):
+        first_row = bases[c] + part.start * sizes_of[c]
+        last_row = bases[c] + part.stop * sizes_of[c]
+        return mixed.at[first_row:last_row, lane_at(index, wide)]
+
+    mixed_sent = [[], []]
     for image in range(images):
         for part in range(2):
             if image == image_parts[part].start:
@@ -534,14 +550,14 @@
         put_rows(stat, image, top + jnp.log(whole))
         out = nn(probs.astype(BF16), qkv[image, :, 2 * wide : 3 * wide])
         split_rows(mixed, image, lane_at(z, wide), pick_heads(out).astype(BF16))
-    mixed_sent = [
-        [send(at_mixed(z, c), at_mixed(z, c), zpeer(k)) for k in reversed(zs)] for c in range(2)
-    ]
+        for part in image_parts:
+            if image == part.stop - 1:
+                for c in range(2):
+                    there = at_mixed(z, c, part)
+                    mixed_sent[c] += [send(there, there, zpeer(k)) for k in reversed(zs)]
 
     def at_stat(index):
         return stat.at[index]
-
-    stat_started = ctx_start(at_stat)
 
     for copy in cot_load:
         copy.wait()
@@ -563,35 +579,47 @@
             wot_more.append(send(there, there, sib))
     wup_own.wait()
     wdt_passed, wdt_halves = relay_forward(wdt_started, at_wdt)
+    q_started = ctx_start(at_q)
+    stat_started = ctx_start(at_stat)
     wup_passed += relay_last(wup_halves, at_wup)
     for copy in wot_more:
         copy.wait_recv()
 
     some = group // (width // TILE)
 
+    def pieces(c):
+        return range(0, sizes_of[c], ROWS)
+
+    def block_at(c, index, at):
+        first_row = bases[c] + index * sizes_of[c] + at
+        return pl.ds(pl.multiple_of(first_row, ROWS), ROWS)
+
+    def slots_at(c, at):
+        return slice(starts[c] + at, starts[c] + at + ROWS)
+
     def scatter(part, recv, relay, c):
-        marks = [fresh() for _ in range(5)]
-
-        def onward(j):
+        marks = {at: [fresh() for _ in range(4)] for at in pieces(c)}
+
+        def onward(j, at):
             return remote(
-                part.at[rows_at(c, flip(z, 3 - j)), :],
-                relay.at[j, slot_part(c), :],
+                part.at[block_at(c, flip(z, 3 - j), at), :],
+                relay.at[j, slots_at(c, at), :],
                 zpeer(1),
-                marks[j],
-                marks[j],
+                marks[at][j],
+                marks[at][j],
             )
 
-        def passed(j):
+        def passed(j, at):
             return remote(
-                relay.at[j, slot_part(c), :],
-                recv.at[1, slot_part(c), :],
+                relay.at[j, slots_at(c, at), :],
+                recv.at[1, slots_at(c, at), :],
                 zpeer(2 + j),
-                marks[2 + j],
-                marks[2],
+                marks[at][2 + j],
+                marks[at][2],
             )
 
-        for j in range(2):
-            send_if(at_end, functools.partial(onward, j))
+        both = [(at, j) for at in pieces(c) for j in range(2)]
+        send_if(at_end, [functools.partial(onward, j, at) for at, j in both])
         near = []
 
         def send_near():
@@ -599,53 +627,66 @@
             near.append(send(source, recv.at[0, slot_part(c), :], zpeer(1)))
 
         def pass_on():
-            for j in range(2):
-
-                @pl.when(inside)
-                def _():
-                    onward(j).wait_recv()
-                    value = part[rows_at(c, flip(z, 2 + j)), :].astype(F32)
-                    value = value + relay[j, slot_part(c), :].astype(F32)
-                    relay[j, slot_part(c), :] = value.astype(BF16)
-
-                send_if(inside, functools.partial(passed, j))
+            guarded.append((inside, [functools.partial(passed, j, at) for at, j in both]))
+
+            @pl.when(inside)
+            def _():
+                for at, j in both:
+                    onward(j, at).wait_recv()
+                    value = part[block_at(c, flip(z, 2 + j), at), :].astype(F32)
+                    value = value + relay[j, slots_at(c, at), :].astype(F32)
+                    relay[j, slots_at(c, at), :] = value.astype(BF16)
+                    passed(j, at).start()
 
         def finish():
             near[0].wait_recv()
-            passed(0).wait_recv()
+            for at in pieces(c):
+                passed(0, at).wait_recv()
 
         return pass_on, finish, send_near
 
-    def spread(source, at):
-        marks = [fresh() for _ in range(4)]
-        near = send(source, at(z), zpeer(1))
-
-        def far(k):
-            return remote(source, at(z), zpeer(k), marks[k - 2], marks[k - 2])
-
-        def passed(k):
-            block = at(flip(z, k))
-            return remote(block, block, zpeer(1), marks[k], marks[3 - k])
-
-        send_if(at_end, functools.partial(far, 2))
-        send_if(inside, functools.partial(far, 3))
+    def to_all(source, target, c):
+        marks = {at: [fresh() for _ in range(4)] for at in pieces(c)}
+
+        def block(index):
+            first_row = index * slots + starts[c]
+            return target.at[pl.ds(pl.multiple_of(first_row, ROWS), sizes_of[c]), :]
+
+        def piece_of(index, at):
+            first_row = index * slots + starts[c] + at
+            return target.at[pl.ds(pl.multiple_of(first_row, ROWS), ROWS), :]
+
+        def far(k, at):
+            mark = marks[at][k - 2]
+            return remote(source.at[slots_at(c, at), :], piece_of(z, at), zpeer(k), mark, mark)
+
+        def passed(k, at):
+            there = piece_of(flip(z, k), at)
+            return remote(there, there, zpeer(1), marks[at][k], marks[at][3 - k])
+
+        send_if(at_end, [functools.partial(far, 2, at) for at in pieces(c)])
+        send_if(inside, [functools.partial(far, 3, at) for at in pieces(c)])
+        own_part = source.at[slot_part(c), :]
+        near = send(own_part, block(z), zpeer(1))
+        stays.append(local(own_part, block(z)))
+        both = [(k, at) for at in pieces(c) for k in (3, 2)]
 
         def pass_on():
-            for k in (3, 2):
-
-                @pl.when(inside)
-                def _():
-                    far(k).wait_recv()
-
-                send_if(inside, functools.partial(passed, k))
+            guarded.append((inside, [functools.partial(passed, k, at) for k, at in both]))
+
+            @pl.when(inside)
+            def _():
+                for k, at in both:
+                    far(k, at).wait_recv()
+                    passed(k, at).start()
 
         def finish():
             near.wait_recv()
 
             @pl.when(at_end)
             def _():
-                far(2).wait_recv()
-                far(3).wait_recv()
+                for k, at in both:
+                    far(k, at).wait_recv()
 
         return pass_on, finish
 
@@ -724,6 +765,7 @@
     attended(1)
     sent2.append(feed_forward(1))
     sent2[1][2]()
+    sent2[0][0]()
 
     def contract(step, carry):
         weight = g_wdt[pl.ds(step * some, some)].reshape(TILE, hidden)
@@ -731,8 +773,10 @@
         return carry
 
     lax.fori_loop(0, width // TILE, contract, 0)
-    sents = [scatter(parts, recvs, relays, 0)]
-    sents[0][2]()
+    sents = []
+    for c in range(2):
+        sents.append(scatter(parts, recvs, relays, c))
+        sents[c][2]()
 
     def wide_grad(buf, left, right, lanes):
         def one(step, carry):
@@ -766,10 +810,9 @@
 
     wide_grad(b_wdt, gdown, act, hidden)
     wdt_near = grad_near(b_wdt, s_wdt)
-    sent2[0][0]()
+    sent2[1][0]()
     wide_grad(b_wup, h2, gi, hidden)
     wup_near = grad_near(b_wup, s_wup)
-    sent2[1][0]()
     wdt_far = grad_far(wdt_near, b_wdt, s_wdt, t_wdt, r_wdt)
 
     q_passed = ctx_forward(q_started, at_q)
@@ -840,7 +883,10 @@
         do[z, place_at, :] = gm[slot_part(c), lane_at(z, wide)]
         return sent
 
-    to_heads = [second_back(c) for c in range(2)]
+    to_heads = [second_back(0)]
+    sents[0][0]()
+    to_heads.append(second_back(1))
+    sents[1][0]()
 
     per = width // LANES
 
@@ -881,9 +927,6 @@
         ref[...] = value
 
     vector_copies = vector_z(early, early_z, 4 * per)
-    sents.append(scatter(parts, recvs, relays, 1))
-    sents[1][2]()
-    sents[0][0]()
 
     def out_grad(step, carry):
         at = lane_at(step, TILE)
@@ -895,7 +938,6 @@
     lax.fori_loop(0, n_t * wide // TILE, out_grad, 0)
     wot_near = grad_near(b_wot, s_wot)
 
-    stays = []
 
     def block_rows(c):
         sents[c][1]()
@@ -904,15 +946,6 @@
         block_own[slot_part(c), :] = value.astype(BF16)
         return to_all(block_own, out_block, c)
 
-    def to_all(source, target, c):
-        def at(index):
-            here = pl.ds(pl.multiple_of(index * slots + starts[c], ROWS), sizes_of[c])
-            return target.at[here, :]
-
-        part = source.at[slot_part(c), :]
-        stays.append(local(part, at(z)))
-        return spread(part, at)
-
     def at_do(c):
         def at(index):
             first_row = index * slots + starts[c]
@@ -920,6 +953,7 @@
 
         return at
 
+    tail = [block_rows(0)]
     do_started = []
     for c in range(2):
         for copy in to_heads[c]:
@@ -941,10 +975,10 @@
 
     along_started = ctx_start(at_along)
     vector_copy = vector_near(vector_copies, early, early_z, 4 * per, early_sib)
-    wot_far = grad_far(wot_near, b_wot, s_wot, t_wot, r_wot)
+    tail[0][0]()
+    tail.append(block_rows(1))
+    wot_grad_far = grad_far(wot_near, b_wot, s_wot, t_wot, r_wot)
     early_far = vector_far(vector_copy, early, early_sib, early_plane)
-    wup_far = grad_far(wup_near, b_wup, s_wup, t_wup, r_wup)
-    sents[1][0]()
     do_passed = [ctx_forward(do_started[c], at_do(c)) for c in range(2)]
     along_passed = ctx_forward(along_started, at_along)
     for c in range(2):
@@ -983,11 +1017,11 @@
         lax.fori_loop(0, width // TILE, one, 0)
         return scatter(part1, recv1, relay1, c)
 
-    tail = [block_rows(0)]
     sent1 = [in_back(c) for c in range(2)]
     for c in range(2):
         sent1[c][2]()
-    tail.append(block_rows(1))
+    tail[1][0]()
+    wup_far = grad_far(wup_near, b_wup, s_wup, t_wup, r_wup)
 
     for j in range(3):
         out = tn(h1[...], dqkv[:, j * wide : (j + 1) * wide]).astype(BF16)
@@ -1007,7 +1041,7 @@
     win_far = [send(t_win.at[flip(me, k)], r_win.at[k - 1], plane(k)) for k in reversed(planes)]
 
     sent1[1][0]()
-    whole_rows = grad_sum(wot_far, t_wot, r_wot)
+    whole_rows = grad_sum(wot_grad_far, t_wot, r_wot)
     o_wot[...] = whole_rows.astype(BF16)
     to_owner = [
         send(o_wot.at[:, lane_at(flip(z, k), wide)], z_wot.at[k - 1], zpeer(k))
@@ -1029,8 +1063,6 @@
             sums = [old + jnp.sum(term, axis=0, keepdims=True) for old, term in zip(sums, terms)]
         return sums
 
-    for c in range(2):
-        tail[c][0]()
     sums = first_back(0)
     tail.append(to_all(tokens_own, out_tokens, 0))
     for line, (one, two) in enumerate(zip(sums, first_back(1))):
@@ -1066,52 +1098,30 @@
         passing[1]()
     for copy in pending:
         copy.wait_send()
-    for flag, make in guarded:
+    for flag, makes in guarded:
 
         @pl.when(flag)
         def _():
-            make().wait_send()
+            for make in makes:
+                make().wait_send()
 
     for copy in stays:
         copy.wait()
 
 
-def finish_call(sizes, *refs):
-    finish_kernel(sizes, *refs[:13], refs[13:19], *refs[19:21], refs[21:27], refs[27])
-
-
-def finish_kernel(
-    sizes,
-    in_block,
-    in_tokens,
-    in_win,
-    in_wot,
-    in_wup,
-    in_wdt,
-    in_vec,
-    block,
-    tokens,
-    win,
-    wot,
-    wup,
-    wdt,
-    vectors,
-    units,
-    biases,
-    held,
-    sems,
-):
+def finish_kernel(sizes, *refs):
     n_ctx, piece, cut, wide, hidden, width = sizes
+    sources, results, held = refs[:6], refs[7:13], refs[21:27]
+    smalls, own, vec, sems = refs[13:21], refs[27:35], refs[35], refs[36]
     shard = lax.axis_index("dp") * n_ctx + lax.axis_index("ctx")
-    pairs = [(in_block, block), (in_tokens, tokens), (in_win, win)]
-    pairs += [(in_wot, wot), (in_wup, wup), (in_wdt, wdt)]
-    ins = [pltpu.make_async_copy(a, h, sems.at[0, i]) for i, ((a, _), h) in enumerate(zip(pairs, held))]
-    outs = [pltpu.make_async_copy(h, b, sems.at[1, i]) for i, ((_, b), h) in enumerate(zip(pairs, held))]
+    load = pltpu.make_async_copy(refs[6], vec, sems.at[2, 0])
+    load.start()
+    ins, outs = [], []
+    for i in range(6):
+        ins.append(pltpu.make_async_copy(sources[i], held[i], sems.at[0, i]))
+        outs.append(pltpu.make_async_copy(held[i], results[i], sems.at[1, i]))
     for copy in ins:
         copy.start()
-    for into, out_of in zip(ins, outs):
-        into.wait()
-        out_of.start()
 
     def exact(left, right):
         parts, rest = [], left
@@ -1125,23 +1135,32 @@
     heads = wide // HD
     lane = lax.broadcasted_iota(jnp.int32, (width, piece), 0)
     slot = lax.broadcasted_iota(jnp.int32, (width, piece), 1)
-    part = exact(in_vec[0:8, :], jnp.where(lane - slot == shard * piece, 1.0, 0.0))
+    one = jnp.where(lane - slot == shard * piece, 1.0, 0.0)
+    lane = lax.broadcasted_iota(jnp.int32, (hidden, hidden // HD), 0)
+    slot = lax.broadcasted_iota(jnp.int32, (hidden, hidden // HD), 1)
+    by_unit = jnp.where(lane // HD == slot, 1.0, 0.0)
+    load.wait()
+    part = exact(vec[0:8, :], one)
     for line in range(6):
-        vectors[line][...] = part[line : line + 1]
+        own[line][...] = part[line : line + 1]
     channel = lax.broadcasted_iota(jnp.int32, (cut, hidden), 0)
     lane = lax.broadcasted_iota(jnp.int32, (cut, hidden), 1)
-    chosen = jnp.where(lane % HD - channel == shard * cut, in_vec[8:9, 0:hidden], 0.0)
-    lane = lax.broadcasted_iota(jnp.int32, (hidden, hidden // HD), 0)
-    slot = lax.broadcasted_iota(jnp.int32, (hidden, hidden // HD), 1)
-    units[...] = exact(chosen, jnp.where(lane // HD == slot, 1.0, 0.0))
+    chosen = jnp.where(lane % HD - channel == shard * cut, vec[8:9, 0:hidden], 0.0)
+    own[6][...] = exact(chosen, by_unit)
     lane = lax.broadcasted_iota(jnp.int32, (wide, cut), 0)
     slot = lax.broadcasted_iota(jnp.int32, (wide, cut), 1)
     pick = jnp.where(lane % HD - slot == shard * cut, 1.0, 0.0)
     head = lax.broadcasted_iota(jnp.int32, (heads, wide), 0)
     lane = lax.broadcasted_iota(jnp.int32, (heads, wide), 1)
     for j in range(2):
-        chosen = jnp.where(lane // HD == head, in_vec[9 + j : 10 + j, 0:wide], 0.0)
-        biases[j] = exact(chosen, pick)
+        chosen = jnp.where(lane // HD == head, vec[9 + j : 10 + j, 0:wide], 0.0)
+        own[7][j] = exact(chosen, pick)
+    for i in range(8):
+        outs.append(pltpu.make_async_copy(own[i], smalls[i], sems.at[2, 1 + i]))
+        outs[-1].start()
+    for i in range(6):
+        ins[i].wait()
+        outs[i].start()
     for copy in outs:
         copy.wait()
 
@@ -1257,7 +1276,7 @@
         (hidden, piece) if turn else (piece, hidden),
     )
     scratch += [pltpu.VMEM(shape, F32) for shape in shapes]
-    copies = 160 + 20 * group
+    copies = 260 + 20 * group
     scratch += [
         pltpu.SemaphoreType.DMA((copies,)),
         pltpu.SemaphoreType.DMA((copies,)),
@@ -1290,18 +1309,17 @@
         attend_bias,
     )
     vector = jax.ShapeDtypeStruct((1, piece), F32)
+    small = [vector] * 6 + [
+        jax.ShapeDtypeStruct((cut, hidden // HD), F32),
+        jax.ShapeDtypeStruct((2, heads, cut), F32),
+    ]
     placed = pl.pallas_call(
-        functools.partial(finish_call, (n_ctx, piece, cut, wide, hidden, width)),
-        out_shape=(
-            *results,
-            *[vector] * 6,
-            jax.ShapeDtypeStruct((cut, hidden // HD), F32),
-            jax.ShapeDtypeStruct((2, heads, cut), F32),
-        ),
-        in_specs=[hbm] * 6 + [vmem],
-        out_specs=(hbm,) * 6 + (vmem,) * 8,
-        scratch_shapes=[pltpu.VMEM(r.shape, r.dtype) for r in results]
-        + [pltpu.SemaphoreType.DMA((2, 6))],
+        functools.partial(finish_kernel, (n_ctx, piece, cut, wide, hidden, width)),
+        out_shape=(*results, *small),
+        in_specs=[hbm] * 7,
+        out_specs=(hbm,) * 14,
+        scratch_shapes=[pltpu.VMEM(r.shape, r.dtype) for r in (*results, *small)]
+        + [pltpu.VMEM((ROWS, width), F32), pltpu.SemaphoreType.DMA((3, 9))],
         compiler_params=pltpu.CompilerParams(vmem_limit_bytes=63 << 20),
     )(*outs)
     block_out, tokens_grad, d_win, d_wot, d_wup, d_wdt = placed[:6]

time: 135 us -> 130 us (0.963)
  Pallas kernels: 134 us -> 129 us
    pallas_call x1, Pallas kernels: 130 us -> 126 us  [on_device(): pl.pallas_call(functools.partial(block_kernel, sizes), out_shape=(*result...]
where the time goes in v5:
time: 130 us
  Pallas kernels  129 us (99%)
    pallas_call x1, Pallas kernels, on_device(): pl.pallas_call(functools.partial(block_kernel, sizes), out_shape=(*result...  126 us
    pallas_call x1, Pallas kernels, on_device(): pl.pallas_call(functools.partial(finish_kernel, (n_ctx, piece, cut, wide,...  2.96 us

profile of v5, /device:TPU:0, one launch (start us, length us, event | category | flops | bytes accessed | tf_op | source)
XLA Modules:
  0.0 130.0 jit_solution(11151982567395672947)
XLA Ops:
  0.7 126.2 %shard_map.254 = (bf16[320,1024]{1,0:T(8,128)(2,1)}, bf16[320,1024]{1,0:T(8,128)(2,1)}, f32[3,128,256]{2,1,0:T(8,128)}, f32[256,128]{1,0:T(8,128)}, f32[128,1024...) custom-call(bf16[320,1024]{1,0:T(8,128)(2,1)} %bitcast.20, bf16[320,1024]{1,0:T(8,128)(2,1)} %bitcast.21, ...), custom_call_target="tpu_custom_call" | custom-call | tf_op jit(solution)/shard_map/pallas_call | solution.py:1287
  126.9 3.0 %shard_map.255 = (bf16[320,1024]{1,0:T(8,128)(2,1)}, bf16[320,1024]{1,0:T(8,128)(2,1)}, f32[3,128,256]{2,1,0:T(8,128)}, f32[256,128]{1,0:T(8,128)}, f32[128,1024...) custom-call(bf16[320,1024]{1,0:T(8,128)(2,1)} %get-tuple-element.35., ...), custom_call_target="tpu_custom_call" | custom-call | tf_op jit(solution)/shard_map/pallas_call | solution.py:1316

commit v6 on v5

--- a/solution.py
+++ b/solution.py
@@ -638,19 +638,16 @@
                     relay[j, slots_at(c, at), :] = value.astype(BF16)
                     passed(j, at).start()
 
-        def finish():
-            near[0].wait_recv()
-            for at in pieces(c):
+        def finish(some_pieces=None):
+            if some_pieces is None or 0 in some_pieces:
+                near[0].wait_recv()
+            for at in some_pieces or pieces(c):
                 passed(0, at).wait_recv()
 
         return pass_on, finish, send_near
 
     def to_all(source, target, c):
         marks = {at: [fresh() for _ in range(4)] for at in pieces(c)}
-
-        def block(index):
-            first_row = index * slots + starts[c]
-            return target.at[pl.ds(pl.multiple_of(first_row, ROWS), sizes_of[c]), :]
 
         def piece_of(index, at):
             first_row = index * slots + starts[c] + at
@@ -664,11 +661,15 @@
             there = piece_of(flip(z, k), at)
             return remote(there, there, zpeer(1), marks[at][k], marks[at][3 - k])
 
-        send_if(at_end, [functools.partial(far, 2, at) for at in pieces(c)])
-        send_if(inside, [functools.partial(far, 3, at) for at in pieces(c)])
-        own_part = source.at[slot_part(c), :]
-        near = send(own_part, block(z), zpeer(1))
-        stays.append(local(own_part, block(z)))
+        nears = []
+
+        def start(at):
+            own_part = source.at[slots_at(c, at), :]
+            send_if(at_end, [functools.partial(far, 2, at)])
+            send_if(inside, [functools.partial(far, 3, at)])
+            nears.append(send(own_part, piece_of(z, at), zpeer(1)))
+            stays.append(local(own_part, piece_of(z, at)))
+
         both = [(k, at) for at in pieces(c) for k in (3, 2)]
 
         def pass_on():
@@ -681,14 +682,15 @@
                     passed(k, at).start()
 
         def finish():
-            near.wait_recv()
+            for copy in nears:
+                copy.wait_recv()
 
             @pl.when(at_end)
             def _():
                 for k, at in both:
                     far(k, at).wait_recv()
 
-        return pass_on, finish
+        return pass_on, finish, start
 
     def arrived(part, recv, c, at, size):
         here = pl.ds(pl.multiple_of(bases[c] + z * sizes_of[c] + at, ROWS), size)
@@ -800,12 +802,40 @@
         lax.fori_loop(0, group, one, 0)
         return [send(both.at[flip(me, k)], recv.at[k - 1], plane(k)) for k in reversed(planes)]
 
+    def grad_halves(copy, buf, near, both, recv):
+        if not relayed:
+            return grad_far(copy, buf, near, both, recv)
+        copy.wait_recv()
+
+        def one(m, carry):
+            both[m] = (buf[m, core].astype(F32) + near[m].astype(F32)).astype(BF16)
+            return carry
+
+        lax.fori_loop(0, group, one, 0)
+        part = piece // 2
+        corner = flip(me, 3)
+        return [
+            send(both.at[corner, 0:part], recv.at[2, 0:part], plane(1)),
+            send(both.at[corner, part:piece], recv.at[2, part:piece], plane(2)),
+        ]
+
+    def grad_onward(copies, both, recv):
+        if not relayed:
+            return copies
+        part = piece // 2
+        for k, at in ((2, slice(0, part)), (1, slice(part, piece))):
+            copies[2 - k].wait_recv()
+            other = flip(me, k)
+            value = both[other, at].astype(F32) + recv[2, at].astype(F32)
+            both[other, at] = value.astype(BF16)
+        return [send(both.at[flip(me, k)], recv.at[k - 1], plane(k)) for k in (1, 2)]
+
     def grad_sum(copies, both, recv):
         for copy in copies:
             copy.wait_recv()
         value = both[me].astype(F32)
-        for k in planes:
-            value = value + recv[k - 1].astype(F32)
+        for k in range(len(copies)):
+            value = value + recv[k].astype(F32)
         return value
 
     wide_grad(b_wdt, gdown, act, hidden)
@@ -944,7 +974,10 @@
         value = first[rows_at(c, z), :] + arrived(parts, recvs, c, 0, sizes_of[c]) + vx[5:6, :]
         value = jnp.where(own_live[slot_part(c)], value, 0.0)
         block_own[slot_part(c), :] = value.astype(BF16)
-        return to_all(block_own, out_block, c)
+        passing = to_all(block_own, out_block, c)
+        for at in pieces(c):
+            passing[2](at)
+        return passing
 
     def at_do(c):
         def at(index):
@@ -977,7 +1010,7 @@
     vector_copy = vector_near(vector_copies, early, early_z, 4 * per, early_sib)
     tail[0][0]()
     tail.append(block_rows(1))
-    wot_grad_far = grad_far(wot_near, b_wot, s_wot, t_wot, r_wot)
+    wot_grad_far = grad_halves(wot_near, b_wot, s_wot, t_wot, r_wot)
     early_far = vector_far(vector_copy, early, early_sib, early_plane)
     do_passed = [ctx_forward(do_started[c], at_do(c)) for c in range(2)]
     along_passed = ctx_forward(along_started, at_along)
@@ -1020,18 +1053,29 @@
     sent1 = [in_back(c) for c in range(2)]
     for c in range(2):
         sent1[c][2]()
+    sums = [0.0, 0.0]
+    for row in range(0, rows, 2 * BLOCK):
+        term = part1[row : row + 2 * BLOCK, :].astype(F32)
+        weighted = term * n1[row : row + 2 * BLOCK, :]
+        sums[0] = sums[0] + jnp.sum(weighted, axis=0, keepdims=True)
+        sums[1] = sums[1] + jnp.sum(term, axis=0, keepdims=True)
+    for line, value in enumerate(sums):
+        pack(late, line * per, value)
+    late[2 * per :, :] = jnp.zeros((late.shape[0] - 2 * per, LANES), F32)
+    for j, start in enumerate((0, 2 * wide)):
+        value = jnp.sum(dqkv[:, start : start + wide].astype(F32), axis=0, keepdims=True)
+        pack(late, 2 * per + j * (wide // LANES), value)
+    vector_copies = vector_z(late, late_z, 2 * per)
     tail[1][0]()
-    wup_far = grad_far(wup_near, b_wup, s_wup, t_wup, r_wup)
+    wup_far = grad_halves(wup_near, b_wup, s_wup, t_wup, r_wup)
+    wot_grad_far = grad_onward(wot_grad_far, t_wot, r_wot)
 
     for j in range(3):
         out = tn(h1[...], dqkv[:, j * wide : (j + 1) * wide]).astype(BF16)
         b_win[j] = out.reshape(group, 2, piece, wide)
     win_near = send(b_win.at[:, :, 1 - core], s_win, sib)
     sent1[0][0]()
-    late[2 * per :, :] = jnp.zeros((late.shape[0] - 2 * per, LANES), F32)
-    for j, start in enumerate((0, 2 * wide)):
-        value = jnp.sum(dqkv[:, start : start + wide].astype(F32), axis=0, keepdims=True)
-        pack(late, 2 * per + j * (wide // LANES), value)
+    wup_far = grad_onward(wup_far, t_wup, r_wup)
     f_wdt[...] = turned(grad_sum(wdt_far, t_wdt, r_wdt), f_wdt)
     stays.append(local(f_wdt, out_wdt))
     win_near.wait_recv()
@@ -1041,6 +1085,22 @@
     win_far = [send(t_win.at[flip(me, k)], r_win.at[k - 1], plane(k)) for k in reversed(planes)]
 
     sent1[1][0]()
+    def first_back(c, at):
+        sent1[c][1]((at,))
+        normed, inv = norm_parts(tok[block_at(c, z, at), :].astype(F32))
+        grad = arrived(part1, recv1, c, at, ROWS)
+        there = slots_at(c, at)
+        value = gfirst[there, :] + norm_back(grad, normed, inv, vx[0:1, :])
+        tokens_own[there, :] = value.astype(BF16)
+        tail[2 + c][2](at)
+
+    tail += [to_all(tokens_own, out_tokens, c) for c in range(2)]
+    for at in pieces(0):
+        first_back(0, at)
+    for at in pieces(1)[:-1]:
+        first_back(1, at)
+    tail[2][0]()
+    first_back(1, pieces(1)[-1])
     whole_rows = grad_sum(wot_grad_far, t_wot, r_wot)
     o_wot[...] = whole_rows.astype(BF16)
     to_owner = [
@@ -1048,34 +1108,12 @@
         for k in reversed(zs)
     ]
 
-    def first_back(c):
-        sent1[c][1]()
-
-        sums = [0.0, 0.0]
-        for at in range(0, sizes_of[c], ROWS):
-            here = pl.ds(pl.multiple_of(bases[c] + z * sizes_of[c] + at, ROWS), ROWS)
-            grad = arrived(part1, recv1, c, at, ROWS)
-            normed, inv = norm_parts(tok[here, :].astype(F32))
-            there = slice(starts[c] + at, starts[c] + at + ROWS)
-            value = gfirst[there, :] + norm_back(grad, normed, inv, vx[0:1, :])
-            tokens_own[there, :] = value.astype(BF16)
-            terms = (grad * normed, grad)
-            sums = [old + jnp.sum(term, axis=0, keepdims=True) for old, term in zip(sums, terms)]
-        return sums
-
-    sums = first_back(0)
-    tail.append(to_all(tokens_own, out_tokens, 0))
-    for line, (one, two) in enumerate(zip(sums, first_back(1))):
-        pack(late, line * per, one + two)
-    vector_copies = vector_z(late, late_z, 2 * per)
-    tail.append(to_all(tokens_own, out_tokens, 1))
+    vector_copy = vector_near(vector_copies, late, late_z, 2 * per, late_sib)
+    tail[3][0]()
+    late_far = vector_far(vector_copy, late, late_sib, late_plane)
     f_wup[...] = grad_sum(wup_far, t_wup, r_wup)
     stays.append(local(f_wup, out_wup))
     vector_last(early_far, early, early_plane)
-    tail[2][0]()
-    vector_copy = vector_near(vector_copies, late, late_z, 2 * per, late_sib)
-    tail[3][0]()
-    late_far = vector_far(vector_copy, late, late_sib, late_plane)
     f_win[...] = grad_sum(win_far, t_win, r_win)
     stays.append(local(f_win, out_win))
     for copy in to_owner:

time: 130 us -> 129 us (level)
    pallas_call x1, Pallas kernels: 126 us -> 125 us  [on_device(): pl.pallas_call(functools.partial(block_kernel, sizes), out_shape=(*result...]
where the time goes in v6:
time: 129 us
  Pallas kernels  128 us (99%)
    pallas_call x1, Pallas kernels, on_device(): pl.pallas_call(functools.partial(block_kernel, sizes), out_shape=(*result...  125 us
    pallas_call x1, Pallas kernels, on_device(): pl.pallas_call(functools.partial(finish_kernel, (n_ctx, piece, cut, wide,...  2.96 us

profile of v6, /device:TPU:0, one launch (start us, length us, event | category | flops | bytes accessed | tf_op | source)
XLA Modules:
  0.0 128.6 jit_solution(13454913913520213430)
XLA Ops:
  0.7 124.9 %shard_map.254 = (bf16[320,1024]{1,0:T(8,128)(2,1)}, bf16[320,1024]{1,0:T(8,128)(2,1)}, f32[3,128,256]{2,1,0:T(8,128)}, f32[256,128]{1,0:T(8,128)}, f32[128,1024...) custom-call(bf16[320,1024]{1,0:T(8,128)(2,1)} %bitcast.20, bf16[320,1024]{1,0:T(8,128)(2,1)} %bitcast.21, ...), custom_call_target="tpu_custom_call" | custom-call | tf_op jit(solution)/shard_map/pallas_call | solution.py:1325
  125.5 3.0 %shard_map.255 = (bf16[320,1024]{1,0:T(8,128)(2,1)}, bf16[320,1024]{1,0:T(8,128)(2,1)}, f32[3,128,256]{2,1,0:T(8,128)}, f32[256,128]{1,0:T(8,128)}, f32[128,1024...) custom-call(bf16[320,1024]{1,0:T(8,128)(2,1)} %get-tuple-element.35., ...), custom_call_target="tpu_custom_call" | custom-call | tf_op jit(solution)/shard_map/pallas_call | solution.py:1354

commit v7 on v6

--- a/solution.py
+++ b/solution.py
@@ -42,6 +42,14 @@
 
 def tn(left, right):
     return lax.dot_general(left, right, (((0,), (0,)), ((), ())), preferred_element_type=F32)
+
+
+def steps(count, body):
+    if count > 8:
+        lax.fori_loop(0, count, body, 0)
+        return
+    for step in range(count):
+        body(step, 0)
 
 
 def turned(value, ref):
@@ -463,7 +471,7 @@
         g_wdt[me, core, :, at] = nt(unit_one, c_out[at, :]).astype(BF16)
         return carry
 
-    lax.fori_loop(0, hidden // TILE, turn, 0)
+    steps(hidden // TILE, turn)
 
     lengths = BUFFER + jnp.sum(keep[...], axis=1, keepdims=True)
     slot_id = lax.broadcasted_iota(jnp.int32, (slots, 1), 0) + ctx * slots
@@ -710,7 +718,7 @@
             first[at_rows, lane_at(step, TILE)] = nt(mixed[at_rows, :], weight)
             return carry
 
-        lax.fori_loop(0, width // TILE, project_out, 0)
+        steps(width // TILE, project_out)
 
         for row in range(bases[c], bases[c] + images * sizes_of[c], ROWS):
             at = slice(row, row + ROWS)
@@ -734,14 +742,14 @@
             gv[8:9, at] += jnp.sum(grad.astype(F32), axis=0, keepdims=True)
             return carry
 
-        lax.fori_loop(0, hidden // TILE, expand, 0)
+        steps(hidden // TILE, expand)
 
         def up_back(step, carry):
             weight = g_wup[pl.ds(step * some, some)].reshape(TILE, hidden)
             part2[at_rows, lane_at(step, TILE)] = nt(gi[at_rows, :], weight).astype(BF16)
             return carry
 
-        lax.fori_loop(0, width // TILE, up_back, 0)
+        steps(width // TILE, up_back)
         return scatter(part2, recv2, relay2, c)
 
     attended(0)
@@ -758,7 +766,7 @@
             ga[at_rows, at] = nn(gdown[at_rows, :], weight)
             return carry
 
-        lax.fori_loop(0, hidden // TILE, one, 0)
+        steps(hidden // TILE, one)
 
     down_back(0)
     sent2 = [feed_forward(0)]
@@ -774,7 +782,7 @@
         parts[:, lane_at(step, TILE)] = nt(act[...], weight).astype(BF16)
         return carry
 
-    lax.fori_loop(0, width // TILE, contract, 0)
+    steps(width // TILE, contract)
     sents = []
     for c in range(2):
         sents.append(scatter(parts, recvs, relays, c))
@@ -787,7 +795,7 @@
             buf[:, :, :, at] = out.reshape(group, 2, piece, TILE)
             return carry
 
-        lax.fori_loop(0, lanes // TILE, one, 0)
+        steps(lanes // TILE, one)
 
     def grad_near(buf, near):
         return send(buf.at[:, 1 - core], near, sib)
@@ -799,7 +807,7 @@
             both[m] = (buf[m, core].astype(F32) + near[m].astype(F32)).astype(BF16)
             return carry
 
-        lax.fori_loop(0, group, one, 0)
+        steps(group, one)
         return [send(both.at[flip(me, k)], recv.at[k - 1], plane(k)) for k in reversed(planes)]
 
     def grad_halves(copy, buf, near, both, recv):
@@ -811,7 +819,7 @@
             both[m] = (buf[m, core].astype(F32) + near[m].astype(F32)).astype(BF16)
             return carry
 
-        lax.fori_loop(0, group, one, 0)
+        steps(group, one)
         part = piece // 2
         corner = flip(me, 3)
         return [
@@ -900,7 +908,7 @@
             gm[slot_part(c), at] = nn(gown[slot_part(c), :], weight).astype(BF16)
             return carry
 
-        lax.fori_loop(0, n_t, mixed_back, 0)
+        steps(n_t, mixed_back)
         place_at = pl.ds(pl.multiple_of(ctx * slots + starts[c], ROWS), sizes_of[c])
         sent = [
             send(
@@ -965,7 +973,7 @@
         b_wot[:, :, :, at] = out.reshape(group, 2, piece, TILE)
         return carry
 
-    lax.fori_loop(0, n_t * wide // TILE, out_grad, 0)
+    steps(n_t * wide // TILE, out_grad)
     wot_near = grad_near(b_wot, s_wot)
 
 
@@ -1047,7 +1055,7 @@
             part1[at_rows, lane_at(step, TILE)] = out.astype(BF16)
             return carry
 
-        lax.fori_loop(0, width // TILE, one, 0)
+        steps(width // TILE, one)
         return scatter(part1, recv1, relay1, c)
 
     sent1 = [in_back(c) for c in range(2)]

time: 129 us -> 123 us (0.953)
  Pallas kernels: 128 us -> 122 us
    pallas_call x1, Pallas kernels: 125 us -> 119 us  [on_device(): pl.pallas_call(functools.partial(block_kernel, sizes), out_shape=(*result...]
where the time goes in v7:
time: 123 us
  Pallas kernels  122 us (99%)
    pallas_call x1, Pallas kernels, on_device(): pl.pallas_call(functools.partial(block_kernel, sizes), out_shape=(*result...  119 us
    pallas_call x1, Pallas kernels, on_device(): pl.pallas_call(functools.partial(finish_kernel, (n_ctx, piece, cut, wide,...  2.96 us

profile of v7, /device:TPU:0, one launch (start us, length us, event | category | flops | bytes accessed | tf_op | source)
XLA Modules:
  0.0 123.2 jit_solution(5369030944323066975)
XLA Ops:
  0.7 119.4 %shard_map.254 = (bf16[320,1024]{1,0:T(8,128)(2,1)}, bf16[320,1024]{1,0:T(8,128)(2,1)}, f32[3,128,256]{2,1,0:T(8,128)}, f32[256,128]{1,0:T(8,128)}, f32[128,1024...) custom-call(bf16[320,1024]{1,0:T(8,128)(2,1)} %bitcast.20, bf16[320,1024]{1,0:T(8,128)(2,1)} %bitcast.21, ...), custom_call_target="tpu_custom_call" | custom-call | tf_op jit(solution)/shard_map/pallas_call | solution.py:1333
  120.1 3.0 %shard_map.255 = (bf16[320,1024]{1,0:T(8,128)(2,1)}, bf16[320,1024]{1,0:T(8,128)(2,1)}, f32[3,128,256]{2,1,0:T(8,128)}, f32[256,128]{1,0:T(8,128)}, f32[128,1024...) custom-call(bf16[320,1024]{1,0:T(8,128)(2,1)} %get-tuple-element.35., ...), custom_call_target="tpu_custom_call" | custom-call | tf_op jit(solution)/shard_map/pallas_call | solution.py:1362

commit v8 on v7

--- a/solution.py
+++ b/solution.py
@@ -853,6 +853,112 @@
     wup_near = grad_near(b_wup, s_wup)
     wdt_far = grad_far(wdt_near, b_wdt, s_wdt, t_wdt, r_wdt)
 
+    own_live = slot_id < jnp.sum(
+        jnp.where(lax.broadcasted_iota(jnp.int32, (images, 1), 0) == z, lengths, 0),
+        axis=0,
+        keepdims=True,
+    )
+
+    def norm_back(grad, normed, inv, gain):
+        scaled = grad * gain
+        inner = (
+            scaled
+            - jnp.mean(scaled, axis=-1, keepdims=True)
+            - normed * jnp.mean(scaled * normed, axis=-1, keepdims=True)
+        )
+        return inner * inv
+
+    def second_back(c):
+        sent2[c][1]()
+
+        sums = [0.0, 0.0, 0.0, 0.0]
+        for at in range(0, sizes_of[c], ROWS):
+            here = pl.ds(pl.multiple_of(bases[c] + z * sizes_of[c] + at, ROWS), ROWS)
+            grad = arrived(part2, recv2, c, at, ROWS)
+            normed, inv = norm_parts(first[here, :])
+            rows_grad = gdown[here, :].astype(F32)
+            value = rows_grad + norm_back(grad, normed, inv, vx[3:4, :])
+            there = slice(starts[c] + at, starts[c] + at + ROWS)
+            gfirst[there, :] = value
+            gown[there, :] = value.astype(BF16)
+            terms = (value, grad * normed, grad, rows_grad)
+            sums = [old + jnp.sum(term, axis=0, keepdims=True) for old, term in zip(sums, terms)]
+        for line, value in enumerate(sums):
+            gv[2 + line : 3 + line, :] += value
+
+        def mixed_back(step, carry):
+            at = lane_at(step, wide)
+            weight = g_wot[:, :, :, at].reshape(width, wide)
+            gm[slot_part(c), at] = nn(gown[slot_part(c), :], weight).astype(BF16)
+            return carry
+
+        steps(n_t, mixed_back)
+        place_at = pl.ds(pl.multiple_of(ctx * slots + starts[c], ROWS), sizes_of[c])
+        sent = [
+            send(
+                gm.at[slot_part(c), lane_at(flip(z, k), wide)],
+                do.at[z, place_at, :],
+                zpeer(k),
+            )
+            for k in reversed(zs)
+        ]
+        do[z, place_at, :] = gm[slot_part(c), lane_at(z, wide)]
+        return sent
+
+    to_heads = [second_back(0)]
+    sents[0][0]()
+    to_heads.append(second_back(1))
+    sents[1][0]()
+
+    per = width // LANES
+
+    def pack(ref, row, value):
+        for i in range(value.shape[1] // LANES):
+            ref[row + i : row + i + 1, :] = value[:, i * LANES : (i + 1) * LANES]
+
+    def unpack(ref, row, size):
+        return jnp.concatenate([ref[row + i : row + i + 1, :] for i in range(size // LANES)], axis=1)
+
+    for line in range(4):
+        pack(early, line * per, gv[2 + line : 3 + line, :])
+    pack(early, 4 * per, gv[8:9, 0:hidden])
+
+    def vector_z(ref, recv, size):
+        return [send(ref.at[0:size], recv.at[k - 1], zpeer(k)) for k in reversed(zs)]
+
+    def vector_near(copies, ref, recv, size, near):
+        for copy in copies:
+            complete(copy)
+        value = ref[0:size]
+        for k in zs:
+            value = value + recv[k - 1]
+        ref[0:size] = value
+        return send(ref, near, sib)
+
+    def vector_far(copy, ref, near, recv):
+        complete(copy)
+        ref[...] = ref[...] + near[...]
+        return [send(ref, recv.at[k - 1], plane(k)) for k in planes]
+
+    def vector_last(copies, ref, recv):
+        for copy in copies:
+            complete(copy)
+        value = ref[...]
+        for k in planes:
+            value = value + recv[k - 1]
+        ref[...] = value
+
+    vector_copies = vector_z(early, early_z, 4 * per)
+
+    def out_grad(step, carry):
+        at = lane_at(step, TILE)
+        part = jnp.concatenate([mixed[rows_at(c, z), at] for c in range(2)], axis=0)
+        out = tn(gown[...], part).astype(BF16)
+        b_wot[:, :, :, at] = out.reshape(group, 2, piece, TILE)
+        return carry
+
+    steps(n_t * wide // TILE, out_grad)
+    wot_near = grad_near(b_wot, s_wot)
     q_passed = ctx_forward(q_started, at_q)
     stat_passed = ctx_forward(stat_started, at_stat)
     ctx_finish(q_started, q_passed)
@@ -868,113 +974,6 @@
             block = scores[h * slots : (h + 1) * slots]
             block = jnp.where(row_live[image], block, neg_big)
             wk[image, h * slots : (h + 1) * slots, :] = jnp.exp(block - level)
-
-    own_live = slot_id < jnp.sum(
-        jnp.where(lax.broadcasted_iota(jnp.int32, (images, 1), 0) == z, lengths, 0),
-        axis=0,
-        keepdims=True,
-    )
-
-    def norm_back(grad, normed, inv, gain):
-        scaled = grad * gain
-        inner = (
-            scaled
-            - jnp.mean(scaled, axis=-1, keepdims=True)
-            - normed * jnp.mean(scaled * normed, axis=-1, keepdims=True)
-        )
-        return inner * inv
-
-    def second_back(c):
-        sent2[c][1]()
-
-        sums = [0.0, 0.0, 0.0, 0.0]
-        for at in range(0, sizes_of[c], ROWS):
-            here = pl.ds(pl.multiple_of(bases[c] + z * sizes_of[c] + at, ROWS), ROWS)
-            grad = arrived(part2, recv2, c, at, ROWS)
-            normed, inv = norm_parts(first[here, :])
-            rows_grad = gdown[here, :].astype(F32)
-            value = rows_grad + norm_back(grad, normed, inv, vx[3:4, :])
-            there = slice(starts[c] + at, starts[c] + at + ROWS)
-            gfirst[there, :] = value
-            gown[there, :] = value.astype(BF16)
-            terms = (value, grad * normed, grad, rows_grad)
-            sums = [old + jnp.sum(term, axis=0, keepdims=True) for old, term in zip(sums, terms)]
-        for line, value in enumerate(sums):
-            gv[2 + line : 3 + line, :] += value
-
-        def mixed_back(step, carry):
-            at = lane_at(step, wide)
-            weight = g_wot[:, :, :, at].reshape(width, wide)
-            gm[slot_part(c), at] = nn(gown[slot_part(c), :], weight).astype(BF16)
-            return carry
-
-        steps(n_t, mixed_back)
-        place_at = pl.ds(pl.multiple_of(ctx * slots + starts[c], ROWS), sizes_of[c])
-        sent = [
-            send(
-                gm.at[slot_part(c), lane_at(flip(z, k), wide)],
-                do.at[z, place_at, :],
-                zpeer(k),
-            )
-            for k in reversed(zs)
-        ]
-        do[z, place_at, :] = gm[slot_part(c), lane_at(z, wide)]
-        return sent
-
-    to_heads = [second_back(0)]
-    sents[0][0]()
-    to_heads.append(second_back(1))
-    sents[1][0]()
-
-    per = width // LANES
-
-    def pack(ref, row, value):
-        for i in range(value.shape[1] // LANES):
-            ref[row + i : row + i + 1, :] = value[:, i * LANES : (i + 1) * LANES]
-
-    def unpack(ref, row, size):
-        return jnp.concatenate([ref[row + i : row + i + 1, :] for i in range(size // LANES)], axis=1)
-
-    for line in range(4):
-        pack(early, line * per, gv[2 + line : 3 + line, :])
-    pack(early, 4 * per, gv[8:9, 0:hidden])
-
-    def vector_z(ref, recv, size):
-        return [send(ref.at[0:size], recv.at[k - 1], zpeer(k)) for k in reversed(zs)]
-
-    def vector_near(copies, ref, recv, size, near):
-        for copy in copies:
-            complete(copy)
-        value = ref[0:size]
-        for k in zs:
-            value = value + recv[k - 1]
-        ref[0:size] = value
-        return send(ref, near, sib)
-
-    def vector_far(copy, ref, near, recv):
-        complete(copy)
-        ref[...] = ref[...] + near[...]
-        return [send(ref, recv.at[k - 1], plane(k)) for k in planes]
-
-    def vector_last(copies, ref, recv):
-        for copy in copies:
-            complete(copy)
-        value = ref[...]
-        for k in planes:
-            value = value + recv[k - 1]
-        ref[...] = value
-
-    vector_copies = vector_z(early, early_z, 4 * per)
-
-    def out_grad(step, carry):
-        at = lane_at(step, TILE)
-        part = jnp.concatenate([mixed[rows_at(c, z), at] for c in range(2)], axis=0)
-        out = tn(gown[...], part).astype(BF16)
-        b_wot[:, :, :, at] = out.reshape(group, 2, piece, TILE)
-        return carry
-
-    steps(n_t * wide // TILE, out_grad)
-    wot_near = grad_near(b_wot, s_wot)
 
 
     def block_rows(c):

time: 123 us -> 122 us (level)
    pallas_call x1, Pallas kernels: 119 us -> 118 us  [on_device(): pl.pallas_call(functools.partial(block_kernel, sizes), out_shape=(*result...]
where the time goes in v8:
time: 122 us
  Pallas kernels  121 us (99%)
    pallas_call x1, Pallas kernels, on_device(): pl.pallas_call(functools.partial(block_kernel, sizes), out_shape=(*result...  118 us
    pallas_call x1, Pallas kernels, on_device(): pl.pallas_call(functools.partial(finish_kernel, (n_ctx, piece, cut, wide,...  2.96 us

profile of v8, /device:TPU:0, one launch (start us, length us, event | category | flops | bytes accessed | tf_op | source)
XLA Modules:
  0.0 122.0 jit_solution(15053153926092690569)
XLA Ops:
  0.7 118.2 %shard_map.254 = (bf16[320,1024]{1,0:T(8,128)(2,1)}, bf16[320,1024]{1,0:T(8,128)(2,1)}, f32[3,128,256]{2,1,0:T(8,128)}, f32[256,128]{1,0:T(8,128)}, f32[128,1024...) custom-call(bf16[320,1024]{1,0:T(8,128)(2,1)} %bitcast.20, bf16[320,1024]{1,0:T(8,128)(2,1)} %bitcast.21, ...), custom_call_target="tpu_custom_call" | custom-call | tf_op jit(solution)/shard_map/pallas_call | solution.py:1332
  118.9 3.0 %shard_map.255 = (bf16[320,1024]{1,0:T(8,128)(2,1)}, bf16[320,1024]{1,0:T(8,128)(2,1)}, f32[3,128,256]{2,1,0:T(8,128)}, f32[256,128]{1,0:T(8,128)}, f32[128,1024...) custom-call(bf16[320,1024]{1,0:T(8,128)(2,1)} %get-tuple-element.35., ...), custom_call_target="tpu_custom_call" | custom-call | tf_op jit(solution)/shard_map/pallas_call | solution.py:1361

commit v9 on v8

--- a/solution.py
+++ b/solution.py
@@ -558,10 +558,11 @@
         put_rows(stat, image, top + jnp.log(whole))
         out = nn(probs.astype(BF16), qkv[image, :, 2 * wide : 3 * wide])
         split_rows(mixed, image, lane_at(z, wide), pick_heads(out).astype(BF16))
-        for part in image_parts:
+        for part, order in zip(image_parts, ((0,), (0, 1))):
             if image == part.stop - 1:
-                for c in range(2):
-                    there = at_mixed(z, c, part)
+                for c in order:
+                    whole_part = slice(0, images) if c == 1 else part
+                    there = at_mixed(z, c, whole_part)
                     mixed_sent[c] += [send(there, there, zpeer(k)) for k in reversed(zs)]
 
     def at_stat(index):
@@ -1083,8 +1084,6 @@
     win_near = send(b_win.at[:, :, 1 - core], s_win, sib)
     sent1[0][0]()
     wup_far = grad_onward(wup_far, t_wup, r_wup)
-    f_wdt[...] = turned(grad_sum(wdt_far, t_wdt, r_wdt), f_wdt)
-    stays.append(local(f_wdt, out_wdt))
     win_near.wait_recv()
     for j in range(3):
         both = b_win[j, :, pl.ds(core, 1)].reshape(group, piece, wide).astype(F32)
@@ -1118,6 +1117,8 @@
     vector_copy = vector_near(vector_copies, late, late_z, 2 * per, late_sib)
     tail[3][0]()
     late_far = vector_far(vector_copy, late, late_sib, late_plane)
+    f_wdt[...] = turned(grad_sum(wdt_far, t_wdt, r_wdt), f_wdt)
+    stays.append(local(f_wdt, out_wdt))
     f_wup[...] = grad_sum(wup_far, t_wup, r_wup)
     stays.append(local(f_wup, out_wup))
     vector_last(early_far, early, early_plane)

time: 122 us -> 122 us (level)
  no operation moved by 1% of the time
where the time goes in v9:
time: 122 us
  Pallas kernels  121 us (99%)
    pallas_call x1, Pallas kernels, on_device(): pl.pallas_call(functools.partial(block_kernel, sizes), out_shape=(*result...  118 us
    pallas_call x1, Pallas kernels, on_device(): pl.pallas_call(functools.partial(finish_kernel, (n_ctx, piece, cut, wide,...  2.96 us

profile of v9, /device:TPU:0, one launch (start us, length us, event | category | flops | bytes accessed | tf_op | source)
XLA Modules:
  0.0 121.6 jit_solution(7122236020224884894)
XLA Ops:
  0.7 117.8 %shard_map.254 = (bf16[320,1024]{1,0:T(8,128)(2,1)}, bf16[320,1024]{1,0:T(8,128)(2,1)}, f32[3,128,256]{2,1,0:T(8,128)}, f32[256,128]{1,0:T(8,128)}, f32[128,1024...) custom-call(bf16[320,1024]{1,0:T(8,128)(2,1)} %bitcast.20, bf16[320,1024]{1,0:T(8,128)(2,1)} %bitcast.21, ...), custom_call_target="tpu_custom_call" | custom-call | tf_op jit(solution)/shard_map/pallas_call | solution.py:1333
  118.4 3.0 %shard_map.255 = (bf16[320,1024]{1,0:T(8,128)(2,1)}, bf16[320,1024]{1,0:T(8,128)(2,1)}, f32[3,128,256]{2,1,0:T(8,128)}, f32[256,128]{1,0:T(8,128)}, f32[128,1024...) custom-call(bf16[320,1024]{1,0:T(8,128)(2,1)} %get-tuple-element.35., ...), custom_call_target="tpu_custom_call" | custom-call | tf_op jit(solution)/shard_map/pallas_call | solution.py:1362
